TPU v7x, 32 devices: a whole 2x2x4 slice. The times are simulated.
32 devices in a mesh: seq: 8 (over z, x), batch: 4 (over y, core).
Axes of the slice: x: 2, y: 2, z: 4, core: 2. Of those that a mesh axis runs over, the one named last changes fastest.
Arguments:
- inputs: bfloat16 [8, 1024, 1024], P('batch', 'seq'), may hold values from -6 to 6
- memory: bfloat16 [8, 512, 1024], P('batch', 'seq'), may hold values from -6 to 6
- cotangent: bfloat16 [8, 1024, 1024], P('batch', 'seq'), may hold values from -6 to 6
- valid_len: int32 [8], P('batch'), may hold values from 32 to 1024, as said below
- value_routes: int32 [8, 1024, 4, 2], P('batch', 'seq'), may hold values from 0 to 4, all different within a row
- memory_routes: int32 [8, 512, 4, 2], P('batch', 'seq'), may hold values from 0 to 4, all different within a row
- output_routes: int32 [8, 1024, 4, 2], P('batch', 'seq'), may hold values from 0 to 4, all different within a row
- norm1_gain: float32 [1024], replicated, may hold values from 0.5 to 1.5
- norm2_gain: float32 [1024], replicated, may hold values from 0.5 to 1.5
- query_weight: bfloat16 [1024, 448], replicated, may hold values from -0.1875 to 0.1875
- key_weight: bfloat16 [1024, 448], replicated, may hold values from -0.1875 to 0.1875
- value_weight: bfloat16 [1024, 2240], replicated, may hold values from -0.1875 to 0.1875
- router_weight: bfloat16 [1024, 40], replicated, may hold values from -0.12988281 to 0.12988281
- output_weight: bfloat16 [2240, 1024], replicated, may hold values from -15 to 15
- up_weight: bfloat16 [1024, 4096], replicated, may hold values from -0.1875 to 0.1875
- down_weight: bfloat16 [4096, 1024], replicated, may hold values from -0.09375 to 0.09375
Outputs:
- output: bfloat16 [8, 1024, 1024], P('batch', 'seq')
- input_grad: float32 [8, 1024, 1024], P('batch', 'seq')
- norm1_grad: float32 [1024], P(('seq', 'batch'))
- norm2_grad: float32 [1024], P(('seq', 'batch'))
- query_grad: float32 [1024, 448], P(('seq', 'batch'))
- key_grad: float32 [1024, 448], P(('seq', 'batch'))
- value_grad: float32 [1024, 2240], P(('seq', 'batch'))
- router_grad: float32 [1024, 40], P(('seq', 'batch'))
- outproj_grad: float32 [2240, 1024], P(None, ('seq', 'batch'))
- up_grad: float32 [1024, 4096], P(('seq', 'batch'))
- down_grad: float32 [4096, 1024], P(('seq', 'batch'))
Inputs may be any that keep to these rules, and one draw needn't show every extreme that they name: `valid_len`: each aligned run of 2 sequences holds one of full length 1024.
All inputs are finite; a program needn't handle non-finite values.
Results may differ from a plain program's by a relative error of at most 0.015.
Values may be sent and summed in bfloat16 or wider, within the bound.
No kernel may reach another device: no remote copies, remote signals or barrier semaphores. Data moves between devices by JAX's collectives and lax.ppermute only.
A program may use at most 256 MiB of HBM per device.

v0:
```python
import collections
import functools

import jax
import jax.numpy as jnp
import numpy as np
from jax import lax
from jax.experimental import pallas as pl
from jax.experimental.pallas import tpu as pltpu
from jax.sharding import PartitionSpec as P

epsilon = 1e-05
neg_large = -1e30
slope_base = 0.5
log2_e = 1.4426950408889634
lanes = 128
low = jnp.bfloat16
full = jnp.float32
vmem_bytes = 56 << 20
vmem_less = 24 << 20
cost = {'heads_split': 2000000000, 'heads_third': 2000000000, 'heads_join': 6000000000, 'outer_split': 3000000000}
vmem_back = 56 << 20
vmem_finish = 56 << 20
vmem_big = 56 << 20
vmem_attend = 56 << 20
vmem_end = 56 << 20
vmem_delta = 56 << 20
vmem_plane = 56 << 20

names = ["seqs", "seg", "mem", "rows", "heads", "size"]
names += ["experts", "parts", "share", "cycle", "width", "group"]
Dims = collections.namedtuple("Dims", names)


def dot_nn(left, right):
    return lax.dot_general(left, right, (((1,), (0,)), ((), ())), preferred_element_type=full)


def dot_nt(left, right):
    return lax.dot_general(left, right, (((1,), (1,)), ((), ())), preferred_element_type=full)


def dot_tn(left, right):
    return lax.dot_general(left, right, (((0,), (0,)), ((), ())), preferred_element_type=full)


def norm_parts(values):
    centred = values - jnp.mean(values, axis=-1, keepdims=True)
    spread = jnp.mean(centred * centred, axis=-1, keepdims=True)
    inverse = lax.rsqrt(spread + epsilon)
    return centred * inverse, inverse


def norm_back(grad, hat, inverse, gain_row):
    scaled = grad * gain_row
    along = jnp.mean(scaled * hat, axis=-1, keepdims=True)
    return inverse * (scaled - jnp.mean(scaled, axis=-1, keepdims=True) - hat * along)


smem = pl.BlockSpec(memory_space=pltpu.SMEM)
whole = pl.BlockSpec(memory_space=pltpu.VMEM)
unread = pl.BlockSpec(memory_space=pl.ANY)


def by_step(shape, axis):
    return pl.BlockSpec(shape, lambda i: tuple(i if a == axis else 0 for a in range(len(shape))))


def at_all(shape):
    return pl.BlockSpec(shape, lambda *i: (0,) * len(shape))


def call(kernel, steps, operands, outs, scratch=(), vmem=vmem_bytes, flops=1):
    return pl.pallas_call(
        kernel,
        grid=(steps,),
        out_shape=[jax.ShapeDtypeStruct(shape, kind) for shape, kind, _ in outs],
        in_specs=[spec for _, spec in operands],
        out_specs=[spec for _, _, spec in outs],
        scratch_shapes=list(scratch),
        compiler_params=pltpu.CompilerParams(
            vmem_limit_bytes=vmem, dimension_semantics=("arbitrary",)
        ),
        cost_estimate=pl.CostEstimate(flops=flops, bytes_accessed=1, transcendentals=0),
    )(*[a for a, _ in operands])


def picks(routes, experts):
    slots, tokens = routes.shape
    wide = jnp.concatenate([routes.astype(full), jnp.zeros((8 - slots, tokens), full)], axis=0)
    columns = wide.T
    expert = lax.broadcasted_iota(jnp.int32, (tokens, experts), 1).astype(full)
    total = jnp.zeros((tokens, experts), full)
    for slot in range(slots):
        total = total + (columns[:, slot : slot + 1] == expert).astype(full)
    return total


def fill_wall(wall_ref, wq_ref, wk_ref, wv_ref, wr_ref, d):
    size, experts = d.size, d.experts
    blank = jnp.zeros((lanes - size, d.width), low)
    wall_ref[0:size] = wq_ref[...]
    wall_ref[size:lanes] = jnp.concatenate([wr_ref[0], blank[2 * experts :]], axis=0)
    wall_ref[lanes : lanes + size] = wk_ref[...]
    wall_ref[lanes + size : 2 * lanes] = blank
    for e in range(experts):
        first = (2 + e) * lanes
        wall_ref[first : first + size] = wv_ref[e * size : (e + 1) * size]
        wall_ref[first + size : first + lanes] = blank


def prepare(scal_ref, ctx_ref, wq_ref, wk_ref, wv_ref, wr_ref, wo_ref, wall_ref, exp_ref, out_ref, own_ref, d=None):
    fill_wall(wall_ref.at[0], wq_ref, wk_ref, wv_ref, wr_ref, d)
    ctx = ctx_ref[...].reshape(-1, d.width)
    exp_ref[0] = dot_nt(ctx, wall_ref[0, 2 * lanes :]).astype(low)
    for e in range(d.experts):
        out_ref[0, e * lanes : e * lanes + d.size] = wo_ref[e * d.size : (e + 1) * d.size]
        out_ref[0, e * lanes + d.size : (e + 1) * lanes] = jnp.zeros((lanes - d.size, d.width), low)
    rows = own_ref.shape[1]
    if lanes % rows == 0:
        first = scal_ref[3] * rows
        column = pl.ds(pl.multiple_of(lax.div(first, lanes) * lanes, lanes), lanes)
        turned = wall_ref[0, :, column].T
        for at in range(0, lanes, rows):

            @pl.when(lax.rem(first, lanes) == at)
            def _():
                own_ref[0] = turned[at : at + rows]


def project(
    x_ref, m_ref, vr_ref, mr_ref, or_ref, gain_ref, wq_ref, wk_ref, wv_ref, wr_ref,
    pay_ref, ctx_ref, vgate_ref, ogate_ref, wall_ref, held_ref, d=None
):
    size, experts = d.size, d.experts
    spare = lanes - size

    @pl.when(pl.program_id(0) == 0)
    def _():
        for s in range(d.seqs):
            block = jnp.concatenate([m_ref[s], x_ref[s]], axis=0).astype(full)
            hat, _ = norm_parts(block)
            block_low = (hat * gain_ref[...]).astype(low)
            held_ref[s * d.rows : (s + 1) * d.rows] = block_low
            ctx_ref[s] = block_low

    fill_wall(wall_ref, wq_ref, wk_ref, wv_ref, wr_ref, d)
    ctx = held_ref[...]
    every = dot_nt(ctx, wall_ref[...])
    query = every[:, 0:lanes]
    sig = jax.nn.sigmoid(query[:, size : size + 2 * experts])
    pick = []
    out_pick = []
    out_sig = []
    for s in range(d.seqs):
        pick.append(picks(mr_ref[s, 0], experts))
        pick.append(picks(vr_ref[s, 0], experts))
        out_pick.append(picks(or_ref[s, 0], experts))
        out_sig.append(sig[s * d.rows + d.mem : (s + 1) * d.rows, experts:])
    gate = sig[:, :experts] * jnp.concatenate(pick, axis=0)
    vgate_ref[0] = gate
    ogate_ref[0] = jnp.concatenate(out_sig, axis=0) * jnp.concatenate(out_pick, axis=0)
    high = gate.astype(low)
    rest = (gate - high.astype(full)).astype(low)
    count = d.seqs * d.rows
    value = jnp.zeros((count, lanes), full)
    for e in range(experts):
        value = value + gate[:, e : e + 1] * every[:, (2 + e) * lanes : (3 + e) * lanes]
    lane_at = lax.broadcasted_iota(jnp.int32, (count, lanes), 1)
    query = jnp.where(lane_at < size, query, 0.0).astype(low)
    keys = every[:, lanes : 2 * lanes].astype(low)
    value = jnp.concatenate(
        [value[:, :size].astype(low), high, rest, jnp.zeros((count, spare - 2 * experts), low)], axis=1
    )
    half = d.share // 2
    for s in range(d.seqs):
        mine = slice(s * d.rows, (s + 1) * d.rows)
        for p in range(d.parts):
            first = s * d.rows + d.mem + p * d.share
            pay_ref[p, 0, s, 0 : d.rows, 0:lanes] = keys[mine]
            pay_ref[p, 0, s, 0 : d.rows, lanes:] = value[mine]
            pay_ref[p, 0, s, d.rows :, 0:lanes] = query[first : first + half]
            pay_ref[p, 0, s, d.rows :, lanes:] = query[first + half : first + d.share]


def lane_sums(product, experts):
    slot = lax.broadcasted_iota(jnp.int32, (experts * lanes, lanes), 0) // lanes
    target = lax.broadcasted_iota(jnp.int32, (experts * lanes, lanes), 1)
    ones = (slot == target).astype(full).astype(low)
    high = product.astype(low)
    rest = (product - high.astype(full)).astype(low)
    return (dot_nn(high, ones) + dot_nn(rest, ones))[:, :experts]


def turn_context(scal_ref, ctx_ref, *refs, bits=None):
    first_ref, second_ref = refs[-2:]
    value = ctx_ref[...].reshape(-1, ctx_ref.shape[-1])
    turn(value, first_ref, scal_ref[3], bits[0])
    turn(value, second_ref, scal_ref[3], bits[1])


def key_value(pay_ref, k_ref, v_ref, d):
    for j in range(d.cycle):
        k_ref[j * d.mem : (j + 1) * d.mem] = pay_ref[j, 0 : d.mem, 0:lanes]
        v_ref[j * d.mem : (j + 1) * d.mem] = pay_ref[j, 0 : d.mem, lanes:]
        base = d.cycle * d.mem + j * d.seg
        k_ref[base : base + d.seg] = pay_ref[j, d.mem : d.rows, 0:lanes]
        v_ref[base : base + d.seg] = pay_ref[j, d.mem : d.rows, lanes:]


def query_block(pay_ref, first, d):
    found = []
    for j in range(first, first + d.group):
        found.append(pay_ref[j, d.rows :, 0:lanes])
        found.append(pay_ref[j, d.rows :, lanes:])
    return jnp.concatenate(found, axis=0)


def attend(scal_ref, pay_ref, *refs, d=None):
    att_ref, keep_ref, lse_ref, k_ref, v_ref = refs[-5:]
    share, group = d.share, d.group
    mem_len = d.cycle * d.mem
    ctx_len = d.cycle * d.rows
    length, head, part = scal_ref[0], scal_ref[1], scal_ref[2]
    key_value(pay_ref, k_ref, v_ref, d)
    slope = slope_base * (head + 1).astype(full) / ctx_len * log2_e
    place = lax.broadcasted_iota(jnp.int32, (1, ctx_len), 1) - mem_len
    bias = jnp.where(place < length, place.astype(full) * slope, neg_large)
    q_rows = group * share
    for first in range(0, d.cycle, group):
        width = mem_len + (first + group) * d.seg
        cut = width - group * d.seg
        query = query_block(pay_ref, first, d)
        scores = dot_nt(query, k_ref[0:width]) * (d.size**-0.5 * log2_e) + bias[:, :width]
        row = lax.broadcasted_iota(jnp.int32, (q_rows, group * d.seg), 0)
        col = lax.broadcasted_iota(jnp.int32, (q_rows, group * d.seg), 1)
        row_place = (row // share) * d.seg + part * share + row % share
        tail = jnp.where(col <= row_place, scores[:, cut:], neg_large)
        scores = jnp.concatenate([scores[:, :cut], tail], axis=1)
        top = jnp.max(scores, axis=1, keepdims=True)
        weights = jnp.exp2(scores - top)
        total = jnp.sum(weights, axis=1, keepdims=True)
        attended = dot_nn(weights.astype(low), v_ref[0:width]) / total
        keep_ref[first * share : first * share + q_rows] = attended
        lse_ref[first * share : first * share + q_rows] = top + jnp.log2(total)
        for j in range(group):
            att_ref[first + j] = attended[j * share : (j + 1) * share].astype(low)


def attend_back(
    scal_ref, pay_ref, keep_ref, lse_ref, grad_ref, *refs, d=None
):
    out_ref, k_ref, v_ref, dk_ref, dv_ref = refs[-5:]
    share, group, size = d.share, d.group, d.size
    half = share // 2
    mem_len = d.cycle * d.mem
    ctx_len = d.cycle * d.rows
    length, head, part = scal_ref[0], scal_ref[1], scal_ref[2]
    key_value(pay_ref, k_ref, v_ref, d)
    scale = size**-0.5
    slope = slope_base * (head + 1).astype(full) / ctx_len * log2_e
    place = lax.broadcasted_iota(jnp.int32, (ctx_len, lanes), 0) - mem_len
    bias = jnp.where(place < length, place.astype(full) * slope, neg_large)[:, 0:1]
    dk_ref[...] = jnp.zeros_like(dk_ref)
    dv_ref[...] = jnp.zeros_like(dv_ref)
    q_rows = group * share
    lane_at = lax.broadcasted_iota(jnp.int32, (q_rows, lanes), 1)
    for first in range(0, d.cycle, group):
        width = mem_len + (first + group) * d.seg
        cut = width - group * d.seg
        begin = first * share
        query = query_block(pay_ref, first, d)
        raw = jnp.concatenate([grad_ref[j] for j in range(first, first + group)], axis=0)
        grad = jnp.where(lane_at < size, raw, jnp.zeros_like(raw))
        kept = keep_ref[begin : begin + q_rows]
        delta = jnp.sum(jnp.where(lane_at < size, grad.astype(full) * kept, 0.0), axis=1, keepdims=True)
        both = jnp.concatenate(
            [
                jnp.broadcast_to(delta, (q_rows, lanes)),
                jnp.broadcast_to(lse_ref[begin : begin + q_rows], (q_rows, lanes)),
            ],
            axis=1,
        ).T
        delta_row = both[0:1]
        lse_row = both[lanes : lanes + 1]
        scores = dot_nt(k_ref[0:width], query) * (scale * log2_e) + bias[:width]
        weights = jnp.exp2(scores - lse_row)
        row = lax.broadcasted_iota(jnp.int32, (group * d.seg, q_rows), 0)
        col = lax.broadcasted_iota(jnp.int32, (group * d.seg, q_rows), 1)
        col_place = (col // share) * d.seg + part * share + col % share
        weights = jnp.concatenate([weights[:cut], jnp.where(row <= col_place, weights[cut:], 0.0)], axis=0)
        grad_weights = dot_nt(v_ref[0:width], grad)
        grad_scores = (weights * (grad_weights - delta_row)).astype(low)
        dk_ref[0:width] += dot_nn(grad_scores, query)
        dv_ref[0:width] += dot_nn(weights.astype(low), grad)
        dq = (dot_tn(grad_scores, k_ref[0:width]) * scale).astype(low)
        for j in range(group):
            out_ref[first + j, d.rows :, 0:lanes] = dq[j * share : j * share + half]
            out_ref[first + j, d.rows :, lanes:] = dq[j * share + half : (j + 1) * share]
    for j in range(d.cycle):
        base = mem_len + j * d.seg
        dk = jnp.concatenate([dk_ref[j * d.mem : (j + 1) * d.mem], dk_ref[base : base + d.seg]], axis=0)
        dv = jnp.concatenate([dv_ref[j * d.mem : (j + 1) * d.mem], dv_ref[base : base + d.seg]], axis=0)
        out_ref[j, 0 : d.rows, 0:lanes] = (dk * scale).astype(low)
        out_ref[j, 0 : d.rows, lanes:] = dv.astype(low)


def place_of(mask, bits):
    place = jnp.int32(0)
    for at, bit in enumerate(bits):
        place = place + ((mask >> bit) & 1) * (1 << (len(bits) - 1 - at))
    return place


def turn(value, out_ref, me, bits):
    turned = value.T
    count = 1 << len(bits)
    own = turned.shape[0] // count
    for block in range(count):
        place = place_of(block ^ me, bits)
        side = lax.div(place, count // 2)
        inside = lax.rem(place, count // 2)
        out_ref[side, pl.ds(pl.multiple_of(inside * own, own), own), :] = turned[block * own : (block + 1) * own]


def beside(turn_ref, pack_ref):
    half, tokens = turn_ref.shape[1] // 2, turn_ref.shape[2]
    first = pack_ref.shape[1] - 2 * tokens
    pack_ref[:, first : first + tokens] = turn_ref[1, 0:half]
    pack_ref[:, first + tokens :] = turn_ref[1, half:]


def feed(
    scal_ref, att_ref, ogate_ref, x_ref, gain_ref, live_ref, gf_ref, wo_ref, up_ref, down_ref,
    out_mix_ref, act_ref, pack_ref, out_ref, resid_ref, branch_ref, normed_ref, turned_ref, gatt_ref,
    sum_ref, ffn_ref, back_ref, held_ref, turn_ref, d=None, bits=None
):
    step = pl.program_id(0)
    last = pl.num_programs(0) - 1 - d.heads
    experts = d.experts
    me = scal_ref[3]

    @pl.when(step == 0)
    def _():
        for s in range(d.seqs):
            sum_ref[s * d.seg : (s + 1) * d.seg] = x_ref[s].astype(full)
        ffn_ref[...] = jnp.zeros_like(ffn_ref)
        back_ref[...] = jnp.zeros_like(back_ref)

    @pl.when(step < d.heads)
    def _():
        found = [att_ref[p, 0, s] for s in range(d.seqs) for p in range(d.parts)]
        att = jnp.concatenate(found, axis=0).astype(full)
        gate = ogate_ref[0]
        mixed = jnp.concatenate([(gate[:, e : e + 1] * att).astype(low) for e in range(experts)], axis=1)
        wide = mixed.shape[1]
        out_mix_ref[:, pl.ds(pl.multiple_of(step * wide, lanes), wide)] = mixed
        sum_ref[...] += dot_nn(mixed, wo_ref[0])

    @pl.when(step == d.heads - 1)
    def _():
        hat, _ = norm_parts(sum_ref[...])
        normed = (hat * gain_ref[...]).astype(low)
        held_ref[...] = normed
        if bits is None:
            normed_ref[...] = normed
        else:
            turn(normed, turn_ref, me, bits[1])
            normed_ref[...] = turn_ref[0]
            beside(turn_ref, pack_ref)

    @pl.when((step >= d.heads) & (step <= last))
    def _():
        coeff = 0.7978845608028654
        held = held_ref[...]
        outer_grad = gf_ref[...]
        acts = []
        grads = []
        part = up_ref.shape[1] // 4
        for c in range(4):
            mine = slice(c * part, (c + 1) * part)
            value = dot_nn(held, up_ref[:, mine])
            grad_act = dot_nt(outer_grad, down_ref[mine, :])
            square = value * value
            wave = jnp.tanh(value * (coeff + (0.044715 * coeff) * square))
            rise = 0.5 + 0.5 * wave
            acts.append((value * rise).astype(low))
            slope = rise + (0.5 * value) * (1.0 - wave * wave) * (coeff + (3 * 0.044715 * coeff) * square)
            grads.append((grad_act * slope).astype(low))
        act = jnp.concatenate(acts, axis=1)
        gu = jnp.concatenate(grads, axis=1)
        ffn_ref[...] += dot_nn(act, down_ref[...])
        back_ref[...] += dot_nt(gu, up_ref[...])
        block = step - d.heads
        span = act.shape[1]
        if bits is None:
            pack_ref[:, pl.ds(pl.multiple_of(block * span, span), span)] = gu
            act_ref[:, pl.ds(pl.multiple_of(block * span, span), span)] = act
        else:
            half = 1 << (len(bits[0]) - 1)
            own = act_ref.shape[1] // half
            pack_ref[:, pl.ds(pl.multiple_of(half * own + block * span, lanes), span)] = gu
            for b in range(span // own):
                piece = act[:, b * own : (b + 1) * own]
                place = place_of((block * (span // own) + b) ^ me, bits[0])
                inside = pl.ds(pl.multiple_of(lax.rem(place, half) * own, own), own)

                @pl.when(place < half)
                def _():
                    act_ref[:, inside] = piece

                @pl.when(place >= half)
                def _():
                    pack_ref[:, inside] = piece

    @pl.when(step == last)
    def _():
        residual = sum_ref[...]
        out_ref[...] = ((residual + ffn_ref[...]) * live_ref[...]).astype(low)
        hat, inverse = norm_parts(residual)
        grad = gf_ref[...].astype(full) + norm_back(back_ref[...], hat, inverse, gain_ref[...])
        resid_ref[...] = grad
        branch = grad.astype(low)
        branch_ref[...] = branch
        if bits is None:
            turned_ref[...] = branch
        else:
            turn(branch, turn_ref, me, bits[2])
            turned_ref[...] = turn_ref[0]
            beside(turn_ref, out_mix_ref)

    @pl.when(step > last)
    def _():
        unmix(branch_ref, att_ref, ogate_ref, wo_ref, gatt_ref, d=d)


def unmix(branch_ref, att_ref, ogate_ref, wo_ref, out_ref, d=None):
    size, experts = d.size, d.experts
    tokens = d.seqs * d.seg
    grad_mixed = dot_nt(branch_ref[...], wo_ref[0])
    found = [att_ref[p, 0, s] for s in range(d.seqs) for p in range(d.parts)]
    att = jnp.concatenate(found, axis=0).astype(full)
    gate = ogate_ref[0]
    grad = jnp.zeros((tokens, lanes), full)
    product = []
    for e in range(experts):
        piece = grad_mixed[:, e * lanes : (e + 1) * lanes]
        grad = grad + gate[:, e : e + 1] * piece
        product.append(piece * att)
    logit = lane_sums(jnp.concatenate(product, axis=1), experts) * gate * (1.0 - gate)
    joined = jnp.concatenate(
        [grad[:, :size].astype(low), logit.astype(low), jnp.zeros((tokens, lanes - size - experts), low)], axis=1
    )
    for s in range(d.seqs):
        for p in range(d.parts):
            first = s * d.seg + p * d.share
            out_ref[p, 0, s] = joined[first : first + d.share]


def make_deltas(back_ref, grad_ref, vgate_ref, exp_ref, *refs, d=None):
    size, experts = d.size, d.experts
    q_found, kv_found, lo_found = [], [], []
    for s in range(d.seqs):
        kv = back_ref[0, 0, s, 0 : d.rows, :]
        if d.parts > 1:
            kv = kv.astype(full)
            for p in range(1, d.parts):
                kv = kv + back_ref[p, 0, s, 0 : d.rows, :].astype(full)
            kv = kv.astype(low)
        kv_found.append(kv)
        q_found.append(jnp.zeros((d.mem, lanes), low))
        lo_found.append(jnp.zeros((d.mem, lanes), low))
        for p in range(d.parts):
            q_found.append(back_ref[p, 0, s, d.rows :, 0:lanes])
            q_found.append(back_ref[p, 0, s, d.rows :, lanes:])
            lo_found.append(grad_ref[p, 0, s])
    query = jnp.concatenate(q_found, axis=0)
    kv = jnp.concatenate(kv_found, axis=0)
    out_logit = jnp.concatenate(lo_found, axis=0)[:, size : size + experts]
    gate = vgate_ref[0]
    lane_at = lax.broadcasted_iota(jnp.int32, (d.seqs * d.rows, lanes), 1)
    value = jnp.where(lane_at < size, kv[:, lanes:].astype(full), 0.0)
    product = jnp.concatenate(
        [value * exp_ref[0, :, e * lanes : (e + 1) * lanes].astype(full) for e in range(experts)], axis=1
    )
    logit = (lane_sums(product, experts) * gate * (1.0 - gate)).astype(low)
    first = jnp.concatenate(
        [query[:, :size], logit, out_logit, jnp.zeros((d.seqs * d.rows, lanes - size - 2 * experts), low)], axis=1
    )
    step = pl.program_id(0)
    for at, delta_ref in enumerate(refs[-2:]):

        @pl.when(step // (d.heads // 2) == at)
        def _():
            delta_ref[:, 0:lanes] = first
            delta_ref[:, lanes : 2 * lanes] = kv[:, :lanes]
            for e in range(experts):
                delta_ref[:, (2 + e) * lanes : (3 + e) * lanes] = (gate[:, e : e + 1] * value).astype(low)


def finish(first_ref, second_ref, x_ref, gain_ref, resid_ref, wall_ref, *refs, d=None):
    out_ref, sum_ref = refs[-2:]
    step = pl.program_id(0)

    @pl.when(step == 0)
    def _():
        sum_ref[...] = jnp.zeros_like(sum_ref)

    for at, delta_ref in enumerate((first_ref, second_ref)):

        @pl.when(step // (d.heads // 2) == at)
        def _():
            rows = [delta_ref[s * d.rows + d.mem : (s + 1) * d.rows] for s in range(d.seqs)]
            sum_ref[...] += dot_nn(jnp.concatenate(rows, axis=0), wall_ref[0])

    @pl.when(step == pl.num_programs(0) - 1)
    def _():
        for s in range(d.seqs):
            hat, inverse = norm_parts(x_ref[s].astype(full))
            mine = slice(s * d.seg, (s + 1) * d.seg)
            out_ref[s] = resid_ref[mine] + norm_back(sum_ref[mine], hat, inverse, gain_ref[...])


def both(first, second, axis):
    return jnp.concatenate([first, second], axis=axis)


def send_down(gf_ref, act_ref, act_got_ref, *refs):
    refs[-1][...] = dot_nn(gf_ref[...], both(act_ref[...], act_got_ref[...], 0)).astype(low)


def send_up(left_ref, left_got_ref, gu_ref, gu_got_ref, *refs):
    left = both(left_ref[...], left_got_ref[...], 1)
    refs[-1][...] = dot_nn(left, both(gu_ref[...], gu_got_ref[...], 0)).astype(low)


def cross_down(gf_ref, act_ref, act_got_ref, new_ref, *refs):
    send_ref, keep_ref = refs[-2:]
    total = dot_nn(gf_ref[...], both(act_ref[...], act_got_ref[...], 0)) + new_ref[...].astype(full)
    half = total.shape[1] // 2
    keep_ref[...] = total[:, :half]
    send_ref[...] = total[:, half:].astype(low)


def cross_up(left_ref, left_got_ref, gu_ref, gu_got_ref, new_ref, *refs):
    send_ref, keep_ref = refs[-2:]
    left = both(left_ref[...], left_got_ref[...], 1)
    total = dot_nn(left, both(gu_ref[...], gu_got_ref[...], 0)) + new_ref[...].astype(full)
    half = total.shape[0] // 2
    keep_ref[...] = total[:half]
    send_ref[...] = total[half:].astype(low)


def fold_lanes(keep_ref, got_ref, *refs):
    send_ref, left_ref = refs[-2:]
    total = keep_ref[...] + got_ref[...].astype(full)
    half = total.shape[1] // 2
    left_ref[...] = total[:, :half]
    send_ref[...] = total[:, half:].astype(low)


def end_feed(keep_d_ref, got_d_ref, keep_u_ref, got_u_ref, weight_ref, gain_ref, *refs):
    down_ref, up_ref, norm_ref = refs[-3:]
    down_ref[...] = (keep_d_ref[...] + got_d_ref[...].astype(full)).T
    total = keep_u_ref[...] + got_u_ref[...].astype(full)
    up_ref[...] = total
    along = jnp.sum(total * weight_ref[...].astype(full), axis=1, keepdims=True)
    norm_ref[...] = row_of(along / gain_ref[...])


def outer_send(left_ref, left_got_ref, right_ref, right_got_ref, *refs):
    left = both(left_ref[...], left_got_ref[...], 1)
    refs[-1][...] = dot_nn(left, both(right_ref[...], right_got_ref[...], 0)).astype(low)


def outer_split(left_ref, left_got_ref, right_ref, right_got_ref, new_ref, *refs):
    send_ref, keep_ref = refs[-2:]
    left = both(left_ref[...], left_got_ref[...], 1)
    total = dot_nn(left, both(right_ref[...], right_got_ref[...], 0)) + new_ref[...].astype(full)
    half = total.shape[0] // 2
    keep_ref[...] = total[:half]
    send_ref[...] = total[half:].astype(low)


def heads_send(a_ref, a_got_ref, b_ref, b_got_ref, da_ref, da_got_ref, db_ref, db_got_ref, *refs):
    a_out, b_out = refs[-2:]
    a_out[...] = dot_nn(both(a_ref[0], a_got_ref[...], 1), both(da_ref[...], da_got_ref[...], 0)).astype(low)
    b_out[...] = dot_nn(both(b_ref[0], b_got_ref[...], 1), both(db_ref[...], db_got_ref[...], 0)).astype(low)


def heads_split(
    a_ref, a_got_ref, b_ref, b_got_ref, da_ref, da_got_ref, db_ref, db_got_ref, new_a_ref, new_b_ref, *refs
):
    outs = refs[-4:]
    left = both(a_ref[0], a_got_ref[...], 1), both(b_ref[0], b_got_ref[...], 1)
    right = both(da_ref[...], da_got_ref[...], 0), both(db_ref[...], db_got_ref[...], 0)
    for at, new_ref in enumerate((new_a_ref, new_b_ref)):
        total = dot_nn(left[at], right[at]) + new_ref[...].astype(full)
        half = total.shape[0] // 2
        outs[2 + at][...] = total[:half]
        outs[at][...] = total[half:].astype(low)


def heads_third(keep_a_ref, keep_b_ref, got_a_ref, got_b_ref, *refs):
    outs = refs[-4:]
    for at, (keep_ref, got_ref) in enumerate(((keep_a_ref, got_a_ref), (keep_b_ref, got_b_ref))):
        half = keep_ref.shape[0] // 2
        outs[2 + at][...] = keep_ref[:half] + got_ref[:half].astype(full)
        outs[at][...] = (keep_ref[half:] + got_ref[half:].astype(full)).astype(low)


def heads_join(keep_a_ref, keep_b_ref, keep_o_ref, got_a_ref, got_b_ref, got_o_ref, *refs):
    send_ref, left_ref = refs[-2:]
    half = send_ref.shape[0]
    first = 0
    for keep_ref, got_ref in ((keep_a_ref, got_a_ref), (keep_b_ref, got_b_ref), (keep_o_ref, got_o_ref)):
        here = slice(first, first + keep_ref.shape[1])
        left_ref[:, here] = keep_ref[:half] + got_ref[:half].astype(full)
        send_ref[:, here] = (keep_ref[half:] + got_ref[half:].astype(full)).astype(low)
        first += keep_ref.shape[1]


def fold(keep_ref, got_ref, *refs):
    send_ref, left_ref = refs[-2:]
    half = keep_ref.shape[0] // 2
    left_ref[...] = keep_ref[:half] + got_ref[:half].astype(full)
    send_ref[...] = (keep_ref[half:] + got_ref[half:].astype(full)).astype(low)


def row_of(column):
    n = column.shape[0]
    same = lax.broadcasted_iota(jnp.int32, (n, n), 0) == lax.broadcasted_iota(jnp.int32, (n, n), 1)
    return jnp.sum(jnp.where(same, column, 0.0), axis=0, keepdims=True)


def assemble(keep_ref, got_ref, wall_ref, gain_ref, *refs, d=None):
    q_ref, k_ref, v_ref, r_ref, out_ref, norm_ref = refs[-6:]
    size, experts = d.size, d.experts
    slots = 2 + experts

    def total(first):
        here = slice(first * lanes, (first + 1) * lanes)
        return keep_ref[:, here] + got_ref[:, here].astype(full)

    every = [[total(h * slots + at) for at in range(slots)] for h in range(d.heads)]
    along = jnp.zeros(every[0][0].shape, full)
    for h in range(d.heads):
        for at in range(slots):
            along = along + every[h][at] * wall_ref[h, :, at * lanes : (at + 1) * lanes].astype(full)
    norm_ref[...] = row_of(jnp.sum(along, axis=1, keepdims=True) / gain_ref[...])
    q_ref[...] = jnp.concatenate([one[0][:, :size] for one in every], axis=1)
    k_ref[...] = jnp.concatenate([one[1][:, :size] for one in every], axis=1)
    v_ref[...] = jnp.concatenate([one[2 + e][:, :size] for one in every for e in range(experts)], axis=1)
    values = [one[0][:, size : size + experts] for one in every]
    outs = [one[0][:, size + experts : size + 2 * experts] for one in every]
    r_ref[...] = jnp.concatenate(values + outs, axis=1)
    out_ref[...] = jnp.concatenate([total(d.heads * slots + at)[:, :size] for at in range(d.heads * experts)], axis=1)


class Halver:
    def __init__(self):
        self.cycle = lax.axis_size("seq")
        self.width = lax.axis_size("batch")
        self.low_bits = self.width.bit_length() - 1
        self.high_bits = self.cycle.bit_length() - 1
        self.me = lax.axis_index("seq") * self.width + lax.axis_index("batch")

    def swap(self, value, bit):
        if bit < self.low_bits:
            axis, size, mask = "batch", self.width, 1 << bit
        else:
            axis, size, mask = "seq", self.cycle, 1 << (bit - self.low_bits)
        return lax.ppermute(value, axis, [(i, i ^ mask) for i in range(size)])

    def order(self, bits):
        count = len(bits)
        found = np.zeros(1 << count, np.int32)
        for place in range(1 << count):
            for at, bit in enumerate(bits):
                if place >> (count - 1 - at) & 1:
                    found[place] |= 1 << bit
        return found


def halve(value, axis):
    size = value.shape[axis] // 2
    return (
        lax.slice_in_dim(value, 0, size, axis=axis),
        lax.slice_in_dim(value, size, 2 * size, axis=axis),
    )


def reduced(halver, product, bits, axis):
    got = halver.swap(product(2, 4).astype(low), bits[0])
    got_keep, got_send = halve(got, axis)
    got = halver.swap((product(1, 2) + got_send.astype(full)).astype(low), bits[1])
    keep = product(0, 1) + got_keep.astype(full) + got.astype(full)
    for bit in bits[2:]:
        keep, send = halve(keep, axis)
        keep = keep + halver.swap(send.astype(low), bit).astype(full)
    return keep


def local(
    inputs, memory, cotangent, valid_len, value_routes, memory_routes, output_routes, norm1_gain, norm2_gain,
    query_weight, key_weight, value_weight, router_weight, output_weight, up_weight, down_weight
):
    seqs, seg, width = inputs.shape
    mem = memory.shape[1]
    rows = seg + mem
    heads = value_routes.shape[2]
    slots_count = value_routes.shape[3]
    qk_width = query_weight.shape[1]
    size = qk_width // heads
    experts = value_weight.shape[1] // qk_width
    span = experts * size
    ff = up_weight.shape[1]
    tokens = seqs * seg
    halver = Halver()
    cycle = halver.cycle
    parts = cycle // (seqs * heads)
    share = seg // parts
    d = Dims(seqs, seg, mem, rows, heads, size, experts, parts, share, cycle, width, 2)
    pay_rows = rows + share // 2
    at = lax.axis_index("seq")
    my_seq = at % seqs
    my_head = at // seqs % heads
    my_part = at // (seqs * heads)
    my_length = lax.dynamic_index_in_dim(valid_len, my_seq, 0, keepdims=False)
    scal = jnp.stack([my_length, my_head, my_part, halver.me]).astype(jnp.int32)
    gain_one = norm1_gain.reshape(1, width)
    gain_two = norm2_gain.reshape(1, width)
    place = at * seg + jnp.arange(seg, dtype=jnp.int32)
    live = (place[None, :] < valid_len[:, None]).astype(full).reshape(tokens, 1)
    grad_ffn = (cotangent.reshape(tokens, width).astype(full) * live).astype(low)
    wq, wk, wv, wr = query_weight.T, key_weight.T, value_weight.T, router_weight.T
    wr = jnp.concatenate(
        [wr[: heads * experts].reshape(heads, experts, width), wr[heads * experts :].reshape(heads, experts, width)], axis=1
    )
    v_routes = jnp.transpose(value_routes, (0, 2, 3, 1))
    m_routes = jnp.transpose(memory_routes, (0, 2, 3, 1))
    o_routes = jnp.transpose(output_routes, (0, 2, 3, 1))
    blocks = cycle * halver.width
    own = width // blocks
    wide = experts * lanes
    wall_rows = 2 * lanes + wide
    wall_shape = (heads, wall_rows, width)

    def routes_spec(count):
        return by_step((seqs, 1, slots_count, count), 1)

    def head_spec(*tail):
        return by_step((parts, 1, seqs) + tail, 1)

    def given(array):
        return (array, at_all(array.shape))

    def made(shape, kind):
        return (shape, kind, at_all(shape))

    pay, ctx, vgate, ogate = call(
        functools.partial(project, d=d),
        heads,
        [
            given(inputs),
            given(memory),
            (v_routes, routes_spec(seg)),
            (m_routes, routes_spec(mem)),
            (o_routes, routes_spec(seg)),
            given(gain_one),
            (wq, by_step((size, width), 0)),
            (wk, by_step((size, width), 0)),
            (wv, by_step((span, width), 0)),
            (wr, by_step((1, 2 * experts, width), 0)),
        ],
        [
            ((parts, heads, seqs, pay_rows, 2 * lanes), low, head_spec(pay_rows, 2 * lanes)),
            made((seqs, rows, width), low),
            ((heads, seqs * rows, experts), full, by_step((1, seqs * rows, experts), 0)),
            ((heads, tokens, experts), full, by_step((1, tokens, experts), 0)),
        ],
        scratch=[pltpu.VMEM(wall_shape[1:], low), pltpu.VMEM((seqs * rows, width), low)],
    )
    wall, expanded, wo, wall_own = call(
        functools.partial(prepare, d=d),
        heads,
        [
            (scal, smem),
            given(ctx),
            (wq, by_step((size, width), 0)),
            (wk, by_step((size, width), 0)),
            (wv, by_step((span, width), 0)),
            (wr, by_step((1, 2 * experts, width), 0)),
            (output_weight, by_step((span, width), 0)),
        ],
        [
            (wall_shape, low, by_step((1,) + wall_shape[1:], 0)),
            ((heads, seqs * rows, wide), low, by_step((1, seqs * rows, wide), 0)),
            ((heads, wide, width), low, by_step((1, wide, width), 0)),
            ((heads, own, wall_rows), low, by_step((1, own, wall_rows), 0)),
        ],
    )
    up_own = lax.dynamic_slice_in_dim(up_weight, halver.me * own, own, axis=0)
    bit_count = halver.low_bits + halver.high_bits
    low_b = list(range(halver.low_bits))
    high_b = list(range(halver.low_bits, bit_count))
    core, chip_y, chip_x, chip_z = low_b[:1], low_b[1:], high_b[:1], high_b[1:]
    down_bits = core + chip_x + chip_y + chip_z
    up_bits = core + chip_y + chip_z + chip_x
    out_bits = core + chip_z[:1] + chip_x + chip_y + chip_z[1:]
    fast = own == 32 and ff == blocks * lanes and len(chip_z) == 2 and len(chip_y) == 1

    qkv_bits = down_bits, core + chip_y + chip_z[:1] + chip_x + chip_z[1:]
    grad_ffn_t = grad_ffn.T
    after = [wo]
    if fast:
        turned_ctx = (2, width // 2, seqs * rows)
        ctx_a, ctx_b = call(
            functools.partial(turn_context, bits=qkv_bits),
            1,
            [(scal, smem), given(ctx), (wo, unread)],
            [made(turned_ctx, low), made(turned_ctx, low)],
        )
        grad_ffn_both = jnp.concatenate([grad_ffn_t, halver.swap(grad_ffn_t, core[0])], axis=1)
        ctx_a_got, ctx_b_got = halver.swap(ctx_a[1], core[0]), halver.swap(ctx_b[1], core[0])
        after += [grad_ffn_both, ctx_a_got, ctx_b_got]
    pay = lax.all_to_all(pay.reshape(cycle, pay_rows, 2 * lanes), "seq", 0, 0)
    att, kept, lse = call(
        functools.partial(attend, d=d),
        1,
        [(scal, smem), given(pay)] + [(a, unread) for a in after],
        [
            made((cycle, share, lanes), low),
            made((cycle * share, lanes), full),
            made((cycle * share, 1), full),
        ],
        scratch=[pltpu.VMEM((cycle * rows, lanes), low)] * 2,
        vmem=vmem_attend,
    )
    att = lax.all_to_all(att, "seq", 0, 0)
    steps = 4
    att_heads = att.reshape(parts, heads, seqs, share, lanes)

    def ff_block(i):
        return jnp.clip(i - heads, 0, steps - 1)

    def head_of(i):
        return jnp.where(i < heads + steps, jnp.minimum(i, heads - 1), i - heads - steps)

    def back_of(i):
        return jnp.maximum(i - heads - steps, 0)

    turned_shape = (width // 2, tokens) if fast else (tokens, width)
    act_shape = (tokens, ff // 2) if fast else (tokens, ff)
    pack_shape = (tokens, ff // 2 + ff + 2 * tokens) if fast else (tokens, ff)
    mix_shape = (tokens, heads * wide + 2 * tokens) if fast else (tokens, heads * wide)
    mixed, act, pack, output, grad_residual, grad_branch, normed, turned, grad_out = call(
        functools.partial(feed, d=d, bits=(tuple(down_bits), tuple(up_bits), tuple(out_bits)) if fast else None),
        2 * heads + steps,
        [
            (scal, smem),
            (att_heads, pl.BlockSpec((parts, 1, seqs, share, lanes), lambda i: (0, head_of(i), 0, 0, 0))),
            (ogate, pl.BlockSpec((1, tokens, experts), lambda i: (head_of(i), 0, 0))),
            given(inputs),
            given(gain_two),
            given(live),
            given(grad_ffn),
            (wo, pl.BlockSpec((1, wide, width), lambda i: (head_of(i), 0, 0))),
            (up_weight, pl.BlockSpec((width, ff // steps), lambda i: (0, ff_block(i)))),
            (down_weight, pl.BlockSpec((ff // steps, width), lambda i: (ff_block(i), 0))),
        ],
        [
            made(mix_shape, low),
            made(act_shape, low),
            made(pack_shape, low),
            made((tokens, width), low),
            made((tokens, width), full),
            made((tokens, width), low),
            made(turned_shape, low),
            made(turned_shape, low),
            (
                (parts, heads, seqs, share, lanes),
                low,
                pl.BlockSpec((parts, 1, seqs, share, lanes), lambda i: (0, back_of(i), 0, 0, 0)),
            ),
        ],
        scratch=[pltpu.VMEM((tokens, width), full)] * 3
        + [pltpu.VMEM((tokens, width), low), pltpu.VMEM((2, width // 2, tokens), low)],
    )
    output = output.reshape(seqs, seg, width)

    pay_shape = (cycle, pay_rows, 2 * lanes)

    def attended_back(grad_att, *after):
        (back,) = call(
            functools.partial(attend_back, d=d),
            1,
            [(scal, smem), given(pay), given(kept), given(lse), given(grad_att)]
            + [(a, unread) for a in after],
            [made(pay_shape, low)],
            scratch=[pltpu.VMEM((cycle * rows, lanes), low)] * 2 + [pltpu.VMEM((cycle * rows, lanes), full)] * 2,
            vmem=vmem_back,
        )
        return back

    delta_shape = (seqs * rows, heads // 2 * wall_rows)
    first_half = pl.BlockSpec((seqs * rows, wall_rows), lambda i: (0, jnp.minimum(i, heads // 2 - 1)))
    second_half = pl.BlockSpec((seqs * rows, wall_rows), lambda i: (0, jnp.maximum(i - heads // 2, 0)))

    def head_deltas(returned, grad_out, *after):
        return call(
            functools.partial(make_deltas, d=d),
            heads,
            [
                (returned.reshape(parts, heads, seqs, pay_rows, 2 * lanes), head_spec(pay_rows, 2 * lanes)),
                (grad_out, head_spec(share, lanes)),
                (vgate, by_step((1, seqs * rows, experts), 0)),
                (expanded, by_step((1, seqs * rows, wide), 0)),
            ]
            + [(a, unread) for a in after],
            [(delta_shape, low, first_half), (delta_shape, low, second_half)],
            vmem=vmem_delta,
            flops=cost.get("deltas", 1),
        )

    def finished(deltas, *after):
        (input_grad,) = call(
            functools.partial(finish, d=d),
            heads,
            [
                (deltas[0], first_half),
                (deltas[1], second_half),
                given(inputs),
                given(gain_one),
                given(grad_residual),
                (wall, by_step((1, wall_rows, width), 0)),
            ]
            + [(a, unread) for a in after],
            [made((seqs, seg, width), full)],
            scratch=[pltpu.VMEM((tokens, width), full)],
            vmem=vmem_finish,
        )
        return input_grad

    def rows_by(array, order):
        cols = array.T.reshape(blocks, -1, array.shape[0])
        return jnp.take(cols, order ^ halver.me, axis=0).reshape(-1, array.shape[0])

    def row_product(left, right):
        quarter = left.shape[0] // 4
        return lambda lo, hi: dot_nn(left[lo * quarter : hi * quarter], right)

    gain_rows = lax.dynamic_slice_in_dim(jnp.stack([norm1_gain, norm2_gain], axis=1), halver.me * own, own, axis=0)
    if fast:
        split = 2
        pack_got = halver.swap(pack, core[0])
        mixed_got = halver.swap(mixed, core[0])
        assert width // 4 == tokens

        def down_products(piece):
            return [
                (grad_ffn_both, by_step((width // split, 2 * tokens), 0)),
                (act, pl.BlockSpec((tokens, ff // 4), lambda i: (0, piece))),
                (pack_got, pl.BlockSpec((tokens, ff // 4), lambda i: (0, piece))),
            ]

        def up_products(piece):
            step_u = ff // split
            first_u, first_n = ff // 2 // step_u, (ff // 2 + ff) // tokens
            right = pl.BlockSpec((tokens, step_u), lambda i: (0, first_u + i))
            return [
                (normed, pl.BlockSpec((tokens, tokens), lambda i: (piece, 0))),
                (pack_got, pl.BlockSpec((tokens, tokens), lambda i: (0, first_n + piece))),
                (pack, right),
                (pack_got, right),
            ]

        def d_made(cols, kind):
            return ((width, cols), kind, by_step((width // split, cols), 0))

        def u_made(rows_u, kind):
            return ((rows_u, ff), kind, by_step((rows_u, ff // split), 1))

        def out_products(piece):
            first_t = heads * wide // tokens
            right = by_step((tokens, heads * wide // split), 1)
            return [
                (turned, pl.BlockSpec((tokens, tokens), lambda i: (piece, 0))),
                (mixed_got, pl.BlockSpec((tokens, tokens), lambda i: (0, first_t + piece))),
                (mixed, right),
                (mixed_got, right),
            ]

        def out_made(rows_o, kind):
            return ((rows_o, heads * wide), kind, by_step((rows_o, heads * wide // split), 1))

        span_d = heads // 2 * wall_rows

        def head_products(piece):
            half = width // 4
            turned_spec = pl.BlockSpec((1, half, seqs * rows), lambda i: (0, piece, 0))
            got_spec = pl.BlockSpec((half, seqs * rows), lambda i: (piece, 0))
            right = by_step((seqs * rows, wall_rows), 1)
            return [
                (ctx_a, turned_spec), (ctx_a_got, got_spec), (ctx_b, turned_spec), (ctx_b_got, got_spec),
                (deltas[0], right), (deltas_a, right), (deltas[1], right), (deltas_b, right),
            ]

        def head_made(count, kind):
            return ((count, span_d), kind, by_step((count, wall_rows), 1))

        def then(*after):
            return [(a, unread) for a in after]

        def stage(kernel, steps, operands, after, outs, vmem=vmem_less):
            name = kernel.__name__
            return call(kernel, steps, operands + then(*after), outs, vmem=vmem, flops=cost.get(name, 1))

        def step_fold(kernel, keep, got, axis, *after):
            shape = tuple(n // 2 if a == axis else n for a, n in enumerate(keep.shape))
            return stage(kernel, 1, [given(keep), given(got)], after, [made(shape, low), made(shape, full)])

        grad_att = lax.all_to_all(grad_out.reshape(cycle, share, lanes), "seq", 0, 0)
        (send_u,) = stage(send_up, split, up_products(1), [grad_out], [u_made(width // 4, low)], vmem_plane)
        got_u = halver.swap(send_u, up_bits[1])
        back = attended_back(grad_att, send_u)
        returned = lax.all_to_all(back, "seq", 0, 0)
        (send_d,) = stage(send_down, split, down_products(1), [back], [d_made(ff // 4, low)], vmem_plane)
        got_d = halver.swap(send_d, down_bits[1])
        (send_o,) = stage(outer_send, split, out_products(1), [send_d], [out_made(width // 4, low)], vmem_plane)
        got_o = halver.swap(send_o, out_bits[1])
        deltas = head_deltas(returned, grad_out, send_o)
        deltas_a, deltas_b = halver.swap(deltas[0], core[0]), halver.swap(deltas[1], core[0])
        send_o, keep_o = stage(
            outer_split,
            split,
            out_products(0) + [(got_o, by_step((width // 4, heads * wide // split), 1))],
            [deltas[0]],
            [out_made(width // 8, low), out_made(width // 8, full)],
            vmem_big,
        )
        got_o = halver.swap(send_o, out_bits[2])
        send_a, send_b = stage(
            heads_send, heads // 2, head_products(1), [send_o], [head_made(width // 4, low)] * 2,
            vmem_big,
        )
        got_a, got_b = halver.swap(send_a, qkv_bits[0][1]), halver.swap(send_b, qkv_bits[1][1])
        send_u, keep_u = stage(
            cross_up,
            split,
            up_products(0) + [(got_u, by_step((width // 4, ff // split), 1))],
            [send_a],
            [u_made(width // 8, low), u_made(width // 8, full)],
            vmem_big,
        )
        got_u = halver.swap(send_u, up_bits[2])
        send_d, keep_d = stage(
            cross_down,
            split,
            down_products(0) + [(got_d, by_step((width // split, ff // 4), 0))],
            [send_u],
            [d_made(ff // 8, low), d_made(ff // 8, full)],
            vmem_big,
        )
        got_d = halver.swap(send_d, down_bits[2])
        input_grad = finished(deltas, send_d)
        send_a, send_b, keep_a, keep_b = stage(
            heads_split,
            heads // 2,
            head_products(0)
            + [(got_a, by_step((width // 4, wall_rows), 1)), (got_b, by_step((width // 4, wall_rows), 1))],
            [input_grad],
            [head_made(width // 8, low)] * 2 + [head_made(width // 8, full)] * 2,
            vmem_big,
        )
        got_a, got_b = halver.swap(send_a, qkv_bits[0][2]), halver.swap(send_b, qkv_bits[1][2])
        send_u, keep_u = step_fold(fold, keep_u, got_u, 0, send_a)
        got_u = halver.swap(send_u, up_bits[3])
        send_d, keep_d = step_fold(fold_lanes, keep_d, got_d, 1, send_u)
        got_d = halver.swap(send_d, down_bits[3])
        send_o, keep_o = step_fold(fold, keep_o, got_o, 0, send_d)
        got_o = halver.swap(send_o, out_bits[3])
        a_shape = (width // 16, span_d)
        send_a, send_b, keep_a, keep_b = stage(
            heads_third,
            1,
            [given(a) for a in (keep_a, keep_b, got_a, got_b)],
            [send_o],
            [made(a_shape, low)] * 2 + [made(a_shape, full)] * 2,
        )
        got_a, got_b = halver.swap(send_a, qkv_bits[0][3]), halver.swap(send_b, qkv_bits[1][3])
        send_u, keep_u = step_fold(fold, keep_u, got_u, 0, send_a)
        got_u = halver.swap(send_u, up_bits[4])
        send_d, keep_d = step_fold(fold_lanes, keep_d, got_d, 1, send_u)
        got_d = halver.swap(send_d, down_bits[4])
        h_shape = (own, 2 * span_d + heads * wide)
        send_h, keep_h = stage(
            heads_join,
            1,
            [given(a) for a in (keep_a, keep_b, keep_o, got_a, got_b, got_o)],
            [send_d],
            [made(h_shape, low), made(h_shape, full)],
        )
        got_h = halver.swap(send_h, chip_z[1])
        down_grad, up_grad, norm2_grad = stage(
            end_feed,
            1,
            [given(a) for a in (keep_d, got_d, keep_u, got_u, up_own, gain_rows[:, 1:2])],
            [send_h],
            [made((lanes, width), full), made((own, ff), full), made((1, own), full)],
        )
        norm2_grad = norm2_grad.reshape(own)
        flat = [heads * size, heads * size, heads * span, 2 * heads * experts, heads * span]
        query_grad, key_grad, value_grad, router_grad, outproj_grad, norm1_grad = call(
            functools.partial(assemble, d=d),
            1,
            [given(a) for a in (keep_h, got_h, wall_own, gain_rows[:, 0:1])] + then(up_grad),
            [made((own, cols), full) for cols in flat] + [made((1, own), full)],
            vmem=vmem_less,
        )
        norm1_grad = norm1_grad.reshape(own)
        outproj_grad = outproj_grad.T
    else:
        act = act.reshape(tokens, blocks, -1)
        act = jnp.take(act, halver.order(down_bits) ^ halver.me, axis=1).reshape(tokens, -1)

        def down_product(lo, hi):
            quarter = ff // 4
            return dot_nn(grad_ffn_t, act[:, lo * quarter : hi * quarter])

        up_product = row_product(rows_by(normed, halver.order(up_bits)), pack)
        out_product = row_product(rows_by(grad_branch, halver.order(out_bits)), mixed)
        grad_att = lax.all_to_all(grad_out.reshape(cycle, share, lanes), "seq", 0, 0)
        back = attended_back(grad_att)
        returned = lax.all_to_all(back, "seq", 0, 0)
        deltas = head_deltas(returned, grad_out)
        input_grad = finished(deltas)
        down_grad = reduced(halver, down_product, down_bits, 1).T
        up_grad = reduced(halver, up_product, up_bits, 0)
        outproj_grad = reduced(halver, out_product, out_bits, 0)
        outproj_grad = outproj_grad.reshape(own, heads * experts, lanes)[:, :, :size].reshape(own, -1).T
        qkv_left = rows_by(ctx.reshape(seqs * rows, width), halver.order(qkv_bits[0]))
        qkv_product = row_product(qkv_left, jnp.concatenate(deltas, axis=1))
        by_head = reduced(halver, qkv_product, qkv_bits[0], 0).reshape(own, heads, 2 + experts, lanes)
        query_grad = by_head[:, :, 0, :size].reshape(own, -1)
        key_grad = by_head[:, :, 1, :size].reshape(own, -1)
        value_grad = by_head[:, :, 2:, :size].reshape(own, -1)
        router_grad = jnp.concatenate(
            [by_head[:, :, 0, size + i * experts : size + (i + 1) * experts].reshape(own, -1) for i in range(2)], axis=1
        )

        def own_rows(array):
            return lax.dynamic_slice_in_dim(array, halver.me * own, own, axis=0).astype(full)

        norm1_grad = (
            jnp.sum(own_rows(query_weight) * query_grad, axis=1)
            + jnp.sum(own_rows(key_weight) * key_grad, axis=1)
            + jnp.sum(own_rows(value_weight) * value_grad, axis=1)
            + jnp.sum(own_rows(router_weight) * router_grad, axis=1)
        ) / gain_rows[:, 0]
        norm2_grad = jnp.sum(own_rows(up_weight) * up_grad, axis=1) / gain_rows[:, 1]
    return (
        output, input_grad, norm1_grad, norm2_grad, query_grad, key_grad, value_grad, router_grad,
        outproj_grad, up_grad, down_grad,
    )


def solution(mesh):
    token = P("batch", "seq", None)
    routes = P("batch", "seq", None, None)
    spread = ("seq", "batch")
    return jax.shard_map(
        local,
        mesh=mesh,
        in_specs=(token, token, token, P("batch"), routes, routes, routes) + (P(),) * 9,
        out_specs=(
            token, token, P(spread), P(spread), P(spread, None), P(spread, None), P(spread, None), P(spread, None),
            P(None, spread), P(spread, None), P(spread, None),
        ),
        check_vma=False,
    )
```

profile of v0, /device:TPU:0, one launch (start us, length us, event | category | flops | bytes accessed | tf_op | source)
XLA Modules:
  0.0 274.3 jit_solution(902132264570201156)
XLA Ops:
  2.3 8.5 %shard_map.239 = (bf16[1,4,2,256,256]{4,3,2,1,0:T(8,128)(2,1)}, bf16[2,192,1024]{2,1,0:T(8,128)(2,1)}, f32[4,384,5]{2,1,0:T(8,128)}, f32[4,256,5]{2,1,0:T(8,128)}) custom-call(bf16[2,128,1024]{2,1,0:T(8,128)(2,1)} %x_ref.5, bf16[2,64,1024]{2,1,0:T(8,128)(2,1)} %m_ref.1, s32[2,4,2,128]{3,2,1,0:T(2,128)} %bitcast.50, s32[2,4,2,64]{3,2,1,0:T(2,128)} %bitcast.51, ...), custom_call_target="tpu_custom_call" | custom-call | flops 1 | bytes 1 | tf_op jit(solution)/shard_map/pallas_call | solution.py:74
  10.8 7.4 %all-to-all-start = ((bf16[8,256,256]{2,1,0:T(8,128)(2,1)}), bf16[8,256,256]{2,1,0:T(8,128)(2,1)S(1)}, u32[]{:S(2)}, u32[]{:S(2)}) async-start(bf16[8,256,256]{2,1,0:T(8,128)(2,1)} %bitcast.43), calls=%async_computation | async-start | bytes 2097152 | tf_op jit(solution)/shard_map/all_to_all | solution.py:827
  21.0 11.2 %shard_map.240 = (bf16[4,896,1024]{2,1,0:T(8,128)(2,1)}, bf16[4,384,640]{2,1,0:T(8,128)(2,1)}, bf16[4,640,1024]{2,1,0:T(8,128)(2,1)}, bf16[4,32,896]{2,1,0:T(8,128)(2,1)}) custom-call(s32[4]{0:T(128)} %pad_add_fusion.scal_ref, bf16[2,192,1024]{2,1,0:T(8,128)(2,1)} %get-tuple-element.72.ctx_ref, bf16[448,1024]{1,0:T(8,128)(2,1)} %bitcast.38, ...), custom_call_target="tpu_custom_call" | custom-call | flops 1 | bytes 1 | tf_op jit(solution)/shard_map/pallas_call | solution.py:74
  39.8 4.1 %all-to-all-done.pay_ref = bf16[8,256,256]{2,1,0:T(8,128)(2,1)S(1)} async-done(((bf16[8,256,256]{2,1,0:T(8,128)(2,1)}), bf16[8,256,256]{2,1,0:T(8,128)(2,1)S(1)}, u32[]{:S(2)}, u32[]{:S(2)}) %all-to-all-start) | async-done | bytes 1048608 | tf_op jit(solution)/shard_map/all_to_all | solution.py:827
  45.0 4.8 %shard_map.242 = (bf16[8,128,128]{2,1,0:T(8,128)(2,1)}, f32[1024,128]{1,0:T(8,128)}, f32[1024,1]{1,0:T(8,128)}) custom-call(s32[4]{0:T(128)} %pad_add_fusion.scal_ref, bf16[8,256,256]{2,1,0:T(8,128)(2,1)} %copy-done.17, bf16[4,640,1024]{2,1,0:T(8,128)(2,1)} %get-tuple-element.73.refs_0_.wo_ref, bf16[1024,512]{1,0:T(8,128)(2,1)} %pad_maximum_fusion.refs_1_.gf_ref, ...), custom_call_target="tpu_custom_call" | custom-call | flops 1 | bytes 1 | tf_op jit(solution)/shard_map/pallas_call | solution.py:74
  55.3 7.2 %all-to-all-done.1 = bf16[8,128,128]{2,1,0:T(8,128)(2,1)S(1)} async-done(((bf16[8,128,128]{2,1,0:T(8,128)(2,1)}), bf16[8,128,128]{2,1,0:T(8,128)(2,1)S(1)}, u32[]{:S(2)}, u32[]{:S(2)}) %all-to-all-start.1) | async-done | bytes 262176 | tf_op jit(solution)/shard_map/all_to_all | solution.py:840
  63.2 28.4 %shard_map.243 = (bf16[256,3072]{1,0:T(8,128)(2,1)}, bf16[256,2048]{1,0:T(8,128)(2,1)}, bf16[256,6656]{1,0:T(8,128)(2,1)}, bf16[256,1024]{1,0:T(8,128)(2,1)}, f3...) custom-call(s32[4]{0:T(128)} %pad_add_fusion.scal_ref, ...), custom_call_target="tpu_custom_call" | custom-call | flops 1 | bytes 1 | tf_op jit(solution)/shard_map/pallas_call | solution.py:74
  91.6 4.1 %all-to-all-start.2 = ((bf16[8,128,128]{2,1,0:T(8,128)(2,1)}), bf16[8,128,128]{2,1,0:T(8,128)(2,1)}, u32[]{:S(2)}, u32[]{:S(2)}) async-start(bf16[8,128,128]{2,1,0:T(8,128)(2,1)} %bitcast.41), calls=%async_computation.2 | async-start | bytes 524288 | tf_op jit(solution)/shard_map/all_to_all | solution.py:1023
  99.7 4.1 %shard_map.244.refs_0_ = bf16[256,4096]{1,0:T(8,128)(2,1)} custom-call(bf16[512,256]{1,0:T(8,128)(2,1)} %get-tuple-element.82.left_ref, bf16[256,6656]{1,0:T(8,128)(2,1)} %copy-done.16, bf16[256,6656]{1,0:T(8,128)(2,1)} %get-tuple-element.83.gu_ref, bf16[256,6656]{1,0:T(8,128)(2,1)} %copy-done.16, bf16[1,4,2,128,128]{4,3,2,1,0:T(8,128)(2,1)} %get-tuple-element.81.refs_0_.grad_ref), custom_call_target="tpu_custom_call" | custom-call | flops 1 | bytes 1 | tf_op jit(solution)/shard_map/pallas_call | solution.py:74
  105.6 6.0 %shard_map.245.refs_0_ = bf16[8,256,256]{2,1,0:T(8,128)(2,1)} custom-call(s32[4]{0:T(128)} %pad_add_fusion.scal_ref, bf16[8,256,256]{2,1,0:T(8,128)(2,1)} %copy-done.17, f32[1024,128]{1,0:T(8,128)} %get-tuple-element.79.keep_ref, f32[1024,1]{1,0:T(8,128)} %get-tuple-element.80.lse_ref, bf16[8,128,128]{2,1,0:T(8,128)(2,1)} %all-to-all-done.2.grad_ref, ...), custom_call_target="tpu_custom_call" | custom-call | flops 1 | bytes 1 | tf_op jit(solution)/shard_map/pallas_call | solution.py:74
  111.5 3.9 %all-to-all-start.3 = ((bf16[8,256,256]{2,1,0:T(8,128)(2,1)}), bf16[8,256,256]{2,1,0:T(8,128)(2,1)S(1)}, u32[]{:S(2)}, u32[]{:S(2)}) async-start(bf16[8,256,256]{2,1,0:T(8,128)(2,1)} %shard_map.245.refs_0_), calls=%async_computation.3 | async-start | bytes 2097152 | tf_op jit(solution)/shard_map/all_to_all | solution.py:1027
  128.7 12.7 %all-to-all-done.3 = bf16[8,256,256]{2,1,0:T(8,128)(2,1)S(1)} async-done(((bf16[8,256,256]{2,1,0:T(8,128)(2,1)}), bf16[8,256,256]{2,1,0:T(8,128)(2,1)S(1)}, u32[]{:S(2)}, u32[]{:S(2)}) %all-to-all-start.3) | async-done | bytes 1048608 | tf_op jit(solution)/shard_map/all_to_all | solution.py:1027
  142.3 6.5 %shard_map.248 = (bf16[384,1792]{1,0:T(8,128)(2,1)}, bf16[384,1792]{1,0:T(8,128)(2,1)}) custom-call(bf16[1,4,2,256,256]{4,3,2,1,0:T(8,128)(2,1)} %bitcast.36, bf16[1,4,2,128,128]{4,3,2,1,0:T(8,128)(2,1)} %get-tuple-element.81.refs_0_.grad_ref, f32[4,384,5]{2,1,0:T(8,128)} %get-tuple-element.84.vgate_ref, bf16[4,384,640]{2,1,0:T(8,128)(2,1)} %get-tuple-element.85.exp_ref, ...), custom_call_target="tpu_custom_call" | custom-call | flops 1 | bytes 1 | tf_op jit(solution)/shard_map/pallas_call | solution.py:74
  149.4 13.8 %collective-permute-done.9.new_ref = bf16[256,2560]{1,0:T(8,128)(2,1)} collective-permute-done((bf16[256,2560]{1,0:T(8,128)(2,1)}, bf16[256,2560]{1,0:T(8,128)(2,1)}, u32[]{:S(2)}, u32[]{:S(2)}) %collective-permute-start.9) | collective-permute-done | bytes 1310752 | tf_op jit(solution)/shard_map/ppermute | solution.py:673
  168.4 5.0 %shard_map.250 = (bf16[256,1792]{1,0:T(8,128)(2,1)}, bf16[256,1792]{1,0:T(8,128)(2,1)}) custom-call(bf16[2,512,384]{2,1,0:T(8,128)(2,1)} %get-tuple-element.74.a_ref, bf16[512,384]{1,0:T(8,128)(2,1)} %copy-done.23, bf16[2,512,384]{2,1,0:T(8,128)(2,1)} %get-tuple-element.75.b_ref, bf16[512,384]{1,0:T(8,128)(2,1)} %copy-done.24, ...), custom_call_target="tpu_custom_call" | custom-call | flops 1 | bytes 1 | tf_op jit(solution)/shard_map/pallas_call | solution.py:74
  176.0 4.8 %shard_map.251 = (bf16[128,4096]{1,0:T(8,128)(2,1)}, f32[128,4096]{1,0:T(8,128)}) custom-call(bf16[512,256]{1,0:T(8,128)(2,1)} %get-tuple-element.82.left_ref, bf16[256,6656]{1,0:T(8,128)(2,1)} %copy-done.16, bf16[256,6656]{1,0:T(8,128)(2,1)} %get-tuple-element.83.gu_ref, bf16[256,6656]{1,0:T(8,128)(2,1)} %copy-done.16, ...), custom_call_target="tpu_custom_call" | custom-call | flops 1 | bytes 1 | tf_op jit(solution)/shard_map/pallas_call | solution.py:74
  181.4 4.0 %shard_map.252 = (bf16[1024,512]{1,0:T(8,128)(2,1)}, f32[1024,512]{1,0:T(8,128)}) custom-call(bf16[1024,512]{1,0:T(8,128)(2,1)} %pad_maximum_fusion.refs_1_.gf_ref, bf16[256,2048]{1,0:T(8,128)(2,1)} %get-tuple-element.88.act_ref, bf16[256,6656]{1,0:T(8,128)(2,1)} %copy-done.16, bf16[1024,1024]{1,0:T(8,128)(2,1)} %collective-permute-done.5.new_ref, ...), custom_call_target="tpu_custom_call" | custom-call | flops 1 | bytes 1 | tf_op jit(solution)/shard_map/pallas_call | solution.py:74
  186.5 8.1 %shard_map.253.refs_0_ = f32[2,128,1024]{2,1,0:T(8,128)} custom-call(bf16[384,1792]{1,0:T(8,128)(2,1)} %get-tuple-element.89.refs_0_.da_ref.first_ref, bf16[384,1792]{1,0:T(8,128)(2,1)} %get-tuple-element.90.db_ref.second_ref, bf16[2,128,1024]{2,1,0:T(8,128)(2,1)} %x_ref.5, f32[1,1024]{1,0:T(1,128)} %bitcast.46, f32[256,1024]{1,0:T(8,128)} %get-tuple-element.91.resid_ref, ...), custom_call_target="tpu_custom_call" | custom-call | flops 1 | bytes 1 | tf_op jit(solution)/shard_map/pallas_call | solution.py:74
  200.1 5.7 %shard_map.254 = (bf16[128,1792]{1,0:T(8,128)(2,1)}, bf16[128,1792]{1,0:T(8,128)(2,1)}, f32[128,1792]{1,0:T(8,128)}, f32[128,1792]{1,0:T(8,128)}) custom-call(bf16[2,512,384]{2,1,0:T(8,128)(2,1)} %get-tuple-element.74.a_ref, bf16[512,384]{1,0:T(8,128)(2,1)} %copy-done.23, bf16[2,512,384]{2,1,0:T(8,128)(2,1)} %get-tuple-element.75.b_ref, ...), custom_call_target="tpu_custom_call" | custom-call | flops 2000000000 | bytes 1 | tf_op jit(solution)/shard_map/pallas_call | solution.py:74
  212.6 7.9 %collective-permute-done.15.got_ref = bf16[1024,512]{1,0:T(8,128)(2,1)} collective-permute-done((bf16[1024,512]{1,0:T(8,128)(2,1)}, bf16[1024,512]{1,0:T(8,128)(2,1)}, u32[]{:S(2)}, u32[]{:S(2)}) %collective-permute-start.15) | collective-permute-done | bytes 1048608 | tf_op jit(solution)/shard_map/ppermute | solution.py:673
  237.4 6.0 %collective-permute-done.20.got_ref = bf16[1024,256]{1,0:T(8,128)(2,1)S(1)} collective-permute-done((bf16[1024,256]{1,0:T(8,128)(2,1)}, bf16[1024,256]{1,0:T(8,128)(2,1)S(1)}, u32[]{:S(2)}, u32[]{:S(2)}) %collective-permute-start.20) | collective-permute-done | bytes 524320 | tf_op jit(solution)/shard_map/ppermute | solution.py:673
  245.9 4.4 %collective-permute-done.17.got_a_ref = bf16[64,1792]{1,0:T(8,128)(2,1)} collective-permute-done((bf16[64,1792]{1,0:T(8,128)(2,1)S(1)}, bf16[64,1792]{1,0:T(8,128)(2,1)}, u32[]{:S(2)}, u32[]{:S(2)}) %collective-permute-start.17) | collective-permute-done | bytes 229408 | tf_op jit(solution)/shard_map/ppermute | solution.py:673
  253.1 12.1 %collective-permute-done.23.got_d_ref = bf16[1024,128]{1,0:T(8,128)(2,1)S(1)} collective-permute-done((bf16[1024,128]{1,0:T(8,128)(2,1)S(1)}, bf16[1024,128]{1,0:T(8,128)(2,1)S(1)}, u32[]{:S(2)}, u32[]{:S(2)}) %collective-permute-start.23) | collective-permute-done | bytes 262176 | tf_op jit(solution)/shard_map/ppermute | solution.py:673
  266.4 5.7 %collective-permute-done.22.got_ref = bf16[32,6144]{1,0:T(8,128)(2,1)S(1)} collective-permute-done((bf16[32,6144]{1,0:T(8,128)(2,1)S(1)}, bf16[32,6144]{1,0:T(8,128)(2,1)S(1)}, u32[]{:S(2)}, u32[]{:S(2)}) %collective-permute-start.22) | collective-permute-done | bytes 393248 | tf_op jit(solution)/shard_map/ppermute | solution.py:673
  (147 shorter events, 86.8 us)
Async XLA Ops:
  10.8 33.2 %all-to-all-start = ((bf16[8,256,256]{2,1,0:T(8,128)(2,1)}), bf16[8,256,256]{2,1,0:T(8,128)(2,1)S(1)}, u32[]{:S(2)}, u32[]{:S(2)}) async-start(bf16[8,256,256]{2,1,0:T(8,128)(2,1)} %bitcast.43), calls=%async_computation | async-start | bytes 2097152 | tf_op jit(solution)/shard_map/all_to_all | solution.py:827
  19.1 18.7 %collective-permute-start = (bf16[1024,256]{1,0:T(8,128)(2,1)S(1)}, bf16[1024,256]{1,0:T(8,128)(2,1)}, u32[]{:S(2)}, u32[]{:S(2)}) collective-permute-start(bf16[1024,256]{1,0:T(8,128)(2,1)S(1)} %fusion.4), channel_id=1, source_target_pairs={{0,1},{1,0},{2,3},{3,2},{4,5},{5,4},{6,7},{7,6},{8,9},{9,8},{10,11... | collective-permute-start | bytes 1572872 | tf_op jit(solution)/shard_map/ppermute | solution.py:673
  91.6 13.9 %all-to-all-start.2 = ((bf16[8,128,128]{2,1,0:T(8,128)(2,1)}), bf16[8,128,128]{2,1,0:T(8,128)(2,1)}, u32[]{:S(2)}, u32[]{:S(2)}) async-start(bf16[8,128,128]{2,1,0:T(8,128)(2,1)} %bitcast.41), calls=%async_computation.2 | async-start | bytes 524288 | tf_op jit(solution)/shard_map/all_to_all | solution.py:1023
  111.5 29.8 %all-to-all-start.3 = ((bf16[8,256,256]{2,1,0:T(8,128)(2,1)}), bf16[8,256,256]{2,1,0:T(8,128)(2,1)S(1)}, u32[]{:S(2)}, u32[]{:S(2)}) async-start(bf16[8,256,256]{2,1,0:T(8,128)(2,1)} %shard_map.245.refs_0_), calls=%async_computation.3 | async-start | bytes 2097152 | tf_op jit(solution)/shard_map/all_to_all | solution.py:1027
  123.9 39.2 %collective-permute-start.9 = (bf16[256,2560]{1,0:T(8,128)(2,1)}, bf16[256,2560]{1,0:T(8,128)(2,1)}, u32[]{:S(2)}, u32[]{:S(2)}) collective-permute-start(bf16[256,2560]{1,0:T(8,128)(2,1)} %shard_map.247.refs_0_), channel_id=1, source_target_pairs={{0,8},{4,12},{8,0},{12,4},{16,24},{20,28},{24,16},{28,20},{1,9},{5... | collective-permute-start | bytes 3932168 | tf_op jit(solution)/shard_map/ppermute | solution.py:673
  125.7 50.3 %collective-permute-start.6 = (bf16[256,4096]{1,0:T(8,128)(2,1)S(1)}, bf16[256,4096]{1,0:T(8,128)(2,1)}, u32[]{:S(2)}, u32[]{:S(2)}) collective-permute-start(bf16[256,4096]{1,0:T(8,128)(2,1)S(1)} %copy-done.18), channel_id=1, source_target_pairs={{0,2},{1,3},{2,0},{3,1},{4,6},{5,7},{6,4},{7,5},{8,10},{9,11},{10,... | collective-permute-start | bytes 6291464 | tf_op jit(solution)/shard_map/ppermute | solution.py:673
  127.2 54.2 %collective-permute-start.5 = (bf16[1024,1024]{1,0:T(8,128)(2,1)}, bf16[1024,1024]{1,0:T(8,128)(2,1)}, u32[]{:S(2)}, u32[]{:S(2)}) collective-permute-start(bf16[1024,1024]{1,0:T(8,128)(2,1)} %shard_map.246.refs_0_), channel_id=1, source_target_pairs={{0,4},{4,0},{8,12},{12,8},{16,20},{20,16},{24,28},{28,24},{1,5},{5... | collective-permute-start | bytes 6291464 | tf_op jit(solution)/shard_map/ppermute | solution.py:673
  148.9 18.0 %collective-permute-start.7 = (bf16[384,1792]{1,0:T(8,128)(2,1)}, bf16[384,1792]{1,0:T(8,128)(2,1)S(1)}, u32[]{:S(2)}, u32[]{:S(2)}) collective-permute-start(bf16[384,1792]{1,0:T(8,128)(2,1)} %get-tuple-element.89.refs_0_.da_ref.first_ref), channel_id=1, source_target_pairs={{0,1},{1,0},{2,3},{3,2},{4,5},{5,4},{6,7},{7,6},{8,9},{9,8},{10,11... | collective-permute-start | bytes 4128776 | tf_op jit(solution)/shard_map/ppermute | solution.py:673
  148.9 18.0 %collective-permute-start.8 = (bf16[384,1792]{1,0:T(8,128)(2,1)}, bf16[384,1792]{1,0:T(8,128)(2,1)S(1)}, u32[]{:S(2)}, u32[]{:S(2)}) collective-permute-start(bf16[384,1792]{1,0:T(8,128)(2,1)} %get-tuple-element.90.db_ref.second_ref), channel_id=1, source_target_pairs={{0,1},{1,0},{2,3},{3,2},{4,5},{5,4},{6,7},{7,6},{8,9},{9,8},{10,11... | collective-permute-start | bytes 4128776 | tf_op jit(solution)/shard_map/ppermute | solution.py:673
  173.4 24.8 %collective-permute-start.10 = (bf16[256,1792]{1,0:T(8,128)(2,1)}, bf16[256,1792]{1,0:T(8,128)(2,1)S(1)}, u32[]{:S(2)}, u32[]{:S(2)}) collective-permute-start(bf16[256,1792]{1,0:T(8,128)(2,1)} %get-tuple-element.94.refs_0_), channel_id=1, source_target_pairs={{0,4},{4,0},{8,12},{12,8},{16,20},{20,16},{24,28},{28,24},{1,5},{5... | collective-permute-start | bytes 2752520 | tf_op jit(solution)/shard_map/ppermute | solution.py:673
  174.5 23.7 %collective-permute-start.11 = (bf16[256,1792]{1,0:T(8,128)(2,1)}, bf16[256,1792]{1,0:T(8,128)(2,1)S(1)}, u32[]{:S(2)}, u32[]{:S(2)}) collective-permute-start(bf16[256,1792]{1,0:T(8,128)(2,1)} %get-tuple-element.97), channel_id=1, source_target_pairs={{0,2},{1,3},{2,0},{3,1},{4,6},{5,7},{6,4},{7,5},{8,10},{9,11},{10,... | collective-permute-start | bytes 2752520 | tf_op jit(solution)/shard_map/ppermute | solution.py:673
  180.8 28.4 %collective-permute-start.16 = (bf16[128,4096]{1,0:T(8,128)(2,1)}, bf16[128,4096]{1,0:T(8,128)(2,1)S(1)}, u32[]{:S(2)}, u32[]{:S(2)}) collective-permute-start(bf16[128,4096]{1,0:T(8,128)(2,1)} %get-tuple-element.95.refs_0_), channel_id=1, source_target_pairs={{0,8},{4,12},{8,0},{12,4},{16,24},{20,28},{24,16},{28,20},{1,9},{5... | collective-permute-start | bytes 3145736 | tf_op jit(solution)/shard_map/ppermute | solution.py:673
  185.4 35.1 %collective-permute-start.15 = (bf16[1024,512]{1,0:T(8,128)(2,1)}, bf16[1024,512]{1,0:T(8,128)(2,1)}, u32[]{:S(2)}, u32[]{:S(2)}) collective-permute-start(bf16[1024,512]{1,0:T(8,128)(2,1)} %get-tuple-element.96.refs_0_), channel_id=1, source_target_pairs={{0,2},{1,3},{2,0},{3,1},{4,6},{5,7},{6,4},{7,5},{8,10},{9,11},{10,... | collective-permute-start | bytes 3145736 | tf_op jit(solution)/shard_map/ppermute | solution.py:673
  185.9 37.4 %collective-permute-start.14 = (bf16[128,2560]{1,0:T(8,128)(2,1)}, bf16[128,2560]{1,0:T(8,128)(2,1)}, u32[]{:S(2)}, u32[]{:S(2)}) collective-permute-start(bf16[128,2560]{1,0:T(8,128)(2,1)} %get-tuple-element.93.refs_0_), channel_id=1, source_target_pairs={{0,4},{4,0},{8,12},{12,8},{16,20},{20,16},{24,28},{28,24},{1,5},{5... | collective-permute-start | bytes 1966088 | tf_op jit(solution)/shard_map/ppermute | solution.py:673
  205.8 24.5 %collective-permute-start.12 = (bf16[128,1792]{1,0:T(8,128)(2,1)}, bf16[128,1792]{1,0:T(8,128)(2,1)}, u32[]{:S(2)}, u32[]{:S(2)}) collective-permute-start(bf16[128,1792]{1,0:T(8,128)(2,1)} %get-tuple-element.100.refs_0_), channel_id=1, source_target_pairs={{0,2},{1,3},{2,0},{3,1},{4,6},{5,7},{6,4},{7,5},{8,10},{9,11},{10,... | collective-permute-start | bytes 1376264 | tf_op jit(solution)/shard_map/ppermute | solution.py:673
  206.8 23.6 %collective-permute-start.13 = (bf16[128,1792]{1,0:T(8,128)(2,1)}, bf16[128,1792]{1,0:T(8,128)(2,1)}, u32[]{:S(2)}, u32[]{:S(2)}) collective-permute-start(bf16[128,1792]{1,0:T(8,128)(2,1)} %get-tuple-element.101), channel_id=1, source_target_pairs={{0,8},{4,12},{8,0},{12,4},{16,24},{20,28},{24,16},{28,20},{1,9},{5... | collective-permute-start | bytes 1376264 | tf_op jit(solution)/shard_map/ppermute | solution.py:673
  212.3 24.9 %collective-permute-start.21 = (bf16[64,4096]{1,0:T(8,128)(2,1)}, bf16[64,4096]{1,0:T(8,128)(2,1)S(1)}, u32[]{:S(2)}, u32[]{:S(2)}) collective-permute-start(bf16[64,4096]{1,0:T(8,128)(2,1)} %get-tuple-element.105.refs_0_), channel_id=1, source_target_pairs={{0,16},{4,20},{8,24},{12,28},{16,0},{20,4},{24,8},{28,12},{1,17},{... | collective-permute-start | bytes 1572872 | tf_op jit(solution)/shard_map/ppermute | solution.py:673
  222.7 20.6 %collective-permute-start.20 = (bf16[1024,256]{1,0:T(8,128)(2,1)}, bf16[1024,256]{1,0:T(8,128)(2,1)S(1)}, u32[]{:S(2)}, u32[]{:S(2)}) collective-permute-start(bf16[1024,256]{1,0:T(8,128)(2,1)} %get-tuple-element.106.refs_0_), channel_id=1, source_target_pairs={{0,8},{4,12},{8,0},{12,4},{16,24},{20,28},{24,16},{28,20},{1,9},{5... | collective-permute-start | bytes 1572872 | tf_op jit(solution)/shard_map/ppermute | solution.py:673
  226.1 19.8 %collective-permute-start.19 = (bf16[64,2560]{1,0:T(8,128)(2,1)}, bf16[64,2560]{1,0:T(8,128)(2,1)}, u32[]{:S(2)}, u32[]{:S(2)}) collective-permute-start(bf16[64,2560]{1,0:T(8,128)(2,1)} %get-tuple-element.107.refs_0_), channel_id=1, source_target_pairs={{0,2},{1,3},{2,0},{3,1},{4,6},{5,7},{6,4},{7,5},{8,10},{9,11},{10,... | collective-permute-start | bytes 983048 | tf_op jit(solution)/shard_map/ppermute | solution.py:673
  234.0 16.3 %collective-permute-start.17 = (bf16[64,1792]{1,0:T(8,128)(2,1)S(1)}, bf16[64,1792]{1,0:T(8,128)(2,1)}, u32[]{:S(2)}, u32[]{:S(2)}) collective-permute-start(bf16[64,1792]{1,0:T(8,128)(2,1)S(1)} %get-tuple-element.111.refs_0_), channel_id=1, source_target_pairs={{0,8},{4,12},{8,0},{12,4},{16,24},{20,28},{24,16},{28,20},{1,9},{5... | collective-permute-start | bytes 688136 | tf_op jit(solution)/shard_map/ppermute | solution.py:673
  234.1 16.2 %collective-permute-start.18 = (bf16[64,1792]{1,0:T(8,128)(2,1)}, bf16[64,1792]{1,0:T(8,128)(2,1)}, u32[]{:S(2)}, u32[]{:S(2)}) collective-permute-start(bf16[64,1792]{1,0:T(8,128)(2,1)} %get-tuple-element.112), channel_id=1, source_target_pairs={{0,4},{4,0},{8,12},{12,8},{16,20},{20,16},{24,28},{28,24},{1,5},{5... | collective-permute-start | bytes 688136 | tf_op jit(solution)/shard_map/ppermute | solution.py:673
  237.3 28.0 %collective-permute-start.24 = (bf16[32,4096]{1,0:T(8,128)(2,1)S(1)}, bf16[32,4096]{1,0:T(8,128)(2,1)S(1)}, u32[]{:S(2)}, u32[]{:S(2)}) collective-permute-start(bf16[32,4096]{1,0:T(8,128)(2,1)S(1)} %get-tuple-element.115.refs_0_), channel_id=1, source_target_pairs={{0,4},{4,0},{8,12},{12,8},{16,20},{20,16},{24,28},{28,24},{1,5},{5... | collective-permute-start | bytes 786440 | tf_op jit(solution)/shard_map/ppermute | solution.py:673
  243.5 21.8 %collective-permute-start.23 = (bf16[1024,128]{1,0:T(8,128)(2,1)S(1)}, bf16[1024,128]{1,0:T(8,128)(2,1)S(1)}, u32[]{:S(2)}, u32[]{:S(2)}) collective-permute-start(bf16[1024,128]{1,0:T(8,128)(2,1)S(1)} %get-tuple-element.116.refs_0_), channel_id=1, source_target_pairs={{0,16},{4,20},{8,24},{12,28},{16,0},{20,4},{24,8},{28,12},{1,17},{... | collective-permute-start | bytes 786440 | tf_op jit(solution)/shard_map/ppermute | solution.py:673
  251.7 20.4 %collective-permute-start.22 = (bf16[32,6144]{1,0:T(8,128)(2,1)S(1)}, bf16[32,6144]{1,0:T(8,128)(2,1)S(1)}, u32[]{:S(2)}, u32[]{:S(2)}) collective-permute-start(bf16[32,6144]{1,0:T(8,128)(2,1)S(1)} %get-tuple-element.118.refs_0_), channel_id=1, source_target_pairs={{0,16},{4,20},{8,24},{12,28},{16,0},{20,4},{24,8},{28,12},{1,17},{... | collective-permute-start | bytes 1179656 | tf_op jit(solution)/shard_map/ppermute | solution.py:673
  (38 other events, 203.9 us)
where the time goes:
time: 276 us; the launch traced here: 274 us
  Pallas kernels  122 us (44%)
  waiting for transfers between devices  86.3 us (31%)
  starting transfers between devices  39.1 us (14%)
  local copies, waits for them, and re-layouts  21.7 us (8%)
  other arithmetic  4.5 us (2%)
    pallas_call x25, Pallas kernels, call(): pl.pallas_call(kernel, grid=(steps,), out_shape=[jax.ShapeDtypeStruct(sha...  122 us
    ppermute x25, waiting for transfers between devices, swap(): return lax.ppermute(value, axis, [(i, i ^ mask) for i in range(size)])  60.4 us
    ppermute x25, starting transfers between devices, swap(): return lax.ppermute(value, axis, [(i, i ^ mask) for i in range(size)])  20.1 us
    unnamed x68, local copies, waits for them, and re-layouts  15 us
    all_to_all x1, waiting for transfers between devices, local(): returned = lax.all_to_all(back, 'seq', 0, 0)  12.7 us
    all_to_all x1, starting transfers between devices, local(): pay = lax.all_to_all(pay.reshape(cycle, pay_rows, 2 * lanes), 'seq', 0, 0)  7.42 us
    all_to_all x1, waiting for transfers between devices, local(): att = lax.all_to_all(att, 'seq', 0, 0)  7.18 us
  transfers between devices with their start and end apart: 29, of which 14 were waited for; matrix products, arithmetic and copies ran while one was open for 4% of the time, Pallas kernels for 27%

commit v1 on v0

--- a/solution.py
+++ b/solution.py
@@ -18,7 +18,7 @@
 full = jnp.float32
 vmem_bytes = 56 << 20
 vmem_less = 24 << 20
-cost = {'heads_split': 2000000000, 'heads_third': 2000000000, 'heads_join': 6000000000, 'outer_split': 3000000000}
+cost = {'heads_split': 4000000000, 'heads_third': 4000000000, 'heads_last': 4000000000, 'cross_down': 2000000000, 'end_feed': 6000000000, 'assemble': 3000000000}
 vmem_back = 56 << 20
 vmem_finish = 56 << 20
 vmem_big = 56 << 20
@@ -100,7 +100,15 @@
     size, experts = d.size, d.experts
     blank = jnp.zeros((lanes - size, d.width), low)
     wall_ref[0:size] = wq_ref[...]
-    wall_ref[size:lanes] = jnp.concatenate([wr_ref[0], blank[2 * experts :]], axis=0)
+    router = wr_ref[...]
+    count = router.shape[0] // 2
+    for h in range(d.heads):
+
+        @pl.when(pl.program_id(0) == h)
+        def _():
+            mine = [router[at + h * experts : at + (h + 1) * experts] for at in (0, count)]
+            wall_ref[size:lanes] = jnp.concatenate(mine + [blank[2 * experts :]], axis=0)
+
     wall_ref[lanes : lanes + size] = wk_ref[...]
     wall_ref[lanes + size : 2 * lanes] = blank
     for e in range(experts):
@@ -160,8 +168,6 @@
     gate = sig[:, :experts] * jnp.concatenate(pick, axis=0)
     vgate_ref[0] = gate
     ogate_ref[0] = jnp.concatenate(out_sig, axis=0) * jnp.concatenate(out_pick, axis=0)
-    high = gate.astype(low)
-    rest = (gate - high.astype(full)).astype(low)
     count = d.seqs * d.rows
     value = jnp.zeros((count, lanes), full)
     for e in range(experts):
@@ -169,18 +175,12 @@
     lane_at = lax.broadcasted_iota(jnp.int32, (count, lanes), 1)
     query = jnp.where(lane_at < size, query, 0.0).astype(low)
     keys = every[:, lanes : 2 * lanes].astype(low)
-    value = jnp.concatenate(
-        [value[:, :size].astype(low), high, rest, jnp.zeros((count, spare - 2 * experts), low)], axis=1
-    )
-    half = d.share // 2
+    value = value.astype(low)
     for s in range(d.seqs):
         mine = slice(s * d.rows, (s + 1) * d.rows)
         for p in range(d.parts):
             first = s * d.rows + d.mem + p * d.share
-            pay_ref[p, 0, s, 0 : d.rows, 0:lanes] = keys[mine]
-            pay_ref[p, 0, s, 0 : d.rows, lanes:] = value[mine]
-            pay_ref[p, 0, s, d.rows :, 0:lanes] = query[first : first + half]
-            pay_ref[p, 0, s, d.rows :, lanes:] = query[first + half : first + d.share]
+            pay_ref[p, 0, s] = payload(keys[mine], value[mine], query[first : first + d.share], d)
 
 
 def lane_sums(product, experts):
@@ -199,20 +199,45 @@
     turn(value, second_ref, scal_ref[3], bits[1])
 
 
+def folded_in(d):
+    half = d.share // 2
+    return 2 * d.rows == 6 * half and 7 * (lanes - d.size) == d.size
+
+
+def payload_rows(d):
+    return 2 * d.rows + (d.share // 2 if folded_in(d) else d.share)
+
+
+def payload(keys, values, queries, d):
+    size, half = d.size, d.share // 2
+    if not folded_in(d):
+        return jnp.concatenate([keys, values, queries], axis=0)
+    rows = jnp.concatenate([keys, values, queries[:half]], axis=0)
+    step = lanes - size
+    spare = [queries[half:, at : at + step] for at in range(0, size, step)]
+    return jnp.concatenate([rows[:, :size], jnp.concatenate(spare, axis=0)], axis=1)
+
+
+def payload_queries(block, d):
+    size, half = d.size, d.share // 2
+    blank = jnp.zeros((d.share, lanes - size), block.dtype)
+    if not folded_in(d):
+        return jnp.concatenate([block[2 * d.rows :, :size], blank], axis=1)
+    rest = jnp.concatenate([block[at * half : (at + 1) * half, size:] for at in range(7)], axis=1)
+    return jnp.concatenate([jnp.concatenate([block[2 * d.rows :, :size], rest], axis=0), blank], axis=1)
+
+
 def key_value(pay_ref, k_ref, v_ref, d):
     for j in range(d.cycle):
-        k_ref[j * d.mem : (j + 1) * d.mem] = pay_ref[j, 0 : d.mem, 0:lanes]
-        v_ref[j * d.mem : (j + 1) * d.mem] = pay_ref[j, 0 : d.mem, lanes:]
+        k_ref[j * d.mem : (j + 1) * d.mem] = pay_ref[j, 0 : d.mem]
+        v_ref[j * d.mem : (j + 1) * d.mem] = pay_ref[j, d.rows : d.rows + d.mem]
         base = d.cycle * d.mem + j * d.seg
-        k_ref[base : base + d.seg] = pay_ref[j, d.mem : d.rows, 0:lanes]
-        v_ref[base : base + d.seg] = pay_ref[j, d.mem : d.rows, lanes:]
+        k_ref[base : base + d.seg] = pay_ref[j, d.mem : d.rows]
+        v_ref[base : base + d.seg] = pay_ref[j, d.rows + d.mem : 2 * d.rows]
 
 
 def query_block(pay_ref, first, d):
-    found = []
-    for j in range(first, first + d.group):
-        found.append(pay_ref[j, d.rows :, 0:lanes])
-        found.append(pay_ref[j, d.rows :, lanes:])
+    found = [payload_queries(pay_ref[j], d) for j in range(first, first + d.group)]
     return jnp.concatenate(found, axis=0)
 
 
@@ -252,7 +277,6 @@
 ):
     out_ref, k_ref, v_ref, dk_ref, dv_ref = refs[-5:]
     share, group, size = d.share, d.group, d.size
-    half = share // 2
     mem_len = d.cycle * d.mem
     ctx_len = d.cycle * d.rows
     length, head, part = scal_ref[0], scal_ref[1], scal_ref[2]
@@ -265,6 +289,7 @@
     dv_ref[...] = jnp.zeros_like(dv_ref)
     q_rows = group * share
     lane_at = lax.broadcasted_iota(jnp.int32, (q_rows, lanes), 1)
+    query_grads = []
     for first in range(0, d.cycle, group):
         width = mem_len + (first + group) * d.seg
         cut = width - group * d.seg
@@ -294,15 +319,13 @@
         dk_ref[0:width] += dot_nn(grad_scores, query)
         dv_ref[0:width] += dot_nn(weights.astype(low), grad)
         dq = (dot_tn(grad_scores, k_ref[0:width]) * scale).astype(low)
-        for j in range(group):
-            out_ref[first + j, d.rows :, 0:lanes] = dq[j * share : j * share + half]
-            out_ref[first + j, d.rows :, lanes:] = dq[j * share + half : (j + 1) * share]
+        query_grads.append(dq)
     for j in range(d.cycle):
         base = mem_len + j * d.seg
         dk = jnp.concatenate([dk_ref[j * d.mem : (j + 1) * d.mem], dk_ref[base : base + d.seg]], axis=0)
         dv = jnp.concatenate([dv_ref[j * d.mem : (j + 1) * d.mem], dv_ref[base : base + d.seg]], axis=0)
-        out_ref[j, 0 : d.rows, 0:lanes] = (dk * scale).astype(low)
-        out_ref[j, 0 : d.rows, lanes:] = dv.astype(low)
+        dq = query_grads[j // group][j % group * share : (j % group + 1) * share]
+        out_ref[j] = payload((dk * scale).astype(low), dv.astype(low), dq, d)
 
 
 def place_of(mask, bits):
@@ -332,11 +355,13 @@
 
 def feed(
     scal_ref, att_ref, ogate_ref, x_ref, gain_ref, live_ref, gf_ref, wo_ref, up_ref, down_ref,
-    out_mix_ref, act_ref, pack_ref, out_ref, resid_ref, branch_ref, normed_ref, turned_ref, gatt_ref,
-    sum_ref, ffn_ref, back_ref, held_ref, turn_ref, d=None, bits=None
+    mix_hbm, act_hbm, pack_hbm, out_ref, resid_ref, branch_ref, normed_ref, turned_ref, gatt_ref,
+    sum_ref, ffn_ref, back_ref, held_ref, turn_ref, out_mix_ref, act_ref, pack_ref, copied, d=None, bits=None
 ):
     step = pl.program_id(0)
-    last = pl.num_programs(0) - 1 - d.heads
+    together = wo_ref.shape[0]
+    steps_h = d.heads // together
+    last = pl.num_programs(0) - 1 - steps_h
     experts = d.experts
     me = scal_ref[3]
 
@@ -347,17 +372,20 @@
         ffn_ref[...] = jnp.zeros_like(ffn_ref)
         back_ref[...] = jnp.zeros_like(back_ref)
 
-    @pl.when(step < d.heads)
+    @pl.when(step < steps_h)
     def _():
-        found = [att_ref[p, 0, s] for s in range(d.seqs) for p in range(d.parts)]
-        att = jnp.concatenate(found, axis=0).astype(full)
-        gate = ogate_ref[0]
-        mixed = jnp.concatenate([(gate[:, e : e + 1] * att).astype(low) for e in range(experts)], axis=1)
-        wide = mixed.shape[1]
-        out_mix_ref[:, pl.ds(pl.multiple_of(step * wide, lanes), wide)] = mixed
-        sum_ref[...] += dot_nn(mixed, wo_ref[0])
-
-    @pl.when(step == d.heads - 1)
+        total = sum_ref[...]
+        for k in range(together):
+            found = [att_ref[p, k, s] for s in range(d.seqs) for p in range(d.parts)]
+            att = jnp.concatenate(found, axis=0).astype(full)
+            gate = ogate_ref[k]
+            mixed = jnp.concatenate([(gate[:, e : e + 1] * att).astype(low) for e in range(experts)], axis=1)
+            wide = mixed.shape[1]
+            out_mix_ref[:, pl.ds(pl.multiple_of((step * together + k) * wide, lanes), wide)] = mixed
+            total = total + dot_nn(mixed, wo_ref[k])
+        sum_ref[...] = total
+
+    @pl.when(step == steps_h - 1)
     def _():
         hat, _ = norm_parts(sum_ref[...])
         normed = (hat * gain_ref[...]).astype(low)
@@ -369,7 +397,7 @@
             normed_ref[...] = turn_ref[0]
             beside(turn_ref, pack_ref)
 
-    @pl.when((step >= d.heads) & (step <= last))
+    @pl.when((step >= steps_h) & (step <= last))
     def _():
         coeff = 0.7978845608028654
         held = held_ref[...]
@@ -391,7 +419,7 @@
         gu = jnp.concatenate(grads, axis=1)
         ffn_ref[...] += dot_nn(act, down_ref[...])
         back_ref[...] += dot_nt(gu, up_ref[...])
-        block = step - d.heads
+        block = step - steps_h
         span = act.shape[1]
         if bits is None:
             pack_ref[:, pl.ds(pl.multiple_of(block * span, span), span)] = gu
@@ -429,18 +457,34 @@
             turned_ref[...] = turn_ref[0]
             beside(turn_ref, out_mix_ref)
 
+    moves = [
+        pltpu.make_async_copy(held, result, copied.at[at])
+        for at, (held, result) in enumerate(((out_mix_ref, mix_hbm), (act_ref, act_hbm), (pack_ref, pack_hbm)))
+    ]
+
+    @pl.when(step == last)
+    def _():
+        for move in moves:
+            move.start()
+
     @pl.when(step > last)
     def _():
-        unmix(branch_ref, att_ref, ogate_ref, wo_ref, gatt_ref, d=d)
-
-
-def unmix(branch_ref, att_ref, ogate_ref, wo_ref, out_ref, d=None):
+        for k in range(together):
+            unmix(branch_ref, att_ref, ogate_ref, wo_ref, gatt_ref, k, d)
+
+    @pl.when(step == pl.num_programs(0) - 1)
+    def _():
+        for move in moves:
+            move.wait()
+
+
+def unmix(branch_ref, att_ref, ogate_ref, wo_ref, out_ref, k, d):
     size, experts = d.size, d.experts
     tokens = d.seqs * d.seg
-    grad_mixed = dot_nt(branch_ref[...], wo_ref[0])
-    found = [att_ref[p, 0, s] for s in range(d.seqs) for p in range(d.parts)]
+    grad_mixed = dot_nt(branch_ref[...], wo_ref[k])
+    found = [att_ref[p, k, s] for s in range(d.seqs) for p in range(d.parts)]
     att = jnp.concatenate(found, axis=0).astype(full)
-    gate = ogate_ref[0]
+    gate = ogate_ref[k]
     grad = jnp.zeros((tokens, lanes), full)
     product = []
     for e in range(experts):
@@ -454,32 +498,34 @@
     for s in range(d.seqs):
         for p in range(d.parts):
             first = s * d.seg + p * d.share
-            out_ref[p, 0, s] = joined[first : first + d.share]
+            out_ref[p, k, s] = joined[first : first + d.share]
 
 
 def make_deltas(back_ref, grad_ref, vgate_ref, exp_ref, *refs, d=None):
     size, experts = d.size, d.experts
-    q_found, kv_found, lo_found = [], [], []
+    q_found, k_found, v_found, lo_found = [], [], [], []
     for s in range(d.seqs):
-        kv = back_ref[0, 0, s, 0 : d.rows, :]
+        kv = back_ref[0, 0, s, 0 : 2 * d.rows]
         if d.parts > 1:
             kv = kv.astype(full)
             for p in range(1, d.parts):
-                kv = kv + back_ref[p, 0, s, 0 : d.rows, :].astype(full)
+                kv = kv + back_ref[p, 0, s, 0 : 2 * d.rows].astype(full)
             kv = kv.astype(low)
-        kv_found.append(kv)
+        k_found.append(kv[: d.rows])
+        v_found.append(kv[d.rows :])
         q_found.append(jnp.zeros((d.mem, lanes), low))
         lo_found.append(jnp.zeros((d.mem, lanes), low))
         for p in range(d.parts):
-            q_found.append(back_ref[p, 0, s, d.rows :, 0:lanes])
-            q_found.append(back_ref[p, 0, s, d.rows :, lanes:])
+            q_found.append(payload_queries(back_ref[p, 0, s], d))
             lo_found.append(grad_ref[p, 0, s])
     query = jnp.concatenate(q_found, axis=0)
-    kv = jnp.concatenate(kv_found, axis=0)
+    keys = jnp.concatenate(k_found, axis=0)
+    values = jnp.concatenate(v_found, axis=0)
     out_logit = jnp.concatenate(lo_found, axis=0)[:, size : size + experts]
     gate = vgate_ref[0]
     lane_at = lax.broadcasted_iota(jnp.int32, (d.seqs * d.rows, lanes), 1)
-    value = jnp.where(lane_at < size, kv[:, lanes:].astype(full), 0.0)
+    value = jnp.where(lane_at < size, values.astype(full), 0.0)
+    keys = jnp.where(lane_at < size, keys, jnp.zeros_like(keys))
     product = jnp.concatenate(
         [value * exp_ref[0, :, e * lanes : (e + 1) * lanes].astype(full) for e in range(experts)], axis=1
     )
@@ -493,7 +539,7 @@
         @pl.when(step // (d.heads // 2) == at)
         def _():
             delta_ref[:, 0:lanes] = first
-            delta_ref[:, lanes : 2 * lanes] = kv[:, :lanes]
+            delta_ref[:, lanes : 2 * lanes] = keys
             for e in range(experts):
                 delta_ref[:, (2 + e) * lanes : (3 + e) * lanes] = (gate[:, e : e + 1] * value).astype(low)
 
@@ -609,15 +655,8 @@
         outs[at][...] = (keep_ref[half:] + got_ref[half:].astype(full)).astype(low)
 
 
-def heads_join(keep_a_ref, keep_b_ref, keep_o_ref, got_a_ref, got_b_ref, got_o_ref, *refs):
-    send_ref, left_ref = refs[-2:]
-    half = send_ref.shape[0]
-    first = 0
-    for keep_ref, got_ref in ((keep_a_ref, got_a_ref), (keep_b_ref, got_b_ref), (keep_o_ref, got_o_ref)):
-        here = slice(first, first + keep_ref.shape[1])
-        left_ref[:, here] = keep_ref[:half] + got_ref[:half].astype(full)
-        send_ref[:, here] = (keep_ref[half:] + got_ref[half:].astype(full)).astype(low)
-        first += keep_ref.shape[1]
+def heads_last(*refs):
+    heads_third(*refs)
 
 
 def fold(keep_ref, got_ref, *refs):
@@ -633,16 +672,25 @@
     return jnp.sum(jnp.where(same, column, 0.0), axis=0, keepdims=True)
 
 
-def assemble(keep_ref, got_ref, wall_ref, gain_ref, *refs, d=None):
-    q_ref, k_ref, v_ref, r_ref, out_ref, norm_ref = refs[-6:]
+def assemble_out(kept_ref, got_ref, *refs, d=None):
+    total = kept_ref[...] + got_ref[...].astype(full)
+    refs[-1][...] = jnp.concatenate(
+        [total[:, at * lanes : at * lanes + d.size] for at in range(d.heads * d.experts)], axis=1
+    )
+
+
+def assemble(a_ref, got_a_ref, b_ref, got_b_ref, wall_ref, gain_ref, *refs, d=None):
+    q_ref, k_ref, v_ref, r_ref, norm_ref = refs[-5:]
     size, experts = d.size, d.experts
     slots = 2 + experts
 
-    def total(first):
+    def total(kept, got, first):
         here = slice(first * lanes, (first + 1) * lanes)
-        return keep_ref[:, here] + got_ref[:, here].astype(full)
-
-    every = [[total(h * slots + at) for at in range(slots)] for h in range(d.heads)]
+        return kept[:, here] + got[:, here].astype(full)
+
+    half = d.heads // 2
+    every = [[total(a_ref, got_a_ref, h * slots + at) for at in range(slots)] for h in range(half)]
+    every += [[total(b_ref, got_b_ref, h * slots + at) for at in range(slots)] for h in range(half)]
     along = jnp.zeros(every[0][0].shape, full)
     for h in range(d.heads):
         for at in range(slots):
@@ -654,7 +702,6 @@
     values = [one[0][:, size : size + experts] for one in every]
     outs = [one[0][:, size + experts : size + 2 * experts] for one in every]
     r_ref[...] = jnp.concatenate(values + outs, axis=1)
-    out_ref[...] = jnp.concatenate([total(d.heads * slots + at)[:, :size] for at in range(d.heads * experts)], axis=1)
 
 
 class Halver:
@@ -721,7 +768,7 @@
     parts = cycle // (seqs * heads)
     share = seg // parts
     d = Dims(seqs, seg, mem, rows, heads, size, experts, parts, share, cycle, width, 2)
-    pay_rows = rows + share // 2
+    pay_rows = payload_rows(d)
     at = lax.axis_index("seq")
     my_seq = at % seqs
     my_head = at // seqs % heads
@@ -734,9 +781,6 @@
     live = (place[None, :] < valid_len[:, None]).astype(full).reshape(tokens, 1)
     grad_ffn = (cotangent.reshape(tokens, width).astype(full) * live).astype(low)
     wq, wk, wv, wr = query_weight.T, key_weight.T, value_weight.T, router_weight.T
-    wr = jnp.concatenate(
-        [wr[: heads * experts].reshape(heads, experts, width), wr[heads * experts :].reshape(heads, experts, width)], axis=1
-    )
     v_routes = jnp.transpose(value_routes, (0, 2, 3, 1))
     m_routes = jnp.transpose(memory_routes, (0, 2, 3, 1))
     o_routes = jnp.transpose(output_routes, (0, 2, 3, 1))
@@ -771,10 +815,10 @@
             (wq, by_step((size, width), 0)),
             (wk, by_step((size, width), 0)),
             (wv, by_step((span, width), 0)),
-            (wr, by_step((1, 2 * experts, width), 0)),
+            given(wr),
         ],
         [
-            ((parts, heads, seqs, pay_rows, 2 * lanes), low, head_spec(pay_rows, 2 * lanes)),
+            ((parts, heads, seqs, pay_rows, lanes), low, head_spec(pay_rows, lanes)),
             made((seqs, rows, width), low),
             ((heads, seqs * rows, experts), full, by_step((1, seqs * rows, experts), 0)),
             ((heads, tokens, experts), full, by_step((1, tokens, experts), 0)),
@@ -790,7 +834,7 @@
             (wq, by_step((size, width), 0)),
             (wk, by_step((size, width), 0)),
             (wv, by_step((span, width), 0)),
-            (wr, by_step((1, 2 * experts, width), 0)),
+            given(wr),
             (output_weight, by_step((span, width), 0)),
         ],
         [
@@ -824,7 +868,7 @@
         grad_ffn_both = jnp.concatenate([grad_ffn_t, halver.swap(grad_ffn_t, core[0])], axis=1)
         ctx_a_got, ctx_b_got = halver.swap(ctx_a[1], core[0]), halver.swap(ctx_b[1], core[0])
         after += [grad_ffn_both, ctx_a_got, ctx_b_got]
-    pay = lax.all_to_all(pay.reshape(cycle, pay_rows, 2 * lanes), "seq", 0, 0)
+    pay = lax.all_to_all(pay.reshape(cycle, pay_rows, lanes), "seq", 0, 0)
     att, kept, lse = call(
         functools.partial(attend, d=d),
         1,
@@ -838,17 +882,18 @@
         vmem=vmem_attend,
     )
     att = lax.all_to_all(att, "seq", 0, 0)
-    steps = 4
+    steps, together = 4, 2
+    steps_h = heads // together
     att_heads = att.reshape(parts, heads, seqs, share, lanes)
 
     def ff_block(i):
-        return jnp.clip(i - heads, 0, steps - 1)
+        return jnp.clip(i - steps_h, 0, steps - 1)
 
     def head_of(i):
-        return jnp.where(i < heads + steps, jnp.minimum(i, heads - 1), i - heads - steps)
+        return jnp.where(i < steps_h + steps, jnp.minimum(i, steps_h - 1), i - steps_h - steps)
 
     def back_of(i):
-        return jnp.maximum(i - heads - steps, 0)
+        return jnp.maximum(i - steps_h - steps, 0)
 
     turned_shape = (width // 2, tokens) if fast else (tokens, width)
     act_shape = (tokens, ff // 2) if fast else (tokens, ff)
@@ -856,23 +901,23 @@
     mix_shape = (tokens, heads * wide + 2 * tokens) if fast else (tokens, heads * wide)
     mixed, act, pack, output, grad_residual, grad_branch, normed, turned, grad_out = call(
         functools.partial(feed, d=d, bits=(tuple(down_bits), tuple(up_bits), tuple(out_bits)) if fast else None),
-        2 * heads + steps,
+        2 * steps_h + steps,
         [
             (scal, smem),
-            (att_heads, pl.BlockSpec((parts, 1, seqs, share, lanes), lambda i: (0, head_of(i), 0, 0, 0))),
-            (ogate, pl.BlockSpec((1, tokens, experts), lambda i: (head_of(i), 0, 0))),
+            (att_heads, pl.BlockSpec((parts, together, seqs, share, lanes), lambda i: (0, head_of(i), 0, 0, 0))),
+            (ogate, pl.BlockSpec((together, tokens, experts), lambda i: (head_of(i), 0, 0))),
             given(inputs),
             given(gain_two),
             given(live),
             given(grad_ffn),
-            (wo, pl.BlockSpec((1, wide, width), lambda i: (head_of(i), 0, 0))),
+            (wo, pl.BlockSpec((together, wide, width), lambda i: (head_of(i), 0, 0))),
             (up_weight, pl.BlockSpec((width, ff // steps), lambda i: (0, ff_block(i)))),
             (down_weight, pl.BlockSpec((ff // steps, width), lambda i: (ff_block(i), 0))),
         ],
         [
-            made(mix_shape, low),
-            made(act_shape, low),
-            made(pack_shape, low),
+            (mix_shape, low, unread),
+            (act_shape, low, unread),
+            (pack_shape, low, unread),
             made((tokens, width), low),
             made((tokens, width), full),
             made((tokens, width), low),
@@ -881,15 +926,17 @@
             (
                 (parts, heads, seqs, share, lanes),
                 low,
-                pl.BlockSpec((parts, 1, seqs, share, lanes), lambda i: (0, back_of(i), 0, 0, 0)),
+                pl.BlockSpec((parts, together, seqs, share, lanes), lambda i: (0, back_of(i), 0, 0, 0)),
             ),
         ],
         scratch=[pltpu.VMEM((tokens, width), full)] * 3
-        + [pltpu.VMEM((tokens, width), low), pltpu.VMEM((2, width // 2, tokens), low)],
+        + [pltpu.VMEM((tokens, width), low), pltpu.VMEM((2, width // 2, tokens), low)]
+        + [pltpu.VMEM(shape, low) for shape in (mix_shape, act_shape, pack_shape)]
+        + [pltpu.SemaphoreType.DMA((3,))],
     )
     output = output.reshape(seqs, seg, width)
 
-    pay_shape = (cycle, pay_rows, 2 * lanes)
+    pay_shape = (cycle, pay_rows, lanes)
 
     def attended_back(grad_att, *after):
         (back,) = call(
@@ -912,7 +959,7 @@
             functools.partial(make_deltas, d=d),
             heads,
             [
-                (returned.reshape(parts, heads, seqs, pay_rows, 2 * lanes), head_spec(pay_rows, 2 * lanes)),
+                (returned.reshape(parts, heads, seqs, pay_rows, lanes), head_spec(pay_rows, lanes)),
                 (grad_out, head_spec(share, lanes)),
                 (vgate, by_step((1, seqs * rows, experts), 0)),
                 (expanded, by_step((1, seqs * rows, wide), 0)),
@@ -1031,17 +1078,8 @@
         got_o = halver.swap(send_o, out_bits[1])
         deltas = head_deltas(returned, grad_out, send_o)
         deltas_a, deltas_b = halver.swap(deltas[0], core[0]), halver.swap(deltas[1], core[0])
-        send_o, keep_o = stage(
-            outer_split,
-            split,
-            out_products(0) + [(got_o, by_step((width // 4, heads * wide // split), 1))],
-            [deltas[0]],
-            [out_made(width // 8, low), out_made(width // 8, full)],
-            vmem_big,
-        )
-        got_o = halver.swap(send_o, out_bits[2])
         send_a, send_b = stage(
-            heads_send, heads // 2, head_products(1), [send_o], [head_made(width // 4, low)] * 2,
+            heads_send, heads // 2, head_products(1), [deltas[0]], [head_made(width // 4, low)] * 2,
             vmem_big,
         )
         got_a, got_b = halver.swap(send_a, qkv_bits[0][1]), halver.swap(send_b, qkv_bits[1][1])
@@ -1063,7 +1101,16 @@
             vmem_big,
         )
         got_d = halver.swap(send_d, down_bits[2])
-        input_grad = finished(deltas, send_d)
+        send_o, keep_o = stage(
+            outer_split,
+            split,
+            out_products(0) + [(got_o, by_step((width // 4, heads * wide // split), 1))],
+            [send_d],
+            [out_made(width // 8, low), out_made(width // 8, full)],
+            vmem_big,
+        )
+        got_o = halver.swap(send_o, out_bits[2])
+        input_grad = finished(deltas, send_o)
         send_a, send_b, keep_a, keep_b = stage(
             heads_split,
             heads // 2,
@@ -1089,36 +1136,46 @@
             [made(a_shape, low)] * 2 + [made(a_shape, full)] * 2,
         )
         got_a, got_b = halver.swap(send_a, qkv_bits[0][3]), halver.swap(send_b, qkv_bits[1][3])
-        send_u, keep_u = step_fold(fold, keep_u, got_u, 0, send_a)
+        send_d, keep_d = step_fold(fold_lanes, keep_d, got_d, 1, send_a)
+        got_d = halver.swap(send_d, down_bits[4])
+        send_u, keep_u = step_fold(fold, keep_u, got_u, 0, send_d)
         got_u = halver.swap(send_u, up_bits[4])
-        send_d, keep_d = step_fold(fold_lanes, keep_d, got_d, 1, send_u)
-        got_d = halver.swap(send_d, down_bits[4])
-        h_shape = (own, 2 * span_d + heads * wide)
-        send_h, keep_h = stage(
-            heads_join,
+        send_o, keep_o = step_fold(fold, keep_o, got_o, 0, send_u)
+        got_o = halver.swap(send_o, out_bits[4])
+        a_shape = (own, span_d)
+        send_a, send_b, keep_a, keep_b = stage(
+            heads_last,
             1,
-            [given(a) for a in (keep_a, keep_b, keep_o, got_a, got_b, got_o)],
-            [send_d],
-            [made(h_shape, low), made(h_shape, full)],
-        )
-        got_h = halver.swap(send_h, chip_z[1])
+            [given(a) for a in (keep_a, keep_b, got_a, got_b)],
+            [send_o],
+            [made(a_shape, low)] * 2 + [made(a_shape, full)] * 2,
+        )
+        got_a, got_b = halver.swap(send_a, qkv_bits[0][4]), halver.swap(send_b, qkv_bits[1][4])
         down_grad, up_grad, norm2_grad = stage(
             end_feed,
             1,
             [given(a) for a in (keep_d, got_d, keep_u, got_u, up_own, gain_rows[:, 1:2])],
-            [send_h],
+            [send_a],
             [made((lanes, width), full), made((own, ff), full), made((1, own), full)],
         )
         norm2_grad = norm2_grad.reshape(own)
-        flat = [heads * size, heads * size, heads * span, 2 * heads * experts, heads * span]
-        query_grad, key_grad, value_grad, router_grad, outproj_grad, norm1_grad = call(
+        flat = [heads * size, heads * size, heads * span, 2 * heads * experts]
+        query_grad, key_grad, value_grad, router_grad, norm1_grad = call(
             functools.partial(assemble, d=d),
             1,
-            [given(a) for a in (keep_h, got_h, wall_own, gain_rows[:, 0:1])] + then(up_grad),
+            [given(a) for a in (keep_a, got_a, keep_b, got_b, wall_own, gain_rows[:, 0:1])] + then(up_grad),
             [made((own, cols), full) for cols in flat] + [made((1, own), full)],
             vmem=vmem_less,
+            flops=cost.get("assemble", 1),
         )
         norm1_grad = norm1_grad.reshape(own)
+        (outproj_grad,) = call(
+            functools.partial(assemble_out, d=d),
+            1,
+            [given(keep_o), given(got_o)] + then(router_grad),
+            [made((own, heads * span), full)],
+            vmem=vmem_less,
+        )
         outproj_grad = outproj_grad.T
     else:
         act = act.reshape(tokens, blocks, -1)

time: 276 us -> 269 us (0.975)
  starting transfers between devices: 39.1 us -> 50.1 us
  waiting for transfers between devices: 86.3 us -> 76.8 us
  Pallas kernels: 122 us -> 117 us
  local copies, waits for them, and re-layouts: 21.7 us -> 18.9 us
    ppermute x25 -> x27, starting transfers between devices: 20.1 us -> 29.3 us  [swap(): return lax.ppermute(value, axis, [(i, i ^ mask) for i in range(size)])]
    ppermute x25 -> x27, waiting for transfers between devices: 60.4 us -> 54.7 us  [swap(): return lax.ppermute(value, axis, [(i, i ^ mask) for i in range(size)])]
    pallas_call x25 -> x27, Pallas kernels: 122 us -> 117 us  [call(): pl.pallas_call(kernel, grid=(steps,), out_shape=[jax.ShapeDtypeStruct(sha...]
    all_to_all x1, waiting for transfers between devices: 4.14 us -> 1.29 us  [local(): pay = lax.all_to_all(pay.reshape(cycle, pay_rows, lanes), 'seq', 0, 0)]
    unnamed x68 -> x56, local copies, waits for them, and re-layouts: 15 us -> 13.1 us
  transfers between devices with their start and end apart: 29 -> 31, of which waited for: 14 -> 17; matrix products, arithmetic and copies ran while one was open for 4% -> 4% of each run, Pallas kernels for 27% -> 26%
where the time goes in v1:
time: 269 us; the launch traced here: 267 us
  Pallas kernels  117 us (43%)
  waiting for transfers between devices  76.8 us (29%)
  starting transfers between devices  50.1 us (19%)
  local copies, waits for them, and re-layouts  18.9 us (7%)
  other arithmetic  3.81 us (1%)
    pallas_call x27, Pallas kernels, call(): pl.pallas_call(kernel, grid=(steps,), out_shape=[jax.ShapeDtypeStruct(sha...  117 us
    ppermute x27, waiting for transfers between devices, swap(): return lax.ppermute(value, axis, [(i, i ^ mask) for i in range(size)])  54.7 us
    ppermute x27, starting transfers between devices, swap(): return lax.ppermute(value, axis, [(i, i ^ mask) for i in range(size)])  29.3 us
    unnamed x56, local copies, waits for them, and re-layouts  13.1 us
    all_to_all x1, waiting for transfers between devices, local(): returned = lax.all_to_all(back, 'seq', 0, 0)  11.4 us
    all_to_all x1, waiting for transfers between devices, local(): att = lax.all_to_all(att, 'seq', 0, 0)  7.62 us
    all_to_all x1, starting transfers between devices, local(): pay = lax.all_to_all(pay.reshape(cycle, pay_rows, lanes), 'seq', 0, 0)  7.41 us
    all_to_all x1, starting transfers between devices, local(): att = lax.all_to_all(att, 'seq', 0, 0)  5.54 us
  transfers between devices with their start and end apart: 31, of which 17 were waited for; matrix products, arithmetic and copies ran while one was open for 4% of the time, Pallas kernels for 26%

profile of v1, /device:TPU:0, one launch (start us, length us, event | category | flops | bytes accessed | tf_op | source)
XLA Modules:
  0.0 267.4 jit_solution(9645726259417300469)
XLA Ops:
  0.6 8.8 %shard_map.239 = (bf16[1,4,2,448,128]{4,3,2,1,0:T(8,128)(2,1)}, bf16[2,192,1024]{2,1,0:T(8,128)(2,1)}, f32[4,384,5]{2,1,0:T(8,128)}, f32[4,256,5]{2,1,0:T(8,128)}) custom-call(bf16[2,128,1024]{2,1,0:T(8,128)(2,1)} %x_ref.5, bf16[2,64,1024]{2,1,0:T(8,128)(2,1)} %m_ref.1, s32[2,4,2,128]{3,2,1,0:T(2,128)} %bitcast.52, s32[2,4,2,64]{3,2,1,0:T(2,128)} %bitcast.53, ...), custom_call_target="tpu_custom_call" | custom-call | flops 1 | bytes 1 | tf_op jit(solution)/shard_map/pallas_call | solution.py:74
  9.4 7.4 %all-to-all-start = ((bf16[8,448,128]{2,1,0:T(8,128)(2,1)}), bf16[8,448,128]{2,1,0:T(8,128)(2,1)S(1)}, u32[]{:S(2)}, u32[]{:S(2)}) async-start(bf16[8,448,128]{2,1,0:T(8,128)(2,1)} %bitcast.43), calls=%async_computation | async-start | bytes 1835008 | tf_op jit(solution)/shard_map/all_to_all | solution.py:871
  19.6 11.3 %shard_map.240 = (bf16[4,896,1024]{2,1,0:T(8,128)(2,1)}, bf16[4,384,640]{2,1,0:T(8,128)(2,1)}, bf16[4,640,1024]{2,1,0:T(8,128)(2,1)}, bf16[4,32,896]{2,1,0:T(8,128)(2,1)}) custom-call(s32[4]{0:T(128)} %pad_add_fusion.scal_ref, bf16[2,192,1024]{2,1,0:T(8,128)(2,1)} %get-tuple-element.75.ctx_ref, bf16[448,1024]{1,0:T(8,128)(2,1)} %bitcast.37, ...), custom_call_target="tpu_custom_call" | custom-call | flops 1 | bytes 1 | tf_op jit(solution)/shard_map/pallas_call | solution.py:74
  40.8 4.8 %shard_map.242 = (bf16[8,128,128]{2,1,0:T(8,128)(2,1)}, f32[1024,128]{1,0:T(8,128)}, f32[1024,1]{1,0:T(8,128)}) custom-call(s32[4]{0:T(128)} %pad_add_fusion.scal_ref, bf16[8,448,128]{2,1,0:T(8,128)(2,1)} %copy-done.12, bf16[4,640,1024]{2,1,0:T(8,128)(2,1)} %get-tuple-element.76.refs_0_.wo_ref, bf16[1024,512]{1,0:T(8,128)(2,1)} %pad_maximum_fusion.refs_1_.gf_ref, ...), custom_call_target="tpu_custom_call" | custom-call | flops 1 | bytes 1 | tf_op jit(solution)/shard_map/pallas_call | solution.py:74
  45.6 5.5 %all-to-all-start.1 = ((bf16[8,128,128]{2,1,0:T(8,128)(2,1)}), bf16[8,128,128]{2,1,0:T(8,128)(2,1)S(1)}, u32[]{:S(2)}, u32[]{:S(2)}) async-start(bf16[8,128,128]{2,1,0:T(8,128)(2,1)} %get-tuple-element.79), calls=%async_computation.1 | async-start | bytes 524288 | tf_op jit(solution)/shard_map/all_to_all | solution.py:884
  53.1 7.6 %all-to-all-done.1 = bf16[8,128,128]{2,1,0:T(8,128)(2,1)S(1)} async-done(((bf16[8,128,128]{2,1,0:T(8,128)(2,1)}), bf16[8,128,128]{2,1,0:T(8,128)(2,1)S(1)}, u32[]{:S(2)}, u32[]{:S(2)}) %all-to-all-start.1) | async-done | bytes 262176 | tf_op jit(solution)/shard_map/all_to_all | solution.py:884
  61.4 26.1 %shard_map.243 = (bf16[256,3072]{1,0:T(8,128)(2,1)}, bf16[256,2048]{1,0:T(8,128)(2,1)}, bf16[256,6656]{1,0:T(8,128)(2,1)}, bf16[256,1024]{1,0:T(8,128)(2,1)}, f3...) custom-call(s32[4]{0:T(128)} %pad_add_fusion.scal_ref, ...), custom_call_target="tpu_custom_call" | custom-call | flops 1 | bytes 1 | tf_op jit(solution)/shard_map/pallas_call | solution.py:74
  87.6 4.1 %all-to-all-start.2 = ((bf16[8,128,128]{2,1,0:T(8,128)(2,1)}), bf16[8,128,128]{2,1,0:T(8,128)(2,1)}, u32[]{:S(2)}, u32[]{:S(2)}) async-start(bf16[8,128,128]{2,1,0:T(8,128)(2,1)} %bitcast.41), calls=%async_computation.2 | async-start | bytes 524288 | tf_op jit(solution)/shard_map/all_to_all | solution.py:1070
  95.6 4.1 %shard_map.244.refs_0_ = bf16[256,4096]{1,0:T(8,128)(2,1)} custom-call(bf16[512,256]{1,0:T(8,128)(2,1)} %get-tuple-element.85.left_ref, bf16[256,6656]{1,0:T(8,128)(2,1)} %copy-done.9, bf16[256,6656]{1,0:T(8,128)(2,1)} %get-tuple-element.86.gu_ref, bf16[256,6656]{1,0:T(8,128)(2,1)} %copy-done.9, bf16[1,4,2,128,128]{4,3,2,1,0:T(8,128)(2,1)} %get-tuple-element.84.refs_0_.grad_ref), custom_call_target="tpu_custom_call" | custom-call | flops 1 | bytes 1 | tf_op jit(solution)/shard_map/pallas_call | solution.py:74
  101.5 6.3 %shard_map.245.refs_0_ = bf16[8,448,128]{2,1,0:T(8,128)(2,1)} custom-call(s32[4]{0:T(128)} %pad_add_fusion.scal_ref, bf16[8,448,128]{2,1,0:T(8,128)(2,1)} %copy-done.12, f32[1024,128]{1,0:T(8,128)} %get-tuple-element.82.keep_ref, f32[1024,1]{1,0:T(8,128)} %get-tuple-element.83.lse_ref, bf16[8,128,128]{2,1,0:T(8,128)(2,1)} %all-to-all-done.2.grad_ref, ...), custom_call_target="tpu_custom_call" | custom-call | flops 1 | bytes 1 | tf_op jit(solution)/shard_map/pallas_call | solution.py:74
  107.9 3.8 %all-to-all-start.3 = ((bf16[8,448,128]{2,1,0:T(8,128)(2,1)}), bf16[8,448,128]{2,1,0:T(8,128)(2,1)S(1)}, u32[]{:S(2)}, u32[]{:S(2)}) async-start(bf16[8,448,128]{2,1,0:T(8,128)(2,1)} %shard_map.245.refs_0_), calls=%async_computation.3 | async-start | bytes 1835008 | tf_op jit(solution)/shard_map/all_to_all | solution.py:1074
  113.3 3.8 %shard_map.246.refs_0_ = bf16[1024,1024]{1,0:T(8,128)(2,1)} custom-call(bf16[1024,512]{1,0:T(8,128)(2,1)} %pad_maximum_fusion.refs_1_.gf_ref, bf16[256,2048]{1,0:T(8,128)(2,1)} %get-tuple-element.91.act_ref, bf16[256,6656]{1,0:T(8,128)(2,1)} %copy-done.9, bf16[8,448,128]{2,1,0:T(8,128)(2,1)} %shard_map.245.refs_0_), custom_call_target="tpu_custom_call" | custom-call | flops 1 | bytes 1 | tf_op jit(solution)/shard_map/pallas_call | solution.py:74
  123.3 11.4 %all-to-all-done.3 = bf16[8,448,128]{2,1,0:T(8,128)(2,1)S(1)} async-done(((bf16[8,448,128]{2,1,0:T(8,128)(2,1)}), bf16[8,448,128]{2,1,0:T(8,128)(2,1)S(1)}, u32[]{:S(2)}, u32[]{:S(2)}) %all-to-all-start.3) | async-done | bytes 917536 | tf_op jit(solution)/shard_map/all_to_all | solution.py:1074
  135.7 6.7 %shard_map.248 = (bf16[384,1792]{1,0:T(8,128)(2,1)}, bf16[384,1792]{1,0:T(8,128)(2,1)}) custom-call(bf16[1,4,2,448,128]{4,3,2,1,0:T(8,128)(2,1)} %bitcast.40, bf16[1,4,2,128,128]{4,3,2,1,0:T(8,128)(2,1)} %get-tuple-element.84.refs_0_.grad_ref, f32[4,384,5]{2,1,0:T(8,128)} %get-tuple-element.87.vgate_ref, bf16[4,384,640]{2,1,0:T(8,128)(2,1)} %get-tuple-element.88.exp_ref, ...), custom_call_target="tpu_custom_call" | custom-call | flops 1 | bytes 1 | tf_op jit(solution)/shard_map/pallas_call | solution.py:74
  148.7 5.0 %shard_map.249 = (bf16[256,1792]{1,0:T(8,128)(2,1)}, bf16[256,1792]{1,0:T(8,128)(2,1)}) custom-call(bf16[2,512,384]{2,1,0:T(8,128)(2,1)} %get-tuple-element.77.a_ref, bf16[512,384]{1,0:T(8,128)(2,1)} %copy-done.15, bf16[2,512,384]{2,1,0:T(8,128)(2,1)} %get-tuple-element.78.b_ref, bf16[512,384]{1,0:T(8,128)(2,1)} %copy-done.16, ...), custom_call_target="tpu_custom_call" | custom-call | flops 1 | bytes 1 | tf_op jit(solution)/shard_map/pallas_call | solution.py:74
  156.6 3.7 %collective-permute-done.7.new_ref = bf16[256,4096]{1,0:T(8,128)(2,1)} collective-permute-done((bf16[256,4096]{1,0:T(8,128)(2,1)S(1)}, bf16[256,4096]{1,0:T(8,128)(2,1)}, u32[]{:S(2)}, u32[]{:S(2)}) %collective-permute-start.7) | collective-permute-done | bytes 2097184 | tf_op jit(solution)/shard_map/ppermute | solution.py:720
  160.4 4.8 %shard_map.250 = (bf16[128,4096]{1,0:T(8,128)(2,1)}, f32[128,4096]{1,0:T(8,128)}) custom-call(bf16[512,256]{1,0:T(8,128)(2,1)} %get-tuple-element.85.left_ref, bf16[256,6656]{1,0:T(8,128)(2,1)} %copy-done.9, bf16[256,6656]{1,0:T(8,128)(2,1)} %get-tuple-element.86.gu_ref, bf16[256,6656]{1,0:T(8,128)(2,1)} %copy-done.9, ...), custom_call_target="tpu_custom_call" | custom-call | flops 1 | bytes 1 | tf_op jit(solution)/shard_map/pallas_call | solution.py:74
  170.0 4.0 %shard_map.251 = (bf16[1024,512]{1,0:T(8,128)(2,1)}, f32[1024,512]{1,0:T(8,128)}) custom-call(bf16[1024,512]{1,0:T(8,128)(2,1)} %pad_maximum_fusion.refs_1_.gf_ref, bf16[256,2048]{1,0:T(8,128)(2,1)} %get-tuple-element.91.act_ref, bf16[256,6656]{1,0:T(8,128)(2,1)} %copy-done.9, bf16[1024,1024]{1,0:T(8,128)(2,1)} %collective-permute-done.6.new_ref, ...), custom_call_target="tpu_custom_call" | custom-call | flops 2000000000 | bytes 1 | tf_op jit(solution)/shard_map/pallas_call | solution.py:74
  176.4 3.6 %shard_map.252 = (bf16[128,2560]{1,0:T(8,128)(2,1)}, f32[128,2560]{1,0:T(8,128)}) custom-call(bf16[512,256]{1,0:T(8,128)(2,1)} %get-tuple-element.89.left_ref, bf16[256,3072]{1,0:T(8,128)(2,1)} %copy-done.10, bf16[256,3072]{1,0:T(8,128)(2,1)} %get-tuple-element.90.right_ref, bf16[256,3072]{1,0:T(8,128)(2,1)} %copy-done.10, bf16[256,2560]{1,0:T(8,128)(2,1)} %copy-done.19, ...), custom_call_target="tpu_custom_call" | custom-call | flops 1 | bytes 1 | tf_op jit(solution)/shard_map/pallas_call | solution.py:74
  180.6 8.1 %shard_map.253.refs_0_ = f32[2,128,1024]{2,1,0:T(8,128)} custom-call(bf16[384,1792]{1,0:T(8,128)(2,1)} %get-tuple-element.92.da_ref.refs_0_.first_ref, bf16[384,1792]{1,0:T(8,128)(2,1)} %get-tuple-element.93.db_ref.second_ref, bf16[2,128,1024]{2,1,0:T(8,128)(2,1)} %x_ref.5, f32[1,1024]{1,0:T(1,128)} %bitcast.48, f32[256,1024]{1,0:T(8,128)} %get-tuple-element.94.resid_ref, ...), custom_call_target="tpu_custom_call" | custom-call | flops 1 | bytes 1 | tf_op jit(solution)/shard_map/pallas_call | solution.py:74
  191.5 5.7 %shard_map.254 = (bf16[128,1792]{1,0:T(8,128)(2,1)}, bf16[128,1792]{1,0:T(8,128)(2,1)}, f32[128,1792]{1,0:T(8,128)}, f32[128,1792]{1,0:T(8,128)}) custom-call(bf16[2,512,384]{2,1,0:T(8,128)(2,1)} %get-tuple-element.77.a_ref, bf16[512,384]{1,0:T(8,128)(2,1)} %copy-done.15, bf16[2,512,384]{2,1,0:T(8,128)(2,1)} %get-tuple-element.78.b_ref, ...), custom_call_target="tpu_custom_call" | custom-call | flops 4000000000 | bytes 1 | tf_op jit(solution)/shard_map/pallas_call | solution.py:74
  212.3 8.1 %collective-permute-done.13.got_b_ref = bf16[128,1792]{1,0:T(8,128)(2,1)} collective-permute-done((bf16[128,1792]{1,0:T(8,128)(2,1)}, bf16[128,1792]{1,0:T(8,128)(2,1)}, u32[]{:S(2)}, u32[]{:S(2)}) %collective-permute-start.13) | collective-permute-done | bytes 458784 | tf_op jit(solution)/shard_map/ppermute | solution.py:720
  223.6 11.1 %collective-permute-done.21.got_ref = bf16[1024,256]{1,0:T(8,128)(2,1)S(1)} collective-permute-done((bf16[1024,256]{1,0:T(8,128)(2,1)S(1)}, bf16[1024,256]{1,0:T(8,128)(2,1)S(1)}, u32[]{:S(2)}, u32[]{:S(2)}) %collective-permute-start.21) | collective-permute-done | bytes 524320 | tf_op jit(solution)/shard_map/ppermute | solution.py:720
  245.8 13.0 %collective-permute-done.24.got_d_ref = bf16[1024,128]{1,0:T(8,128)(2,1)S(1)} collective-permute-done((bf16[1024,128]{1,0:T(8,128)(2,1)S(1)}, bf16[1024,128]{1,0:T(8,128)(2,1)S(1)}, u32[]{:S(2)}, u32[]{:S(2)}) %collective-permute-start.24) | collective-permute-done | bytes 262176 | tf_op jit(solution)/shard_map/ppermute | solution.py:720
  (137 shorter events, 87.4 us)
Async XLA Ops:
  9.4 30.4 %all-to-all-start = ((bf16[8,448,128]{2,1,0:T(8,128)(2,1)}), bf16[8,448,128]{2,1,0:T(8,128)(2,1)S(1)}, u32[]{:S(2)}, u32[]{:S(2)}) async-start(bf16[8,448,128]{2,1,0:T(8,128)(2,1)} %bitcast.43), calls=%async_computation | async-start | bytes 1835008 | tf_op jit(solution)/shard_map/all_to_all | solution.py:871
  17.7 18.8 %collective-permute-start = (bf16[1024,256]{1,0:T(8,128)(2,1)S(1)}, bf16[1024,256]{1,0:T(8,128)(2,1)}, u32[]{:S(2)}, u32[]{:S(2)}) collective-permute-start(bf16[1024,256]{1,0:T(8,128)(2,1)S(1)} %fusion.3), channel_id=1, source_target_pairs={{0,1},{1,0},{2,3},{3,2},{4,5},{5,4},{6,7},{7,6},{8,9},{9,8},{10,11... | collective-permute-start | bytes 1572872 | tf_op jit(solution)/shard_map/ppermute | solution.py:720
  45.6 15.1 %all-to-all-start.1 = ((bf16[8,128,128]{2,1,0:T(8,128)(2,1)}), bf16[8,128,128]{2,1,0:T(8,128)(2,1)S(1)}, u32[]{:S(2)}, u32[]{:S(2)}) async-start(bf16[8,128,128]{2,1,0:T(8,128)(2,1)} %get-tuple-element.79), calls=%async_computation.1 | async-start | bytes 524288 | tf_op jit(solution)/shard_map/all_to_all | solution.py:884
  107.9 26.8 %all-to-all-start.3 = ((bf16[8,448,128]{2,1,0:T(8,128)(2,1)}), bf16[8,448,128]{2,1,0:T(8,128)(2,1)S(1)}, u32[]{:S(2)}, u32[]{:S(2)}) async-start(bf16[8,448,128]{2,1,0:T(8,128)(2,1)} %shard_map.245.refs_0_), calls=%async_computation.3 | async-start | bytes 1835008 | tf_op jit(solution)/shard_map/all_to_all | solution.py:1074
  111.7 48.6 %collective-permute-start.7 = (bf16[256,4096]{1,0:T(8,128)(2,1)S(1)}, bf16[256,4096]{1,0:T(8,128)(2,1)}, u32[]{:S(2)}, u32[]{:S(2)}) collective-permute-start(bf16[256,4096]{1,0:T(8,128)(2,1)S(1)} %copy-done.11), channel_id=1, source_target_pairs={{0,2},{1,3},{2,0},{3,1},{4,6},{5,7},{6,4},{7,5},{8,10},{9,11},{10,... | collective-permute-start | bytes 6291464 | tf_op jit(solution)/shard_map/ppermute | solution.py:720
  117.1 52.9 %collective-permute-start.6 = (bf16[1024,1024]{1,0:T(8,128)(2,1)}, bf16[1024,1024]{1,0:T(8,128)(2,1)}, u32[]{:S(2)}, u32[]{:S(2)}) collective-permute-start(bf16[1024,1024]{1,0:T(8,128)(2,1)} %shard_map.246.refs_0_), channel_id=1, source_target_pairs={{0,4},{4,0},{8,12},{12,8},{16,20},{20,16},{24,28},{28,24},{1,5},{5... | collective-permute-start | bytes 6291464 | tf_op jit(solution)/shard_map/ppermute | solution.py:720
  142.9 32.4 %collective-permute-start.5 = (bf16[256,2560]{1,0:T(8,128)(2,1)S(1)}, bf16[256,2560]{1,0:T(8,128)(2,1)S(1)}, u32[]{:S(2)}, u32[]{:S(2)}) collective-permute-start(bf16[256,2560]{1,0:T(8,128)(2,1)S(1)} %copy-done.13), channel_id=1, source_target_pairs={{0,8},{4,12},{8,0},{12,4},{16,24},{20,28},{24,16},{28,20},{1,9},{5... | collective-permute-start | bytes 3932168 | tf_op jit(solution)/shard_map/ppermute | solution.py:720
  153.7 35.8 %collective-permute-start.10 = (bf16[256,1792]{1,0:T(8,128)(2,1)}, bf16[256,1792]{1,0:T(8,128)(2,1)S(1)}, u32[]{:S(2)}, u32[]{:S(2)}) collective-permute-start(bf16[256,1792]{1,0:T(8,128)(2,1)} %get-tuple-element.96.refs_0_), channel_id=1, source_target_pairs={{0,4},{4,0},{8,12},{12,8},{16,20},{20,16},{24,28},{28,24},{1,5},{5... | collective-permute-start | bytes 2752520 | tf_op jit(solution)/shard_map/ppermute | solution.py:720
  155.1 34.4 %collective-permute-start.11 = (bf16[256,1792]{1,0:T(8,128)(2,1)}, bf16[256,1792]{1,0:T(8,128)(2,1)S(1)}, u32[]{:S(2)}, u32[]{:S(2)}) collective-permute-start(bf16[256,1792]{1,0:T(8,128)(2,1)} %get-tuple-element.100), channel_id=1, source_target_pairs={{0,2},{1,3},{2,0},{3,1},{4,6},{5,7},{6,4},{7,5},{8,10},{9,11},{10,... | collective-permute-start | bytes 2752520 | tf_op jit(solution)/shard_map/ppermute | solution.py:720
  165.1 35.5 %collective-permute-start.16 = (bf16[128,4096]{1,0:T(8,128)(2,1)}, bf16[128,4096]{1,0:T(8,128)(2,1)S(1)}, u32[]{:S(2)}, u32[]{:S(2)}) collective-permute-start(bf16[128,4096]{1,0:T(8,128)(2,1)} %get-tuple-element.97.refs_0_), channel_id=1, source_target_pairs={{0,8},{4,12},{8,0},{12,4},{16,24},{20,28},{24,16},{28,20},{1,9},{5... | collective-permute-start | bytes 3145736 | tf_op jit(solution)/shard_map/ppermute | solution.py:720
  174.0 31.2 %collective-permute-start.15 = (bf16[1024,512]{1,0:T(8,128)(2,1)}, bf16[1024,512]{1,0:T(8,128)(2,1)}, u32[]{:S(2)}, u32[]{:S(2)}) collective-permute-start(bf16[1024,512]{1,0:T(8,128)(2,1)} %get-tuple-element.98.refs_0_), channel_id=1, source_target_pairs={{0,2},{1,3},{2,0},{3,1},{4,6},{5,7},{6,4},{7,5},{8,10},{9,11},{10,... | collective-permute-start | bytes 3145736 | tf_op jit(solution)/shard_map/ppermute | solution.py:720
  180.0 26.7 %collective-permute-start.14 = (bf16[128,2560]{1,0:T(8,128)(2,1)}, bf16[128,2560]{1,0:T(8,128)(2,1)}, u32[]{:S(2)}, u32[]{:S(2)}) collective-permute-start(bf16[128,2560]{1,0:T(8,128)(2,1)} %get-tuple-element.99.refs_0_), channel_id=1, source_target_pairs={{0,4},{4,0},{8,12},{12,8},{16,20},{20,16},{24,28},{28,24},{1,5},{5... | collective-permute-start | bytes 1966088 | tf_op jit(solution)/shard_map/ppermute | solution.py:720
  197.3 15.1 %collective-permute-start.12 = (bf16[128,1792]{1,0:T(8,128)(2,1)}, bf16[128,1792]{1,0:T(8,128)(2,1)}, u32[]{:S(2)}, u32[]{:S(2)}) collective-permute-start(bf16[128,1792]{1,0:T(8,128)(2,1)} %get-tuple-element.103.refs_0_), channel_id=1, source_target_pairs={{0,2},{1,3},{2,0},{3,1},{4,6},{5,7},{6,4},{7,5},{8,10},{9,11},{10,... | collective-permute-start | bytes 1376264 | tf_op jit(solution)/shard_map/ppermute | solution.py:720
  198.6 21.9 %collective-permute-start.13 = (bf16[128,1792]{1,0:T(8,128)(2,1)}, bf16[128,1792]{1,0:T(8,128)(2,1)}, u32[]{:S(2)}, u32[]{:S(2)}) collective-permute-start(bf16[128,1792]{1,0:T(8,128)(2,1)} %get-tuple-element.104), channel_id=1, source_target_pairs={{0,8},{4,12},{8,0},{12,4},{16,24},{20,28},{24,16},{28,20},{1,9},{5... | collective-permute-start | bytes 1376264 | tf_op jit(solution)/shard_map/ppermute | solution.py:720
  202.0 35.8 %collective-permute-start.20 = (bf16[64,4096]{1,0:T(8,128)(2,1)S(1)}, bf16[64,4096]{1,0:T(8,128)(2,1)S(1)}, u32[]{:S(2)}, u32[]{:S(2)}) collective-permute-start(bf16[64,4096]{1,0:T(8,128)(2,1)S(1)} %get-tuple-element.108.refs_0_), channel_id=1, source_target_pairs={{0,16},{4,20},{8,24},{12,28},{16,0},{20,4},{24,8},{28,12},{1,17},{... | collective-permute-start | bytes 1572872 | tf_op jit(solution)/shard_map/ppermute | solution.py:720
  206.6 28.1 %collective-permute-start.21 = (bf16[1024,256]{1,0:T(8,128)(2,1)S(1)}, bf16[1024,256]{1,0:T(8,128)(2,1)S(1)}, u32[]{:S(2)}, u32[]{:S(2)}) collective-permute-start(bf16[1024,256]{1,0:T(8,128)(2,1)S(1)} %get-tuple-element.109.refs_0_), channel_id=1, source_target_pairs={{0,8},{4,12},{8,0},{12,4},{16,24},{20,28},{24,16},{28,20},{1,9},{5... | collective-permute-start | bytes 1572872 | tf_op jit(solution)/shard_map/ppermute | solution.py:720
  208.0 30.7 %collective-permute-start.19 = (bf16[64,2560]{1,0:T(8,128)(2,1)S(1)}, bf16[64,2560]{1,0:T(8,128)(2,1)S(1)}, u32[]{:S(2)}, u32[]{:S(2)}) collective-permute-start(bf16[64,2560]{1,0:T(8,128)(2,1)S(1)} %get-tuple-element.110.refs_0_), channel_id=1, source_target_pairs={{0,2},{1,3},{2,0},{3,1},{4,6},{5,7},{6,4},{7,5},{8,10},{9,11},{10,... | collective-permute-start | bytes 983048 | tf_op jit(solution)/shard_map/ppermute | solution.py:720
  221.8 21.0 %collective-permute-start.17 = (bf16[64,1792]{1,0:T(8,128)(2,1)S(1)}, bf16[64,1792]{1,0:T(8,128)(2,1)S(1)}, u32[]{:S(2)}, u32[]{:S(2)}) collective-permute-start(bf16[64,1792]{1,0:T(8,128)(2,1)S(1)} %get-tuple-element.113.refs_0_), channel_id=1, source_target_pairs={{0,8},{4,12},{8,0},{12,4},{16,24},{20,28},{24,16},{28,20},{1,9},{5... | collective-permute-start | bytes 688136 | tf_op jit(solution)/shard_map/ppermute | solution.py:720
  221.9 20.9 %collective-permute-start.18 = (bf16[64,1792]{1,0:T(8,128)(2,1)S(1)}, bf16[64,1792]{1,0:T(8,128)(2,1)S(1)}, u32[]{:S(2)}, u32[]{:S(2)}) collective-permute-start(bf16[64,1792]{1,0:T(8,128)(2,1)S(1)} %get-tuple-element.114), channel_id=1, source_target_pairs={{0,4},{4,0},{8,12},{12,8},{16,20},{20,16},{24,28},{28,24},{1,5},{5... | collective-permute-start | bytes 688136 | tf_op jit(solution)/shard_map/ppermute | solution.py:720
  234.8 24.0 %collective-permute-start.24 = (bf16[1024,128]{1,0:T(8,128)(2,1)S(1)}, bf16[1024,128]{1,0:T(8,128)(2,1)S(1)}, u32[]{:S(2)}, u32[]{:S(2)}) collective-permute-start(bf16[1024,128]{1,0:T(8,128)(2,1)S(1)} %get-tuple-element.118.refs_0_), channel_id=1, source_target_pairs={{0,16},{4,20},{8,24},{12,28},{16,0},{20,4},{24,8},{28,12},{1,17},{... | collective-permute-start | bytes 786440 | tf_op jit(solution)/shard_map/ppermute | solution.py:720
  237.9 20.9 %collective-permute-start.25 = (bf16[32,4096]{1,0:T(8,128)(2,1)S(1)}, bf16[32,4096]{1,0:T(8,128)(2,1)S(1)}, u32[]{:S(2)}, u32[]{:S(2)}) collective-permute-start(bf16[32,4096]{1,0:T(8,128)(2,1)S(1)} %get-tuple-element.119.refs_0_), channel_id=1, source_target_pairs={{0,4},{4,0},{8,12},{12,8},{16,20},{20,16},{24,28},{28,24},{1,5},{5... | collective-permute-start | bytes 786440 | tf_op jit(solution)/shard_map/ppermute | solution.py:720
  238.8 27.0 %collective-permute-start.26 = (bf16[32,2560]{1,0:T(8,128)(2,1)S(1)}, bf16[32,2560]{1,0:T(8,128)(2,1)S(1)}, u32[]{:S(2)}, u32[]{:S(2)}) collective-permute-start(bf16[32,2560]{1,0:T(8,128)(2,1)S(1)} %get-tuple-element.120.refs_4_), channel_id=1, source_target_pairs={{0,16},{4,20},{8,24},{12,28},{16,0},{20,4},{24,8},{28,12},{1,17},{... | collective-permute-start | bytes 491528 | tf_op jit(solution)/shard_map/ppermute | solution.py:720
  242.8 19.7 %collective-permute-start.22 = (bf16[32,1792]{1,0:T(8,128)(2,1)S(1)}, bf16[32,1792]{1,0:T(8,128)(2,1)S(1)}, u32[]{:S(2)}, u32[]{:S(2)}) collective-permute-start(bf16[32,1792]{1,0:T(8,128)(2,1)S(1)} %get-tuple-element.122.refs_0_), channel_id=1, source_target_pairs={{0,16},{4,20},{8,24},{12,28},{16,0},{20,4},{24,8},{28,12},{1,17},{... | collective-permute-start | bytes 344072 | tf_op jit(solution)/shard_map/ppermute | solution.py:720
  242.9 20.9 %collective-permute-start.23 = (bf16[32,1792]{1,0:T(8,128)(2,1)S(1)}, bf16[32,1792]{1,0:T(8,128)(2,1)S(1)}, u32[]{:S(2)}, u32[]{:S(2)}) collective-permute-start(bf16[32,1792]{1,0:T(8,128)(2,1)S(1)} %get-tuple-element.124), channel_id=1, source_target_pairs={{0,16},{4,20},{8,24},{12,28},{16,0},{20,4},{24,8},{28,12},{1,17},{... | collective-permute-start | bytes 344072 | tf_op jit(solution)/shard_map/ppermute | solution.py:720
  (34 other events, 162.0 us)

commit v2 on v1

--- a/solution.py
+++ b/solution.py
@@ -18,7 +18,7 @@
 full = jnp.float32
 vmem_bytes = 56 << 20
 vmem_less = 24 << 20
-cost = {'heads_split': 4000000000, 'heads_third': 4000000000, 'heads_last': 4000000000, 'cross_down': 2000000000, 'end_feed': 6000000000, 'assemble': 3000000000}
+cost = {'heads_split': 4000000000, 'heads_third': 4000000000, 'heads_last': 4000000000, 'cross_down': 2000000000, 'end_down': 6000000000, 'end_up': 3000000000, 'assemble': 3000000000}
 vmem_back = 56 << 20
 vmem_finish = 56 << 20
 vmem_big = 56 << 20
@@ -605,9 +605,12 @@
     send_ref[...] = total[:, half:].astype(low)
 
 
-def end_feed(keep_d_ref, got_d_ref, keep_u_ref, got_u_ref, weight_ref, gain_ref, *refs):
-    down_ref, up_ref, norm_ref = refs[-3:]
-    down_ref[...] = (keep_d_ref[...] + got_d_ref[...].astype(full)).T
+def end_down(keep_ref, got_ref, *refs):
+    refs[-1][...] = (keep_ref[...] + got_ref[...].astype(full)).T
+
+
+def end_up(keep_u_ref, got_u_ref, weight_ref, gain_ref, *refs):
+    up_ref, norm_ref = refs[-2:]
     total = keep_u_ref[...] + got_u_ref[...].astype(full)
     up_ref[...] = total
     along = jnp.sum(total * weight_ref[...].astype(full), axis=1, keepdims=True)
@@ -672,15 +675,8 @@
     return jnp.sum(jnp.where(same, column, 0.0), axis=0, keepdims=True)
 
 
-def assemble_out(kept_ref, got_ref, *refs, d=None):
-    total = kept_ref[...] + got_ref[...].astype(full)
-    refs[-1][...] = jnp.concatenate(
-        [total[:, at * lanes : at * lanes + d.size] for at in range(d.heads * d.experts)], axis=1
-    )
-
-
-def assemble(a_ref, got_a_ref, b_ref, got_b_ref, wall_ref, gain_ref, *refs, d=None):
-    q_ref, k_ref, v_ref, r_ref, norm_ref = refs[-5:]
+def assemble(a_ref, got_a_ref, b_ref, got_b_ref, o_ref, got_o_ref, wall_ref, gain_ref, *refs, d=None):
+    q_ref, k_ref, v_ref, r_ref, out_ref, norm_ref = refs[-6:]
     size, experts = d.size, d.experts
     slots = 2 + experts
 
@@ -702,6 +698,9 @@
     values = [one[0][:, size : size + experts] for one in every]
     outs = [one[0][:, size + experts : size + 2 * experts] for one in every]
     r_ref[...] = jnp.concatenate(values + outs, axis=1)
+    out_ref[...] = jnp.concatenate(
+        [total(o_ref, got_o_ref, at)[:, :size] for at in range(d.heads * experts)], axis=1
+    )
 
 
 class Halver:
@@ -850,7 +849,7 @@
     high_b = list(range(halver.low_bits, bit_count))
     core, chip_y, chip_x, chip_z = low_b[:1], low_b[1:], high_b[:1], high_b[1:]
     down_bits = core + chip_x + chip_y + chip_z
-    up_bits = core + chip_y + chip_z + chip_x
+    up_bits = core + chip_y + chip_z[:1] + chip_x + chip_z[1:]
     out_bits = core + chip_z[:1] + chip_x + chip_y + chip_z[1:]
     fast = own == 32 and ff == blocks * lanes and len(chip_z) == 2 and len(chip_y) == 1
 
@@ -1127,55 +1126,49 @@
         got_d = halver.swap(send_d, down_bits[3])
         send_o, keep_o = step_fold(fold, keep_o, got_o, 0, send_d)
         got_o = halver.swap(send_o, out_bits[3])
+        send_u, keep_u = step_fold(fold, keep_u, got_u, 0, send_o)
+        got_u = halver.swap(send_u, up_bits[4])
         a_shape = (width // 16, span_d)
         send_a, send_b, keep_a, keep_b = stage(
             heads_third,
             1,
             [given(a) for a in (keep_a, keep_b, got_a, got_b)],
-            [send_o],
+            [send_u],
             [made(a_shape, low)] * 2 + [made(a_shape, full)] * 2,
         )
         got_a, got_b = halver.swap(send_a, qkv_bits[0][3]), halver.swap(send_b, qkv_bits[1][3])
         send_d, keep_d = step_fold(fold_lanes, keep_d, got_d, 1, send_a)
         got_d = halver.swap(send_d, down_bits[4])
-        send_u, keep_u = step_fold(fold, keep_u, got_u, 0, send_d)
-        got_u = halver.swap(send_u, up_bits[4])
-        send_o, keep_o = step_fold(fold, keep_o, got_o, 0, send_u)
+        send_o, keep_o = step_fold(fold, keep_o, got_o, 0, send_d)
         got_o = halver.swap(send_o, out_bits[4])
+        up_grad, norm2_grad = stage(
+            end_up,
+            1,
+            [given(a) for a in (keep_u, got_u, up_own, gain_rows[:, 1:2])],
+            [send_o],
+            [made((own, ff), full), made((1, own), full)],
+        )
         a_shape = (own, span_d)
         send_a, send_b, keep_a, keep_b = stage(
             heads_last,
             1,
             [given(a) for a in (keep_a, keep_b, got_a, got_b)],
-            [send_o],
+            [up_grad],
             [made(a_shape, low)] * 2 + [made(a_shape, full)] * 2,
         )
         got_a, got_b = halver.swap(send_a, qkv_bits[0][4]), halver.swap(send_b, qkv_bits[1][4])
-        down_grad, up_grad, norm2_grad = stage(
-            end_feed,
-            1,
-            [given(a) for a in (keep_d, got_d, keep_u, got_u, up_own, gain_rows[:, 1:2])],
-            [send_a],
-            [made((lanes, width), full), made((own, ff), full), made((1, own), full)],
-        )
+        (down_grad,) = stage(end_down, 1, [given(keep_d), given(got_d)], [send_a], [made((lanes, width), full)])
         norm2_grad = norm2_grad.reshape(own)
-        flat = [heads * size, heads * size, heads * span, 2 * heads * experts]
-        query_grad, key_grad, value_grad, router_grad, norm1_grad = call(
+        flat = [heads * size, heads * size, heads * span, 2 * heads * experts, heads * span]
+        query_grad, key_grad, value_grad, router_grad, outproj_grad, norm1_grad = call(
             functools.partial(assemble, d=d),
             1,
-            [given(a) for a in (keep_a, got_a, keep_b, got_b, wall_own, gain_rows[:, 0:1])] + then(up_grad),
+            [given(a) for a in (keep_a, got_a, keep_b, got_b, keep_o, got_o, wall_own, gain_rows[:, 0:1])] + then(down_grad),
             [made((own, cols), full) for cols in flat] + [made((1, own), full)],
             vmem=vmem_less,
             flops=cost.get("assemble", 1),
         )
         norm1_grad = norm1_grad.reshape(own)
-        (outproj_grad,) = call(
-            functools.partial(assemble_out, d=d),
-            1,
-            [given(keep_o), given(got_o)] + then(router_grad),
-            [made((own, heads * span), full)],
-            vmem=vmem_less,
-        )
         outproj_grad = outproj_grad.T
     else:
         act = act.reshape(tokens, blocks, -1)

time: 269 us -> 261 us (0.970)
  waiting for transfers between devices: 76.8 us -> 69.8 us
    ppermute x27, waiting for transfers between devices: 54.7 us -> 47.5 us  [swap(): return lax.ppermute(value, axis, [(i, i ^ mask) for i in range(size)])]
  transfers between devices with their start and end apart: 31 -> 31, of which waited for: 17 -> 17; matrix products, arithmetic and copies ran while one was open for 4% -> 4% of each run, Pallas kernels for 26% -> 28%
where the time goes in v2:
time: 261 us; the launch traced here: 260 us
  Pallas kernels  119 us (46%)
  waiting for transfers between devices  69.8 us (27%)
  starting transfers between devices  47.7 us (18%)
  local copies, waits for them, and re-layouts  18.5 us (7%)
  other arithmetic  3.81 us (1%)
    pallas_call x27, Pallas kernels, call(): pl.pallas_call(kernel, grid=(steps,), out_shape=[jax.ShapeDtypeStruct(sha...  119 us
    ppermute x27, waiting for transfers between devices, swap(): return lax.ppermute(value, axis, [(i, i ^ mask) for i in range(size)])  47.5 us
    ppermute x27, starting transfers between devices, swap(): return lax.ppermute(value, axis, [(i, i ^ mask) for i in range(size)])  27.1 us
    unnamed x56, local copies, waits for them, and re-layouts  12 us
    all_to_all x1, waiting for transfers between devices, local(): returned = lax.all_to_all(back, 'seq', 0, 0)  11.4 us
    all_to_all x1, waiting for transfers between devices, local(): att = lax.all_to_all(att, 'seq', 0, 0)  7.61 us
    all_to_all x1, starting transfers between devices, local(): pay = lax.all_to_all(pay.reshape(cycle, pay_rows, lanes), 'seq', 0, 0)  7.41 us
    all_to_all x1, starting transfers between devices, local(): att = lax.all_to_all(att, 'seq', 0, 0)  5.42 us
  transfers between devices with their start and end apart: 31, of which 17 were waited for; matrix products, arithmetic and copies ran while one was open for 4% of the time, Pallas kernels for 28%

profile of v2, /device:TPU:0, one launch (start us, length us, event | category | flops | bytes accessed | tf_op | source)
XLA Modules:
  0.0 259.7 jit_solution(15315796180611710830)
XLA Ops:
  0.6 8.8 %shard_map.239 = (bf16[1,4,2,448,128]{4,3,2,1,0:T(8,128)(2,1)}, bf16[2,192,1024]{2,1,0:T(8,128)(2,1)}, f32[4,384,5]{2,1,0:T(8,128)}, f32[4,256,5]{2,1,0:T(8,128)}) custom-call(bf16[2,128,1024]{2,1,0:T(8,128)(2,1)} %x_ref.5, bf16[2,64,1024]{2,1,0:T(8,128)(2,1)} %m_ref.1, s32[2,4,2,128]{3,2,1,0:T(2,128)} %bitcast.51, s32[2,4,2,64]{3,2,1,0:T(2,128)} %bitcast.52, ...), custom_call_target="tpu_custom_call" | custom-call | flops 1 | bytes 1 | tf_op jit(solution)/shard_map/pallas_call | solution.py:74
  9.4 7.4 %all-to-all-start = ((bf16[8,448,128]{2,1,0:T(8,128)(2,1)}), bf16[8,448,128]{2,1,0:T(8,128)(2,1)S(1)}, u32[]{:S(2)}, u32[]{:S(2)}) async-start(bf16[8,448,128]{2,1,0:T(8,128)(2,1)} %bitcast.43), calls=%async_computation | async-start | bytes 1835008 | tf_op jit(solution)/shard_map/all_to_all | solution.py:870
  19.6 11.2 %shard_map.240 = (bf16[4,896,1024]{2,1,0:T(8,128)(2,1)}, bf16[4,384,640]{2,1,0:T(8,128)(2,1)}, bf16[4,640,1024]{2,1,0:T(8,128)(2,1)}, bf16[4,32,896]{2,1,0:T(8,128)(2,1)}) custom-call(s32[4]{0:T(128)} %pad_add_fusion.scal_ref, bf16[2,192,1024]{2,1,0:T(8,128)(2,1)} %get-tuple-element.75.ctx_ref, bf16[448,1024]{1,0:T(8,128)(2,1)} %bitcast.37, ...), custom_call_target="tpu_custom_call" | custom-call | flops 1 | bytes 1 | tf_op jit(solution)/shard_map/pallas_call | solution.py:74
  40.8 4.8 %shard_map.242 = (bf16[8,128,128]{2,1,0:T(8,128)(2,1)}, f32[1024,128]{1,0:T(8,128)}, f32[1024,1]{1,0:T(8,128)}) custom-call(s32[4]{0:T(128)} %pad_add_fusion.scal_ref, bf16[8,448,128]{2,1,0:T(8,128)(2,1)} %copy-done.15, bf16[4,640,1024]{2,1,0:T(8,128)(2,1)} %get-tuple-element.76.refs_0_.wo_ref, bf16[1024,512]{1,0:T(8,128)(2,1)} %pad_maximum_fusion.refs_1_.gf_ref, ...), custom_call_target="tpu_custom_call" | custom-call | flops 1 | bytes 1 | tf_op jit(solution)/shard_map/pallas_call | solution.py:74
  45.6 5.4 %all-to-all-start.1 = ((bf16[8,128,128]{2,1,0:T(8,128)(2,1)}), bf16[8,128,128]{2,1,0:T(8,128)(2,1)S(1)}, u32[]{:S(2)}, u32[]{:S(2)}) async-start(bf16[8,128,128]{2,1,0:T(8,128)(2,1)} %get-tuple-element.79), calls=%async_computation.1 | async-start | bytes 524288 | tf_op jit(solution)/shard_map/all_to_all | solution.py:883
  53.0 7.6 %all-to-all-done.1 = bf16[8,128,128]{2,1,0:T(8,128)(2,1)S(1)} async-done(((bf16[8,128,128]{2,1,0:T(8,128)(2,1)}), bf16[8,128,128]{2,1,0:T(8,128)(2,1)S(1)}, u32[]{:S(2)}, u32[]{:S(2)}) %all-to-all-start.1) | async-done | bytes 262176 | tf_op jit(solution)/shard_map/all_to_all | solution.py:883
  61.3 26.1 %shard_map.243 = (bf16[256,3072]{1,0:T(8,128)(2,1)}, bf16[256,2048]{1,0:T(8,128)(2,1)}, bf16[256,6656]{1,0:T(8,128)(2,1)}, bf16[256,1024]{1,0:T(8,128)(2,1)}, f3...) custom-call(s32[4]{0:T(128)} %pad_add_fusion.scal_ref, ...), custom_call_target="tpu_custom_call" | custom-call | flops 1 | bytes 1 | tf_op jit(solution)/shard_map/pallas_call | solution.py:74
  87.5 4.1 %all-to-all-start.2 = ((bf16[8,128,128]{2,1,0:T(8,128)(2,1)}), bf16[8,128,128]{2,1,0:T(8,128)(2,1)}, u32[]{:S(2)}, u32[]{:S(2)}) async-start(bf16[8,128,128]{2,1,0:T(8,128)(2,1)} %bitcast.41), calls=%async_computation.2 | async-start | bytes 524288 | tf_op jit(solution)/shard_map/all_to_all | solution.py:1069
  95.5 4.1 %shard_map.244.refs_0_ = bf16[256,4096]{1,0:T(8,128)(2,1)} custom-call(bf16[512,256]{1,0:T(8,128)(2,1)} %get-tuple-element.85.left_ref, bf16[256,6656]{1,0:T(8,128)(2,1)} %copy-done.12, bf16[256,6656]{1,0:T(8,128)(2,1)} %get-tuple-element.86.gu_ref, bf16[256,6656]{1,0:T(8,128)(2,1)} %copy-done.12, bf16[1,4,2,128,128]{4,3,2,1,0:T(8,128)(2,1)} %get-tuple-element.84.refs_0_.grad_ref), custom_call_target="tpu_custom_call" | custom-call | flops 1 | bytes 1 | tf_op jit(solution)/shard_map/pallas_call | solution.py:74
  101.4 6.3 %shard_map.245.refs_0_ = bf16[8,448,128]{2,1,0:T(8,128)(2,1)} custom-call(s32[4]{0:T(128)} %pad_add_fusion.scal_ref, bf16[8,448,128]{2,1,0:T(8,128)(2,1)} %copy-done.15, f32[1024,128]{1,0:T(8,128)} %get-tuple-element.82.keep_ref, f32[1024,1]{1,0:T(8,128)} %get-tuple-element.83.lse_ref, bf16[8,128,128]{2,1,0:T(8,128)(2,1)} %all-to-all-done.2.grad_ref, ...), custom_call_target="tpu_custom_call" | custom-call | flops 1 | bytes 1 | tf_op jit(solution)/shard_map/pallas_call | solution.py:74
  107.7 3.8 %all-to-all-start.3 = ((bf16[8,448,128]{2,1,0:T(8,128)(2,1)}), bf16[8,448,128]{2,1,0:T(8,128)(2,1)S(1)}, u32[]{:S(2)}, u32[]{:S(2)}) async-start(bf16[8,448,128]{2,1,0:T(8,128)(2,1)} %shard_map.245.refs_0_), calls=%async_computation.3 | async-start | bytes 1835008 | tf_op jit(solution)/shard_map/all_to_all | solution.py:1073
  113.2 3.8 %shard_map.246.refs_0_ = bf16[1024,1024]{1,0:T(8,128)(2,1)} custom-call(bf16[1024,512]{1,0:T(8,128)(2,1)} %pad_maximum_fusion.refs_1_.gf_ref, bf16[256,2048]{1,0:T(8,128)(2,1)} %get-tuple-element.91.act_ref, bf16[256,6656]{1,0:T(8,128)(2,1)} %copy-done.12, bf16[8,448,128]{2,1,0:T(8,128)(2,1)} %shard_map.245.refs_0_), custom_call_target="tpu_custom_call" | custom-call | flops 1 | bytes 1 | tf_op jit(solution)/shard_map/pallas_call | solution.py:74
  123.1 11.4 %all-to-all-done.3 = bf16[8,448,128]{2,1,0:T(8,128)(2,1)S(1)} async-done(((bf16[8,448,128]{2,1,0:T(8,128)(2,1)}), bf16[8,448,128]{2,1,0:T(8,128)(2,1)S(1)}, u32[]{:S(2)}, u32[]{:S(2)}) %all-to-all-start.3) | async-done | bytes 917536 | tf_op jit(solution)/shard_map/all_to_all | solution.py:1073
  135.5 6.5 %shard_map.248 = (bf16[384,1792]{1,0:T(8,128)(2,1)}, bf16[384,1792]{1,0:T(8,128)(2,1)}) custom-call(bf16[1,4,2,448,128]{4,3,2,1,0:T(8,128)(2,1)} %bitcast.40, bf16[1,4,2,128,128]{4,3,2,1,0:T(8,128)(2,1)} %get-tuple-element.84.refs_0_.grad_ref, f32[4,384,5]{2,1,0:T(8,128)} %get-tuple-element.87.vgate_ref, bf16[4,384,640]{2,1,0:T(8,128)(2,1)} %get-tuple-element.88.exp_ref, ...), custom_call_target="tpu_custom_call" | custom-call | flops 1 | bytes 1 | tf_op jit(solution)/shard_map/pallas_call | solution.py:74
  148.4 4.9 %shard_map.249 = (bf16[256,1792]{1,0:T(8,128)(2,1)}, bf16[256,1792]{1,0:T(8,128)(2,1)}) custom-call(bf16[2,512,384]{2,1,0:T(8,128)(2,1)} %get-tuple-element.77.a_ref, bf16[512,384]{1,0:T(8,128)(2,1)} %copy-done.17, bf16[2,512,384]{2,1,0:T(8,128)(2,1)} %get-tuple-element.78.b_ref, bf16[512,384]{1,0:T(8,128)(2,1)} %copy-done.18, ...), custom_call_target="tpu_custom_call" | custom-call | flops 1 | bytes 1 | tf_op jit(solution)/shard_map/pallas_call | solution.py:74
  156.2 4.0 %collective-permute-done.7.new_ref = bf16[256,4096]{1,0:T(8,128)(2,1)} collective-permute-done((bf16[256,4096]{1,0:T(8,128)(2,1)S(1)}, bf16[256,4096]{1,0:T(8,128)(2,1)}, u32[]{:S(2)}, u32[]{:S(2)}) %collective-permute-start.7) | collective-permute-done | bytes 2097184 | tf_op jit(solution)/shard_map/ppermute | solution.py:719
  160.2 4.8 %shard_map.250 = (bf16[128,4096]{1,0:T(8,128)(2,1)}, f32[128,4096]{1,0:T(8,128)}) custom-call(bf16[512,256]{1,0:T(8,128)(2,1)} %get-tuple-element.85.left_ref, bf16[256,6656]{1,0:T(8,128)(2,1)} %copy-done.12, bf16[256,6656]{1,0:T(8,128)(2,1)} %get-tuple-element.86.gu_ref, bf16[256,6656]{1,0:T(8,128)(2,1)} %copy-done.12, ...), custom_call_target="tpu_custom_call" | custom-call | flops 1 | bytes 1 | tf_op jit(solution)/shard_map/pallas_call | solution.py:74
  169.8 4.1 %shard_map.251 = (bf16[1024,512]{1,0:T(8,128)(2,1)}, f32[1024,512]{1,0:T(8,128)}) custom-call(bf16[1024,512]{1,0:T(8,128)(2,1)} %pad_maximum_fusion.refs_1_.gf_ref, bf16[256,2048]{1,0:T(8,128)(2,1)} %get-tuple-element.91.act_ref, bf16[256,6656]{1,0:T(8,128)(2,1)} %copy-done.12, bf16[1024,1024]{1,0:T(8,128)(2,1)} %collective-permute-done.6.new_ref, ...), custom_call_target="tpu_custom_call" | custom-call | flops 2000000000 | bytes 1 | tf_op jit(solution)/shard_map/pallas_call | solution.py:74
  175.1 3.7 %shard_map.252 = (bf16[128,2560]{1,0:T(8,128)(2,1)}, f32[128,2560]{1,0:T(8,128)}) custom-call(bf16[512,256]{1,0:T(8,128)(2,1)} %get-tuple-element.89.left_ref, bf16[256,3072]{1,0:T(8,128)(2,1)} %copy-done.13, bf16[256,3072]{1,0:T(8,128)(2,1)} %get-tuple-element.90.right_ref, bf16[256,3072]{1,0:T(8,128)(2,1)} %copy-done.13, ...), custom_call_target="tpu_custom_call" | custom-call | flops 1 | bytes 1 | tf_op jit(solution)/shard_map/pallas_call | solution.py:74
  179.4 8.1 %shard_map.253.refs_0_ = f32[2,128,1024]{2,1,0:T(8,128)} custom-call(bf16[384,1792]{1,0:T(8,128)(2,1)} %get-tuple-element.92.da_ref.refs_0_.first_ref, bf16[384,1792]{1,0:T(8,128)(2,1)} %get-tuple-element.93.db_ref.second_ref, bf16[2,128,1024]{2,1,0:T(8,128)(2,1)} %x_ref.5, f32[1,1024]{1,0:T(1,128)} %bitcast.47, f32[256,1024]{1,0:T(8,128)} %get-tuple-element.94.resid_ref, ...), custom_call_target="tpu_custom_call" | custom-call | flops 1 | bytes 1 | tf_op jit(solution)/shard_map/pallas_call | solution.py:74
  190.3 5.7 %shard_map.254 = (bf16[128,1792]{1,0:T(8,128)(2,1)}, bf16[128,1792]{1,0:T(8,128)(2,1)}, f32[128,1792]{1,0:T(8,128)}, f32[128,1792]{1,0:T(8,128)}) custom-call(bf16[2,512,384]{2,1,0:T(8,128)(2,1)} %get-tuple-element.77.a_ref, bf16[512,384]{1,0:T(8,128)(2,1)} %copy-done.17, bf16[2,512,384]{2,1,0:T(8,128)(2,1)} %get-tuple-element.78.b_ref, ...), custom_call_target="tpu_custom_call" | custom-call | flops 4000000000 | bytes 1 | tf_op jit(solution)/shard_map/pallas_call | solution.py:74
  208.1 6.4 %collective-permute-done.15.got_ref = bf16[64,4096]{1,0:T(8,128)(2,1)} collective-permute-done((bf16[64,4096]{1,0:T(8,128)(2,1)}, bf16[64,4096]{1,0:T(8,128)(2,1)}, u32[]{:S(2)}, u32[]{:S(2)}) %collective-permute-start.15) | collective-permute-done | bytes 524320 | tf_op jit(solution)/shard_map/ppermute | solution.py:719
  222.1 5.2 %collective-permute-done.22.got_ref = bf16[1024,256]{1,0:T(8,128)(2,1)} collective-permute-done((bf16[1024,256]{1,0:T(8,128)(2,1)}, bf16[1024,256]{1,0:T(8,128)(2,1)}, u32[]{:S(2)}, u32[]{:S(2)}) %collective-permute-start.22) | collective-permute-done | bytes 524320 | tf_op jit(solution)/shard_map/ppermute | solution.py:719
  239.0 10.6 %collective-permute-done.26.got_ref = bf16[1024,128]{1,0:T(8,128)(2,1)S(1)} collective-permute-done((bf16[1024,128]{1,0:T(8,128)(2,1)S(1)}, bf16[1024,128]{1,0:T(8,128)(2,1)S(1)}, u32[]{:S(2)}, u32[]{:S(2)}) %collective-permute-start.26) | collective-permute-done | bytes 262176 | tf_op jit(solution)/shard_map/ppermute | solution.py:719
  (137 shorter events, 89.7 us)
Async XLA Ops:
  9.4 30.4 %all-to-all-start = ((bf16[8,448,128]{2,1,0:T(8,128)(2,1)}), bf16[8,448,128]{2,1,0:T(8,128)(2,1)S(1)}, u32[]{:S(2)}, u32[]{:S(2)}) async-start(bf16[8,448,128]{2,1,0:T(8,128)(2,1)} %bitcast.43), calls=%async_computation | async-start | bytes 1835008 | tf_op jit(solution)/shard_map/all_to_all | solution.py:870
  17.7 18.7 %collective-permute-start = (bf16[1024,256]{1,0:T(8,128)(2,1)S(1)}, bf16[1024,256]{1,0:T(8,128)(2,1)}, u32[]{:S(2)}, u32[]{:S(2)}) collective-permute-start(bf16[1024,256]{1,0:T(8,128)(2,1)S(1)} %fusion.3), channel_id=1, source_target_pairs={{0,1},{1,0},{2,3},{3,2},{4,5},{5,4},{6,7},{7,6},{8,9},{9,8},{10,11... | collective-permute-start | bytes 1572872 | tf_op jit(solution)/shard_map/ppermute | solution.py:719
  45.6 15.0 %all-to-all-start.1 = ((bf16[8,128,128]{2,1,0:T(8,128)(2,1)}), bf16[8,128,128]{2,1,0:T(8,128)(2,1)S(1)}, u32[]{:S(2)}, u32[]{:S(2)}) async-start(bf16[8,128,128]{2,1,0:T(8,128)(2,1)} %get-tuple-element.79), calls=%async_computation.1 | async-start | bytes 524288 | tf_op jit(solution)/shard_map/all_to_all | solution.py:883
  87.5 13.9 %all-to-all-start.2 = ((bf16[8,128,128]{2,1,0:T(8,128)(2,1)}), bf16[8,128,128]{2,1,0:T(8,128)(2,1)}, u32[]{:S(2)}, u32[]{:S(2)}) async-start(bf16[8,128,128]{2,1,0:T(8,128)(2,1)} %bitcast.41), calls=%async_computation.2 | async-start | bytes 524288 | tf_op jit(solution)/shard_map/all_to_all | solution.py:1069
  107.7 26.8 %all-to-all-start.3 = ((bf16[8,448,128]{2,1,0:T(8,128)(2,1)}), bf16[8,448,128]{2,1,0:T(8,128)(2,1)S(1)}, u32[]{:S(2)}, u32[]{:S(2)}) async-start(bf16[8,448,128]{2,1,0:T(8,128)(2,1)} %shard_map.245.refs_0_), calls=%async_computation.3 | async-start | bytes 1835008 | tf_op jit(solution)/shard_map/all_to_all | solution.py:1073
  111.6 48.6 %collective-permute-start.7 = (bf16[256,4096]{1,0:T(8,128)(2,1)S(1)}, bf16[256,4096]{1,0:T(8,128)(2,1)}, u32[]{:S(2)}, u32[]{:S(2)}) collective-permute-start(bf16[256,4096]{1,0:T(8,128)(2,1)S(1)} %copy-done.14), channel_id=1, source_target_pairs={{0,2},{1,3},{2,0},{3,1},{4,6},{5,7},{6,4},{7,5},{8,10},{9,11},{10,... | collective-permute-start | bytes 6291464 | tf_op jit(solution)/shard_map/ppermute | solution.py:719
  116.9 52.9 %collective-permute-start.6 = (bf16[1024,1024]{1,0:T(8,128)(2,1)}, bf16[1024,1024]{1,0:T(8,128)(2,1)}, u32[]{:S(2)}, u32[]{:S(2)}) collective-permute-start(bf16[1024,1024]{1,0:T(8,128)(2,1)} %shard_map.246.refs_0_), channel_id=1, source_target_pairs={{0,4},{4,0},{8,12},{12,8},{16,20},{20,16},{24,28},{28,24},{1,5},{5... | collective-permute-start | bytes 6291464 | tf_op jit(solution)/shard_map/ppermute | solution.py:719
  142.5 32.6 %collective-permute-start.5 = (bf16[256,2560]{1,0:T(8,128)(2,1)}, bf16[256,2560]{1,0:T(8,128)(2,1)}, u32[]{:S(2)}, u32[]{:S(2)}) collective-permute-start(bf16[256,2560]{1,0:T(8,128)(2,1)} %shard_map.247.refs_0_), channel_id=1, source_target_pairs={{0,8},{4,12},{8,0},{12,4},{16,24},{20,28},{24,16},{28,20},{1,9},{5... | collective-permute-start | bytes 3932168 | tf_op jit(solution)/shard_map/ppermute | solution.py:719
  153.3 36.0 %collective-permute-start.10 = (bf16[256,1792]{1,0:T(8,128)(2,1)}, bf16[256,1792]{1,0:T(8,128)(2,1)S(1)}, u32[]{:S(2)}, u32[]{:S(2)}) collective-permute-start(bf16[256,1792]{1,0:T(8,128)(2,1)} %get-tuple-element.96.refs_0_), channel_id=1, source_target_pairs={{0,4},{4,0},{8,12},{12,8},{16,20},{20,16},{24,28},{28,24},{1,5},{5... | collective-permute-start | bytes 2752520 | tf_op jit(solution)/shard_map/ppermute | solution.py:719
  154.7 34.7 %collective-permute-start.11 = (bf16[256,1792]{1,0:T(8,128)(2,1)}, bf16[256,1792]{1,0:T(8,128)(2,1)}, u32[]{:S(2)}, u32[]{:S(2)}) collective-permute-start(bf16[256,1792]{1,0:T(8,128)(2,1)} %get-tuple-element.100), channel_id=1, source_target_pairs={{0,2},{1,3},{2,0},{3,1},{4,6},{5,7},{6,4},{7,5},{8,10},{9,11},{10,... | collective-permute-start | bytes 2752520 | tf_op jit(solution)/shard_map/ppermute | solution.py:719
  165.0 34.2 %collective-permute-start.14 = (bf16[128,4096]{1,0:T(8,128)(2,1)}, bf16[128,4096]{1,0:T(8,128)(2,1)S(1)}, u32[]{:S(2)}, u32[]{:S(2)}) collective-permute-start(bf16[128,4096]{1,0:T(8,128)(2,1)} %get-tuple-element.97.refs_0_), channel_id=1, source_target_pairs={{0,8},{4,12},{8,0},{12,4},{16,24},{20,28},{24,16},{28,20},{1,9},{5... | collective-permute-start | bytes 3145736 | tf_op jit(solution)/shard_map/ppermute | solution.py:719
  173.9 30.4 %collective-permute-start.17 = (bf16[1024,512]{1,0:T(8,128)(2,1)}, bf16[1024,512]{1,0:T(8,128)(2,1)S(1)}, u32[]{:S(2)}, u32[]{:S(2)}) collective-permute-start(bf16[1024,512]{1,0:T(8,128)(2,1)} %get-tuple-element.98.refs_0_), channel_id=1, source_target_pairs={{0,2},{1,3},{2,0},{3,1},{4,6},{5,7},{6,4},{7,5},{8,10},{9,11},{10,... | collective-permute-start | bytes 3145736 | tf_op jit(solution)/shard_map/ppermute | solution.py:719
  178.8 26.8 %collective-permute-start.16 = (bf16[128,2560]{1,0:T(8,128)(2,1)}, bf16[128,2560]{1,0:T(8,128)(2,1)}, u32[]{:S(2)}, u32[]{:S(2)}) collective-permute-start(bf16[128,2560]{1,0:T(8,128)(2,1)} %get-tuple-element.99.refs_0_), channel_id=1, source_target_pairs={{0,4},{4,0},{8,12},{12,8},{16,20},{20,16},{24,28},{28,24},{1,5},{5... | collective-permute-start | bytes 1966088 | tf_op jit(solution)/shard_map/ppermute | solution.py:719
  196.0 23.3 %collective-permute-start.12 = (bf16[128,1792]{1,0:T(8,128)(2,1)}, bf16[128,1792]{1,0:T(8,128)(2,1)}, u32[]{:S(2)}, u32[]{:S(2)}) collective-permute-start(bf16[128,1792]{1,0:T(8,128)(2,1)} %get-tuple-element.103.refs_0_), channel_id=1, source_target_pairs={{0,2},{1,3},{2,0},{3,1},{4,6},{5,7},{6,4},{7,5},{8,10},{9,11},{10,... | collective-permute-start | bytes 1376264 | tf_op jit(solution)/shard_map/ppermute | solution.py:719
  197.3 22.0 %collective-permute-start.13 = (bf16[128,1792]{1,0:T(8,128)(2,1)}, bf16[128,1792]{1,0:T(8,128)(2,1)}, u32[]{:S(2)}, u32[]{:S(2)}) collective-permute-start(bf16[128,1792]{1,0:T(8,128)(2,1)} %get-tuple-element.104), channel_id=1, source_target_pairs={{0,8},{4,12},{8,0},{12,4},{16,24},{20,28},{24,16},{28,20},{1,9},{5... | collective-permute-start | bytes 1376264 | tf_op jit(solution)/shard_map/ppermute | solution.py:719
  205.3 22.1 %collective-permute-start.22 = (bf16[1024,256]{1,0:T(8,128)(2,1)}, bf16[1024,256]{1,0:T(8,128)(2,1)}, u32[]{:S(2)}, u32[]{:S(2)}) collective-permute-start(bf16[1024,256]{1,0:T(8,128)(2,1)} %get-tuple-element.110.refs_0_), channel_id=1, source_target_pairs={{0,8},{4,12},{8,0},{12,4},{16,24},{20,28},{24,16},{28,20},{1,9},{5... | collective-permute-start | bytes 1572872 | tf_op jit(solution)/shard_map/ppermute | solution.py:719
  207.0 21.6 %collective-permute-start.21 = (bf16[64,2560]{1,0:T(8,128)(2,1)S(1)}, bf16[64,2560]{1,0:T(8,128)(2,1)S(1)}, u32[]{:S(2)}, u32[]{:S(2)}) collective-permute-start(bf16[64,2560]{1,0:T(8,128)(2,1)S(1)} %get-tuple-element.111.refs_0_), channel_id=1, source_target_pairs={{0,2},{1,3},{2,0},{3,1},{4,6},{5,7},{6,4},{7,5},{8,10},{9,11},{10,... | collective-permute-start | bytes 983048 | tf_op jit(solution)/shard_map/ppermute | solution.py:719
  215.7 15.9 %collective-permute-start.20 = (bf16[32,4096]{1,0:T(8,128)(2,1)S(1)}, bf16[32,4096]{1,0:T(8,128)(2,1)S(1)}, u32[]{:S(2)}, u32[]{:S(2)}) collective-permute-start(bf16[32,4096]{1,0:T(8,128)(2,1)S(1)} %get-tuple-element.112.refs_0_), channel_id=1, source_target_pairs={{0,16},{4,20},{8,24},{12,28},{16,0},{20,4},{24,8},{28,12},{1,17},{... | collective-permute-start | bytes 786440 | tf_op jit(solution)/shard_map/ppermute | solution.py:719
  220.7 14.2 %collective-permute-start.18 = (bf16[64,1792]{1,0:T(8,128)(2,1)S(1)}, bf16[64,1792]{1,0:T(8,128)(2,1)S(1)}, u32[]{:S(2)}, u32[]{:S(2)}) collective-permute-start(bf16[64,1792]{1,0:T(8,128)(2,1)S(1)} %get-tuple-element.115.refs_0_), channel_id=1, source_target_pairs={{0,8},{4,12},{8,0},{12,4},{16,24},{20,28},{24,16},{28,20},{1,9},{5... | collective-permute-start | bytes 688136 | tf_op jit(solution)/shard_map/ppermute | solution.py:719
  222.1 12.8 %collective-permute-start.19 = (bf16[64,1792]{1,0:T(8,128)(2,1)S(1)}, bf16[64,1792]{1,0:T(8,128)(2,1)S(1)}, u32[]{:S(2)}, u32[]{:S(2)}) collective-permute-start(bf16[64,1792]{1,0:T(8,128)(2,1)S(1)} %get-tuple-element.116), channel_id=1, source_target_pairs={{0,4},{4,0},{8,12},{12,8},{16,20},{20,16},{24,28},{28,24},{1,5},{5... | collective-permute-start | bytes 688136 | tf_op jit(solution)/shard_map/ppermute | solution.py:719
  228.5 21.2 %collective-permute-start.26 = (bf16[1024,128]{1,0:T(8,128)(2,1)S(1)}, bf16[1024,128]{1,0:T(8,128)(2,1)S(1)}, u32[]{:S(2)}, u32[]{:S(2)}) collective-permute-start(bf16[1024,128]{1,0:T(8,128)(2,1)S(1)} %get-tuple-element.120.refs_0_), channel_id=1, source_target_pairs={{0,16},{4,20},{8,24},{12,28},{16,0},{20,4},{24,8},{28,12},{1,17},{... | collective-permute-start | bytes 786440 | tf_op jit(solution)/shard_map/ppermute | solution.py:719
  228.6 25.2 %collective-permute-start.25 = (bf16[32,2560]{1,0:T(8,128)(2,1)S(1)}, bf16[32,2560]{1,0:T(8,128)(2,1)S(1)}, u32[]{:S(2)}, u32[]{:S(2)}) collective-permute-start(bf16[32,2560]{1,0:T(8,128)(2,1)S(1)} %get-tuple-element.121.refs_0_), channel_id=1, source_target_pairs={{0,16},{4,20},{8,24},{12,28},{16,0},{20,4},{24,8},{28,12},{1,17},{... | collective-permute-start | bytes 491528 | tf_op jit(solution)/shard_map/ppermute | solution.py:719
  236.0 19.0 %collective-permute-start.23 = (bf16[32,1792]{1,0:T(8,128)(2,1)S(1)}, bf16[32,1792]{1,0:T(8,128)(2,1)S(1)}, u32[]{:S(2)}, u32[]{:S(2)}) collective-permute-start(bf16[32,1792]{1,0:T(8,128)(2,1)S(1)} %get-tuple-element.124.refs_0_), channel_id=1, source_target_pairs={{0,16},{4,20},{8,24},{12,28},{16,0},{20,4},{24,8},{28,12},{1,17},{... | collective-permute-start | bytes 344072 | tf_op jit(solution)/shard_map/ppermute | solution.py:719
  236.9 20.6 %collective-permute-start.24 = (bf16[32,1792]{1,0:T(8,128)(2,1)S(1)}, bf16[32,1792]{1,0:T(8,128)(2,1)S(1)}, u32[]{:S(2)}, u32[]{:S(2)}) collective-permute-start(bf16[32,1792]{1,0:T(8,128)(2,1)S(1)} %get-tuple-element.126), channel_id=1, source_target_pairs={{0,16},{4,20},{8,24},{12,28},{16,0},{20,4},{24,8},{28,12},{1,17},{... | collective-permute-start | bytes 344072 | tf_op jit(solution)/shard_map/ppermute | solution.py:719
  (34 other events, 181.9 us)

commit v3 on v2

--- a/solution.py
+++ b/solution.py
@@ -659,7 +659,14 @@
 
 
 def heads_last(*refs):
-    heads_third(*refs)
+    send_ref, left_ref = refs[-2:]
+    half = send_ref.shape[0]
+    first = 0
+    for keep_ref, got_ref in (refs[0:2], refs[2:4], refs[4:6]):
+        here = slice(first, first + keep_ref.shape[1])
+        left_ref[:, here] = keep_ref[:half] + got_ref[:half].astype(full)
+        send_ref[:, here] = (keep_ref[half:] + got_ref[half:].astype(full)).astype(low)
+        first += keep_ref.shape[1]
 
 
 def fold(keep_ref, got_ref, *refs):
@@ -675,7 +682,7 @@
     return jnp.sum(jnp.where(same, column, 0.0), axis=0, keepdims=True)
 
 
-def assemble(a_ref, got_a_ref, b_ref, got_b_ref, o_ref, got_o_ref, wall_ref, gain_ref, *refs, d=None):
+def assemble(keep_ref, got_ref, wall_ref, gain_ref, *refs, d=None):
     q_ref, k_ref, v_ref, r_ref, out_ref, norm_ref = refs[-6:]
     size, experts = d.size, d.experts
     slots = 2 + experts
@@ -684,9 +691,7 @@
         here = slice(first * lanes, (first + 1) * lanes)
         return kept[:, here] + got[:, here].astype(full)
 
-    half = d.heads // 2
-    every = [[total(a_ref, got_a_ref, h * slots + at) for at in range(slots)] for h in range(half)]
-    every += [[total(b_ref, got_b_ref, h * slots + at) for at in range(slots)] for h in range(half)]
+    every = [[total(keep_ref, got_ref, h * slots + at) for at in range(slots)] for h in range(d.heads)]
     along = jnp.zeros(every[0][0].shape, full)
     for h in range(d.heads):
         for at in range(slots):
@@ -699,7 +704,7 @@
     outs = [one[0][:, size + experts : size + 2 * experts] for one in every]
     r_ref[...] = jnp.concatenate(values + outs, axis=1)
     out_ref[...] = jnp.concatenate(
-        [total(o_ref, got_o_ref, at)[:, :size] for at in range(d.heads * experts)], axis=1
+        [total(keep_ref, got_ref, d.heads * slots + at)[:, :size] for at in range(d.heads * experts)], axis=1
     )
 
 
@@ -1139,31 +1144,30 @@
         got_a, got_b = halver.swap(send_a, qkv_bits[0][3]), halver.swap(send_b, qkv_bits[1][3])
         send_d, keep_d = step_fold(fold_lanes, keep_d, got_d, 1, send_a)
         got_d = halver.swap(send_d, down_bits[4])
-        send_o, keep_o = step_fold(fold, keep_o, got_o, 0, send_d)
-        got_o = halver.swap(send_o, out_bits[4])
         up_grad, norm2_grad = stage(
             end_up,
             1,
             [given(a) for a in (keep_u, got_u, up_own, gain_rows[:, 1:2])],
-            [send_o],
+            [send_d],
             [made((own, ff), full), made((1, own), full)],
-        )
-        a_shape = (own, span_d)
-        send_a, send_b, keep_a, keep_b = stage(
+            vmem_big,
+        )
+        h_shape = (own, 2 * span_d + heads * wide)
+        send_h, keep_h = stage(
             heads_last,
             1,
-            [given(a) for a in (keep_a, keep_b, got_a, got_b)],
+            [given(a) for a in (keep_a, got_a, keep_b, got_b, keep_o, got_o)],
             [up_grad],
-            [made(a_shape, low)] * 2 + [made(a_shape, full)] * 2,
-        )
-        got_a, got_b = halver.swap(send_a, qkv_bits[0][4]), halver.swap(send_b, qkv_bits[1][4])
-        (down_grad,) = stage(end_down, 1, [given(keep_d), given(got_d)], [send_a], [made((lanes, width), full)])
+            [made(h_shape, low), made(h_shape, full)],
+        )
+        got_h = halver.swap(send_h, chip_z[1])
+        (down_grad,) = stage(end_down, 1, [given(keep_d), given(got_d)], [send_h], [made((lanes, width), full)], vmem_big)
         norm2_grad = norm2_grad.reshape(own)
         flat = [heads * size, heads * size, heads * span, 2 * heads * experts, heads * span]
         query_grad, key_grad, value_grad, router_grad, outproj_grad, norm1_grad = call(
             functools.partial(assemble, d=d),
             1,
-            [given(a) for a in (keep_a, got_a, keep_b, got_b, keep_o, got_o, wall_own, gain_rows[:, 0:1])] + then(down_grad),
+            [given(a) for a in (keep_h, got_h, wall_own, gain_rows[:, 0:1])] + then(down_grad),
             [made((own, cols), full) for cols in flat] + [made((1, own), full)],
             vmem=vmem_less,
             flops=cost.get("assemble", 1),

time: 261 us -> 261 us (level); the launches traced: 260 us -> 256 us
  waiting for transfers between devices: 69.8 us -> 65 us
  starting transfers between devices: 47.7 us -> 43.1 us
  local copies, waits for them, and re-layouts: 18.5 us -> 22 us
    ppermute x27 -> x25, waiting for transfers between devices: 47.5 us -> 42.7 us  [swap(): return lax.ppermute(value, axis, [(i, i ^ mask) for i in range(size)])]
    ppermute x27 -> x25, starting transfers between devices: 27.1 us -> 22.4 us  [swap(): return lax.ppermute(value, axis, [(i, i ^ mask) for i in range(size)])]
    unnamed x56 -> x66, local copies, waits for them, and re-layouts: 12 us -> 15.6 us
    pallas_call x27 -> x26, Pallas kernels: 119 us -> 121 us  [call(): pl.pallas_call(kernel, grid=(steps,), out_shape=[jax.ShapeDtypeStruct(sha...]
  transfers between devices with their start and end apart: 31 -> 29, of which waited for: 17 -> 15; matrix products, arithmetic and copies ran while one was open for 4% -> 4% of each run, Pallas kernels for 28% -> 29%
where the time goes in v3:
time: 261 us; the launch traced here: 256 us
  Pallas kernels  121 us (46%)
  waiting for transfers between devices  65 us (25%)
  starting transfers between devices  43.1 us (17%)
  local copies, waits for them, and re-layouts  22 us (8%)
  other arithmetic  3.81 us (1%)
    pallas_call x26, Pallas kernels, call(): pl.pallas_call(kernel, grid=(steps,), out_shape=[jax.ShapeDtypeStruct(sha...  121 us
    ppermute x25, waiting for transfers between devices, swap(): return lax.ppermute(value, axis, [(i, i ^ mask) for i in range(size)])  42.7 us
    ppermute x25, starting transfers between devices, swap(): return lax.ppermute(value, axis, [(i, i ^ mask) for i in range(size)])  22.4 us
    unnamed x66, local copies, waits for them, and re-layouts  15.6 us
    all_to_all x1, waiting for transfers between devices, local(): returned = lax.all_to_all(back, 'seq', 0, 0)  11.4 us
    all_to_all x1, waiting for transfers between devices, local(): att = lax.all_to_all(att, 'seq', 0, 0)  7.62 us
    all_to_all x1, starting transfers between devices, local(): pay = lax.all_to_all(pay.reshape(cycle, pay_rows, lanes), 'seq', 0, 0)  7.41 us
    all_to_all x1, starting transfers between devices, local(): att = lax.all_to_all(att, 'seq', 0, 0)  5.41 us
  transfers between devices with their start and end apart: 29, of which 15 were waited for; matrix products, arithmetic and copies ran while one was open for 4% of the time, Pallas kernels for 29%

profile of v3, /device:TPU:0, one launch (start us, length us, event | category | flops | bytes accessed | tf_op | source)
XLA Modules:
  0.0 256.1 jit_solution(5428102735311422026)
XLA Ops:
  0.6 8.8 %shard_map.239 = (bf16[1,4,2,448,128]{4,3,2,1,0:T(8,128)(2,1)}, bf16[2,192,1024]{2,1,0:T(8,128)(2,1)}, f32[4,384,5]{2,1,0:T(8,128)}, f32[4,256,5]{2,1,0:T(8,128)}) custom-call(bf16[2,128,1024]{2,1,0:T(8,128)(2,1)} %x_ref.5, bf16[2,64,1024]{2,1,0:T(8,128)(2,1)} %m_ref.1, s32[2,4,2,128]{3,2,1,0:T(2,128)} %bitcast.51, s32[2,4,2,64]{3,2,1,0:T(2,128)} %bitcast.52, ...), custom_call_target="tpu_custom_call" | custom-call | flops 1 | bytes 1 | tf_op jit(solution)/shard_map/pallas_call | solution.py:74
  9.4 7.4 %all-to-all-start = ((bf16[8,448,128]{2,1,0:T(8,128)(2,1)}), bf16[8,448,128]{2,1,0:T(8,128)(2,1)S(1)}, u32[]{:S(2)}, u32[]{:S(2)}) async-start(bf16[8,448,128]{2,1,0:T(8,128)(2,1)} %bitcast.43), calls=%async_computation | async-start | bytes 1835008 | tf_op jit(solution)/shard_map/all_to_all | solution.py:875
  19.6 11.2 %shard_map.240 = (bf16[4,896,1024]{2,1,0:T(8,128)(2,1)}, bf16[4,384,640]{2,1,0:T(8,128)(2,1)}, bf16[4,640,1024]{2,1,0:T(8,128)(2,1)}, bf16[4,32,896]{2,1,0:T(8,128)(2,1)}) custom-call(s32[4]{0:T(128)} %pad_add_fusion.scal_ref, bf16[2,192,1024]{2,1,0:T(8,128)(2,1)} %get-tuple-element.71.ctx_ref, bf16[448,1024]{1,0:T(8,128)(2,1)} %bitcast.37, ...), custom_call_target="tpu_custom_call" | custom-call | flops 1 | bytes 1 | tf_op jit(solution)/shard_map/pallas_call | solution.py:74
  40.8 4.8 %shard_map.242 = (bf16[8,128,128]{2,1,0:T(8,128)(2,1)}, f32[1024,128]{1,0:T(8,128)}, f32[1024,1]{1,0:T(8,128)}) custom-call(s32[4]{0:T(128)} %pad_add_fusion.scal_ref, bf16[8,448,128]{2,1,0:T(8,128)(2,1)} %copy-done.18, bf16[4,640,1024]{2,1,0:T(8,128)(2,1)} %get-tuple-element.72.refs_0_.wo_ref, bf16[1024,512]{1,0:T(8,128)(2,1)} %pad_maximum_fusion.refs_1_.gf_ref, ...), custom_call_target="tpu_custom_call" | custom-call | flops 1 | bytes 1 | tf_op jit(solution)/shard_map/pallas_call | solution.py:74
  45.6 5.4 %all-to-all-start.1 = ((bf16[8,128,128]{2,1,0:T(8,128)(2,1)}), bf16[8,128,128]{2,1,0:T(8,128)(2,1)S(1)}, u32[]{:S(2)}, u32[]{:S(2)}) async-start(bf16[8,128,128]{2,1,0:T(8,128)(2,1)} %get-tuple-element.75), calls=%async_computation.1 | async-start | bytes 524288 | tf_op jit(solution)/shard_map/all_to_all | solution.py:888
  53.0 7.6 %all-to-all-done.1 = bf16[8,128,128]{2,1,0:T(8,128)(2,1)S(1)} async-done(((bf16[8,128,128]{2,1,0:T(8,128)(2,1)}), bf16[8,128,128]{2,1,0:T(8,128)(2,1)S(1)}, u32[]{:S(2)}, u32[]{:S(2)}) %all-to-all-start.1) | async-done | bytes 262176 | tf_op jit(solution)/shard_map/all_to_all | solution.py:888
  61.3 26.1 %shard_map.243 = (bf16[256,3072]{1,0:T(8,128)(2,1)}, bf16[256,2048]{1,0:T(8,128)(2,1)}, bf16[256,6656]{1,0:T(8,128)(2,1)}, bf16[256,1024]{1,0:T(8,128)(2,1)}, f3...) custom-call(s32[4]{0:T(128)} %pad_add_fusion.scal_ref, ...), custom_call_target="tpu_custom_call" | custom-call | flops 1 | bytes 1 | tf_op jit(solution)/shard_map/pallas_call | solution.py:74
  87.5 4.1 %all-to-all-start.2 = ((bf16[8,128,128]{2,1,0:T(8,128)(2,1)}), bf16[8,128,128]{2,1,0:T(8,128)(2,1)}, u32[]{:S(2)}, u32[]{:S(2)}) async-start(bf16[8,128,128]{2,1,0:T(8,128)(2,1)} %bitcast.41), calls=%async_computation.2 | async-start | bytes 524288 | tf_op jit(solution)/shard_map/all_to_all | solution.py:1074
  95.5 4.1 %shard_map.244.refs_0_ = bf16[256,4096]{1,0:T(8,128)(2,1)} custom-call(bf16[512,256]{1,0:T(8,128)(2,1)} %get-tuple-element.81.left_ref, bf16[256,6656]{1,0:T(8,128)(2,1)} %copy-done.15, bf16[256,6656]{1,0:T(8,128)(2,1)} %get-tuple-element.82.gu_ref, bf16[256,6656]{1,0:T(8,128)(2,1)} %copy-done.15, bf16[1,4,2,128,128]{4,3,2,1,0:T(8,128)(2,1)} %get-tuple-element.80.refs_0_.grad_ref), custom_call_target="tpu_custom_call" | custom-call | flops 1 | bytes 1 | tf_op jit(solution)/shard_map/pallas_call | solution.py:74
  101.4 6.3 %shard_map.245.refs_0_ = bf16[8,448,128]{2,1,0:T(8,128)(2,1)} custom-call(s32[4]{0:T(128)} %pad_add_fusion.scal_ref, bf16[8,448,128]{2,1,0:T(8,128)(2,1)} %copy-done.18, f32[1024,128]{1,0:T(8,128)} %get-tuple-element.78.keep_ref, f32[1024,1]{1,0:T(8,128)} %get-tuple-element.79.lse_ref, bf16[8,128,128]{2,1,0:T(8,128)(2,1)} %all-to-all-done.2.grad_ref, ...), custom_call_target="tpu_custom_call" | custom-call | flops 1 | bytes 1 | tf_op jit(solution)/shard_map/pallas_call | solution.py:74
  107.7 3.8 %all-to-all-start.3 = ((bf16[8,448,128]{2,1,0:T(8,128)(2,1)}), bf16[8,448,128]{2,1,0:T(8,128)(2,1)S(1)}, u32[]{:S(2)}, u32[]{:S(2)}) async-start(bf16[8,448,128]{2,1,0:T(8,128)(2,1)} %shard_map.245.refs_0_), calls=%async_computation.3 | async-start | bytes 1835008 | tf_op jit(solution)/shard_map/all_to_all | solution.py:1078
  113.1 3.8 %shard_map.246.refs_0_ = bf16[1024,1024]{1,0:T(8,128)(2,1)} custom-call(bf16[1024,512]{1,0:T(8,128)(2,1)} %pad_maximum_fusion.refs_1_.gf_ref, bf16[256,2048]{1,0:T(8,128)(2,1)} %get-tuple-element.87.act_ref, bf16[256,6656]{1,0:T(8,128)(2,1)} %copy-done.15, bf16[8,448,128]{2,1,0:T(8,128)(2,1)} %shard_map.245.refs_0_), custom_call_target="tpu_custom_call" | custom-call | flops 1 | bytes 1 | tf_op jit(solution)/shard_map/pallas_call | solution.py:74
  123.1 11.4 %all-to-all-done.3 = bf16[8,448,128]{2,1,0:T(8,128)(2,1)S(1)} async-done(((bf16[8,448,128]{2,1,0:T(8,128)(2,1)}), bf16[8,448,128]{2,1,0:T(8,128)(2,1)S(1)}, u32[]{:S(2)}, u32[]{:S(2)}) %all-to-all-start.3) | async-done | bytes 917536 | tf_op jit(solution)/shard_map/all_to_all | solution.py:1078
  135.4 6.5 %shard_map.248 = (bf16[384,1792]{1,0:T(8,128)(2,1)}, bf16[384,1792]{1,0:T(8,128)(2,1)}) custom-call(bf16[1,4,2,448,128]{4,3,2,1,0:T(8,128)(2,1)} %bitcast.40, bf16[1,4,2,128,128]{4,3,2,1,0:T(8,128)(2,1)} %get-tuple-element.80.refs_0_.grad_ref, f32[4,384,5]{2,1,0:T(8,128)} %get-tuple-element.83.vgate_ref, bf16[4,384,640]{2,1,0:T(8,128)(2,1)} %get-tuple-element.84.exp_ref, ...), custom_call_target="tpu_custom_call" | custom-call | flops 1 | bytes 1 | tf_op jit(solution)/shard_map/pallas_call | solution.py:74
  148.4 5.0 %shard_map.249 = (bf16[256,1792]{1,0:T(8,128)(2,1)}, bf16[256,1792]{1,0:T(8,128)(2,1)}) custom-call(bf16[2,512,384]{2,1,0:T(8,128)(2,1)} %get-tuple-element.73.a_ref, bf16[512,384]{1,0:T(8,128)(2,1)} %copy-done.20, bf16[2,512,384]{2,1,0:T(8,128)(2,1)} %get-tuple-element.74.b_ref, bf16[512,384]{1,0:T(8,128)(2,1)} %copy-done.21, ...), custom_call_target="tpu_custom_call" | custom-call | flops 1 | bytes 1 | tf_op jit(solution)/shard_map/pallas_call | solution.py:74
  156.2 3.9 %collective-permute-done.7.new_ref = bf16[256,4096]{1,0:T(8,128)(2,1)} collective-permute-done((bf16[256,4096]{1,0:T(8,128)(2,1)S(1)}, bf16[256,4096]{1,0:T(8,128)(2,1)}, u32[]{:S(2)}, u32[]{:S(2)}) %collective-permute-start.7) | collective-permute-done | bytes 2097184 | tf_op jit(solution)/shard_map/ppermute | solution.py:724
  160.2 4.8 %shard_map.250 = (bf16[128,4096]{1,0:T(8,128)(2,1)}, f32[128,4096]{1,0:T(8,128)}) custom-call(bf16[512,256]{1,0:T(8,128)(2,1)} %get-tuple-element.81.left_ref, bf16[256,6656]{1,0:T(8,128)(2,1)} %copy-done.15, bf16[256,6656]{1,0:T(8,128)(2,1)} %get-tuple-element.82.gu_ref, bf16[256,6656]{1,0:T(8,128)(2,1)} %copy-done.15, ...), custom_call_target="tpu_custom_call" | custom-call | flops 1 | bytes 1 | tf_op jit(solution)/shard_map/pallas_call | solution.py:74
  169.8 4.1 %shard_map.251 = (bf16[1024,512]{1,0:T(8,128)(2,1)}, f32[1024,512]{1,0:T(8,128)}) custom-call(bf16[1024,512]{1,0:T(8,128)(2,1)} %pad_maximum_fusion.refs_1_.gf_ref, bf16[256,2048]{1,0:T(8,128)(2,1)} %get-tuple-element.87.act_ref, bf16[256,6656]{1,0:T(8,128)(2,1)} %copy-done.15, bf16[1024,1024]{1,0:T(8,128)(2,1)} %collective-permute-done.6.new_ref, ...), custom_call_target="tpu_custom_call" | custom-call | flops 2000000000 | bytes 1 | tf_op jit(solution)/shard_map/pallas_call | solution.py:74
  179.4 8.1 %shard_map.253.refs_0_ = f32[2,128,1024]{2,1,0:T(8,128)} custom-call(bf16[384,1792]{1,0:T(8,128)(2,1)} %get-tuple-element.88.da_ref.refs_0_.first_ref, bf16[384,1792]{1,0:T(8,128)(2,1)} %get-tuple-element.89.db_ref.second_ref, bf16[2,128,1024]{2,1,0:T(8,128)(2,1)} %x_ref.5, f32[1,1024]{1,0:T(1,128)} %bitcast.47, f32[256,1024]{1,0:T(8,128)} %get-tuple-element.90.resid_ref, ...), custom_call_target="tpu_custom_call" | custom-call | flops 1 | bytes 1 | tf_op jit(solution)/shard_map/pallas_call | solution.py:74
  190.3 5.7 %shard_map.254 = (bf16[128,1792]{1,0:T(8,128)(2,1)}, bf16[128,1792]{1,0:T(8,128)(2,1)}, f32[128,1792]{1,0:T(8,128)}, f32[128,1792]{1,0:T(8,128)}) custom-call(bf16[2,512,384]{2,1,0:T(8,128)(2,1)} %get-tuple-element.73.a_ref, bf16[512,384]{1,0:T(8,128)(2,1)} %copy-done.20, bf16[2,512,384]{2,1,0:T(8,128)(2,1)} %get-tuple-element.74.b_ref, ...), custom_call_target="tpu_custom_call" | custom-call | flops 4000000000 | bytes 1 | tf_op jit(solution)/shard_map/pallas_call | solution.py:74
  208.7 5.9 %collective-permute-done.15.got_ref = bf16[64,4096]{1,0:T(8,128)(2,1)} collective-permute-done((bf16[64,4096]{1,0:T(8,128)(2,1)}, bf16[64,4096]{1,0:T(8,128)(2,1)}, u32[]{:S(2)}, u32[]{:S(2)}) %collective-permute-start.15) | collective-permute-done | bytes 524320 | tf_op jit(solution)/shard_map/ppermute | solution.py:724
  227.5 4.1 %collective-permute-done.21.got_u_ref = bf16[32,4096]{1,0:T(8,128)(2,1)S(1)} collective-permute-done((bf16[32,4096]{1,0:T(8,128)(2,1)S(1)}, bf16[32,4096]{1,0:T(8,128)(2,1)S(1)}, u32[]{:S(2)}, u32[]{:S(2)}) %collective-permute-start.21) | collective-permute-done | bytes 262176 | tf_op jit(solution)/shard_map/ppermute | solution.py:724
  236.9 10.4 %collective-permute-done.24.got_ref = bf16[1024,128]{1,0:T(8,128)(2,1)S(1)} collective-permute-done((bf16[1024,128]{1,0:T(8,128)(2,1)S(1)}, bf16[1024,128]{1,0:T(8,128)(2,1)S(1)}, u32[]{:S(2)}, u32[]{:S(2)}) %collective-permute-start.24) | collective-permute-done | bytes 262176 | tf_op jit(solution)/shard_map/ppermute | solution.py:724
  250.2 3.8 %collective-permute-done.23.got_ref = bf16[32,6144]{1,0:T(8,128)(2,1)S(1)} collective-permute-done((bf16[32,6144]{1,0:T(8,128)(2,1)S(1)}, bf16[32,6144]{1,0:T(8,128)(2,1)S(1)}, u32[]{:S(2)}, u32[]{:S(2)}) %collective-permute-start.23) | collective-permute-done | bytes 393248 | tf_op jit(solution)/shard_map/ppermute | solution.py:724
  (142 shorter events, 88.1 us)
Async XLA Ops:
  9.4 30.4 %all-to-all-start = ((bf16[8,448,128]{2,1,0:T(8,128)(2,1)}), bf16[8,448,128]{2,1,0:T(8,128)(2,1)S(1)}, u32[]{:S(2)}, u32[]{:S(2)}) async-start(bf16[8,448,128]{2,1,0:T(8,128)(2,1)} %bitcast.43), calls=%async_computation | async-start | bytes 1835008 | tf_op jit(solution)/shard_map/all_to_all | solution.py:875
  17.7 18.6 %collective-permute-start = (bf16[1024,256]{1,0:T(8,128)(2,1)S(1)}, bf16[1024,256]{1,0:T(8,128)(2,1)}, u32[]{:S(2)}, u32[]{:S(2)}) collective-permute-start(bf16[1024,256]{1,0:T(8,128)(2,1)S(1)} %fusion.3), channel_id=1, source_target_pairs={{0,1},{1,0},{2,3},{3,2},{4,5},{5,4},{6,7},{7,6},{8,9},{9,8},{10,11... | collective-permute-start | bytes 1572872 | tf_op jit(solution)/shard_map/ppermute | solution.py:724
  45.6 14.9 %all-to-all-start.1 = ((bf16[8,128,128]{2,1,0:T(8,128)(2,1)}), bf16[8,128,128]{2,1,0:T(8,128)(2,1)S(1)}, u32[]{:S(2)}, u32[]{:S(2)}) async-start(bf16[8,128,128]{2,1,0:T(8,128)(2,1)} %get-tuple-element.75), calls=%async_computation.1 | async-start | bytes 524288 | tf_op jit(solution)/shard_map/all_to_all | solution.py:888
  87.5 13.9 %all-to-all-start.2 = ((bf16[8,128,128]{2,1,0:T(8,128)(2,1)}), bf16[8,128,128]{2,1,0:T(8,128)(2,1)}, u32[]{:S(2)}, u32[]{:S(2)}) async-start(bf16[8,128,128]{2,1,0:T(8,128)(2,1)} %bitcast.41), calls=%async_computation.2 | async-start | bytes 524288 | tf_op jit(solution)/shard_map/all_to_all | solution.py:1074
  107.7 26.8 %all-to-all-start.3 = ((bf16[8,448,128]{2,1,0:T(8,128)(2,1)}), bf16[8,448,128]{2,1,0:T(8,128)(2,1)S(1)}, u32[]{:S(2)}, u32[]{:S(2)}) async-start(bf16[8,448,128]{2,1,0:T(8,128)(2,1)} %shard_map.245.refs_0_), calls=%async_computation.3 | async-start | bytes 1835008 | tf_op jit(solution)/shard_map/all_to_all | solution.py:1078
  111.5 7.2 %collective-permute-start.4 = (bf16[256,3072]{1,0:T(8,128)(2,1)}, bf16[256,3072]{1,0:T(8,128)(2,1)S(1)}, u32[]{:S(2)}, u32[]{:S(2)}) collective-permute-start(bf16[256,3072]{1,0:T(8,128)(2,1)} %get-tuple-element.86.right_ref), channel_id=1, source_target_pairs={{0,1},{1,0},{2,3},{3,2},{4,5},{5,4},{6,7},{7,6},{8,9},{9,8},{10,11... | collective-permute-start | bytes 4718600 | tf_op jit(solution)/shard_map/ppermute | solution.py:724
  111.6 48.6 %collective-permute-start.7 = (bf16[256,4096]{1,0:T(8,128)(2,1)S(1)}, bf16[256,4096]{1,0:T(8,128)(2,1)}, u32[]{:S(2)}, u32[]{:S(2)}) collective-permute-start(bf16[256,4096]{1,0:T(8,128)(2,1)S(1)} %copy-done.17), channel_id=1, source_target_pairs={{0,2},{1,3},{2,0},{3,1},{4,6},{5,7},{6,4},{7,5},{8,10},{9,11},{10,... | collective-permute-start | bytes 6291464 | tf_op jit(solution)/shard_map/ppermute | solution.py:724
  116.9 52.9 %collective-permute-start.6 = (bf16[1024,1024]{1,0:T(8,128)(2,1)}, bf16[1024,1024]{1,0:T(8,128)(2,1)}, u32[]{:S(2)}, u32[]{:S(2)}) collective-permute-start(bf16[1024,1024]{1,0:T(8,128)(2,1)} %shard_map.246.refs_0_), channel_id=1, source_target_pairs={{0,4},{4,0},{8,12},{12,8},{16,20},{20,16},{24,28},{28,24},{1,5},{5... | collective-permute-start | bytes 6291464 | tf_op jit(solution)/shard_map/ppermute | solution.py:724
  142.5 32.6 %collective-permute-start.5 = (bf16[256,2560]{1,0:T(8,128)(2,1)}, bf16[256,2560]{1,0:T(8,128)(2,1)}, u32[]{:S(2)}, u32[]{:S(2)}) collective-permute-start(bf16[256,2560]{1,0:T(8,128)(2,1)} %shard_map.247.refs_0_), channel_id=1, source_target_pairs={{0,8},{4,12},{8,0},{12,4},{16,24},{20,28},{24,16},{28,20},{1,9},{5... | collective-permute-start | bytes 3932168 | tf_op jit(solution)/shard_map/ppermute | solution.py:724
  153.4 36.0 %collective-permute-start.10 = (bf16[256,1792]{1,0:T(8,128)(2,1)}, bf16[256,1792]{1,0:T(8,128)(2,1)S(1)}, u32[]{:S(2)}, u32[]{:S(2)}) collective-permute-start(bf16[256,1792]{1,0:T(8,128)(2,1)} %get-tuple-element.92.refs_0_), channel_id=1, source_target_pairs={{0,4},{4,0},{8,12},{12,8},{16,20},{20,16},{24,28},{28,24},{1,5},{5... | collective-permute-start | bytes 2752520 | tf_op jit(solution)/shard_map/ppermute | solution.py:724
  154.7 34.6 %collective-permute-start.11 = (bf16[256,1792]{1,0:T(8,128)(2,1)}, bf16[256,1792]{1,0:T(8,128)(2,1)}, u32[]{:S(2)}, u32[]{:S(2)}) collective-permute-start(bf16[256,1792]{1,0:T(8,128)(2,1)} %get-tuple-element.96), channel_id=1, source_target_pairs={{0,2},{1,3},{2,0},{3,1},{4,6},{5,7},{6,4},{7,5},{8,10},{9,11},{10,... | collective-permute-start | bytes 2752520 | tf_op jit(solution)/shard_map/ppermute | solution.py:724
  164.9 34.2 %collective-permute-start.14 = (bf16[128,4096]{1,0:T(8,128)(2,1)}, bf16[128,4096]{1,0:T(8,128)(2,1)S(1)}, u32[]{:S(2)}, u32[]{:S(2)}) collective-permute-start(bf16[128,4096]{1,0:T(8,128)(2,1)} %get-tuple-element.93.refs_0_), channel_id=1, source_target_pairs={{0,8},{4,12},{8,0},{12,4},{16,24},{20,28},{24,16},{28,20},{1,9},{5... | collective-permute-start | bytes 3145736 | tf_op jit(solution)/shard_map/ppermute | solution.py:724
  173.8 30.4 %collective-permute-start.17 = (bf16[1024,512]{1,0:T(8,128)(2,1)}, bf16[1024,512]{1,0:T(8,128)(2,1)S(1)}, u32[]{:S(2)}, u32[]{:S(2)}) collective-permute-start(bf16[1024,512]{1,0:T(8,128)(2,1)} %get-tuple-element.94.refs_0_), channel_id=1, source_target_pairs={{0,2},{1,3},{2,0},{3,1},{4,6},{5,7},{6,4},{7,5},{8,10},{9,11},{10,... | collective-permute-start | bytes 3145736 | tf_op jit(solution)/shard_map/ppermute | solution.py:724
  178.8 27.4 %collective-permute-start.16 = (bf16[128,2560]{1,0:T(8,128)(2,1)}, bf16[128,2560]{1,0:T(8,128)(2,1)}, u32[]{:S(2)}, u32[]{:S(2)}) collective-permute-start(bf16[128,2560]{1,0:T(8,128)(2,1)} %get-tuple-element.95.refs_0_), channel_id=1, source_target_pairs={{0,4},{4,0},{8,12},{12,8},{16,20},{20,16},{24,28},{28,24},{1,5},{5... | collective-permute-start | bytes 1966088 | tf_op jit(solution)/shard_map/ppermute | solution.py:724
  196.0 24.1 %collective-permute-start.12 = (bf16[128,1792]{1,0:T(8,128)(2,1)}, bf16[128,1792]{1,0:T(8,128)(2,1)}, u32[]{:S(2)}, u32[]{:S(2)}) collective-permute-start(bf16[128,1792]{1,0:T(8,128)(2,1)} %get-tuple-element.99.refs_0_), channel_id=1, source_target_pairs={{0,2},{1,3},{2,0},{3,1},{4,6},{5,7},{6,4},{7,5},{8,10},{9,11},{10,... | collective-permute-start | bytes 1376264 | tf_op jit(solution)/shard_map/ppermute | solution.py:724
  197.3 22.7 %collective-permute-start.13 = (bf16[128,1792]{1,0:T(8,128)(2,1)}, bf16[128,1792]{1,0:T(8,128)(2,1)}, u32[]{:S(2)}, u32[]{:S(2)}) collective-permute-start(bf16[128,1792]{1,0:T(8,128)(2,1)} %get-tuple-element.100), channel_id=1, source_target_pairs={{0,8},{4,12},{8,0},{12,4},{16,24},{20,28},{24,16},{28,20},{1,9},{5... | collective-permute-start | bytes 1376264 | tf_op jit(solution)/shard_map/ppermute | solution.py:724
  202.1 12.5 %collective-permute-start.15 = (bf16[64,4096]{1,0:T(8,128)(2,1)}, bf16[64,4096]{1,0:T(8,128)(2,1)}, u32[]{:S(2)}, u32[]{:S(2)}) collective-permute-start(bf16[64,4096]{1,0:T(8,128)(2,1)} %get-tuple-element.103.refs_0_), channel_id=1, source_target_pairs={{0,4},{4,0},{8,12},{12,8},{16,20},{20,16},{24,28},{28,24},{1,5},{5... | collective-permute-start | bytes 1572872 | tf_op jit(solution)/shard_map/ppermute | solution.py:724
  205.2 20.3 %collective-permute-start.22 = (bf16[1024,256]{1,0:T(8,128)(2,1)}, bf16[1024,256]{1,0:T(8,128)(2,1)}, u32[]{:S(2)}, u32[]{:S(2)}) collective-permute-start(bf16[1024,256]{1,0:T(8,128)(2,1)} %get-tuple-element.106.refs_0_), channel_id=1, source_target_pairs={{0,8},{4,12},{8,0},{12,4},{16,24},{20,28},{24,16},{28,20},{1,9},{5... | collective-permute-start | bytes 1572872 | tf_op jit(solution)/shard_map/ppermute | solution.py:724
  207.6 26.7 %collective-permute-start.20 = (bf16[64,2560]{1,0:T(8,128)(2,1)S(1)}, bf16[64,2560]{1,0:T(8,128)(2,1)S(1)}, u32[]{:S(2)}, u32[]{:S(2)}) collective-permute-start(bf16[64,2560]{1,0:T(8,128)(2,1)S(1)} %get-tuple-element.107.refs_0_), channel_id=1, source_target_pairs={{0,2},{1,3},{2,0},{3,1},{4,6},{5,7},{6,4},{7,5},{8,10},{9,11},{10,... | collective-permute-start | bytes 983048 | tf_op jit(solution)/shard_map/ppermute | solution.py:724
  216.5 15.1 %collective-permute-start.21 = (bf16[32,4096]{1,0:T(8,128)(2,1)S(1)}, bf16[32,4096]{1,0:T(8,128)(2,1)S(1)}, u32[]{:S(2)}, u32[]{:S(2)}) collective-permute-start(bf16[32,4096]{1,0:T(8,128)(2,1)S(1)} %get-tuple-element.108.refs_0_), channel_id=1, source_target_pairs={{0,16},{4,20},{8,24},{12,28},{16,0},{20,4},{24,8},{28,12},{1,17},{... | collective-permute-start | bytes 786440 | tf_op jit(solution)/shard_map/ppermute | solution.py:724
  221.4 12.9 %collective-permute-start.18 = (bf16[64,1792]{1,0:T(8,128)(2,1)S(1)}, bf16[64,1792]{1,0:T(8,128)(2,1)S(1)}, u32[]{:S(2)}, u32[]{:S(2)}) collective-permute-start(bf16[64,1792]{1,0:T(8,128)(2,1)S(1)} %get-tuple-element.110.refs_0_), channel_id=1, source_target_pairs={{0,8},{4,12},{8,0},{12,4},{16,24},{20,28},{24,16},{28,20},{1,9},{5... | collective-permute-start | bytes 688136 | tf_op jit(solution)/shard_map/ppermute | solution.py:724
  222.8 11.5 %collective-permute-start.19 = (bf16[64,1792]{1,0:T(8,128)(2,1)S(1)}, bf16[64,1792]{1,0:T(8,128)(2,1)S(1)}, u32[]{:S(2)}, u32[]{:S(2)}) collective-permute-start(bf16[64,1792]{1,0:T(8,128)(2,1)S(1)} %get-tuple-element.112), channel_id=1, source_target_pairs={{0,4},{4,0},{8,12},{12,8},{16,20},{20,16},{24,28},{28,24},{1,5},{5... | collective-permute-start | bytes 688136 | tf_op jit(solution)/shard_map/ppermute | solution.py:724
  227.5 19.9 %collective-permute-start.24 = (bf16[1024,128]{1,0:T(8,128)(2,1)S(1)}, bf16[1024,128]{1,0:T(8,128)(2,1)S(1)}, u32[]{:S(2)}, u32[]{:S(2)}) collective-permute-start(bf16[1024,128]{1,0:T(8,128)(2,1)S(1)} %get-tuple-element.116.refs_0_), channel_id=1, source_target_pairs={{0,16},{4,20},{8,24},{12,28},{16,0},{20,4},{24,8},{28,12},{1,17},{... | collective-permute-start | bytes 786440 | tf_op jit(solution)/shard_map/ppermute | solution.py:724
  235.5 18.4 %collective-permute-start.23 = (bf16[32,6144]{1,0:T(8,128)(2,1)S(1)}, bf16[32,6144]{1,0:T(8,128)(2,1)S(1)}, u32[]{:S(2)}, u32[]{:S(2)}) collective-permute-start(bf16[32,6144]{1,0:T(8,128)(2,1)S(1)} %get-tuple-element.119.refs_0_), channel_id=1, source_target_pairs={{0,16},{4,20},{8,24},{12,28},{16,0},{20,4},{24,8},{28,12},{1,17},{... | collective-permute-start | bytes 1179656 | tf_op jit(solution)/shard_map/ppermute | solution.py:724
  (37 other events, 169.2 us)
